TPU v7x, 32 devices: a whole 2x2x4 slice. The times are simulated.
32 devices in a mesh: section: 4 (over z), dp: 8 (over y, x, core).
Axes of the slice: x: 2, y: 2, z: 4, core: 2. Of those that a mesh axis runs over, the one named last changes fastest.
Arguments:
- residues: bfloat16 [16, 256, 640], P('dp'), may hold values from -6 to 6
- out_grad: bfloat16 [16, 256, 640], P('dp'), may hold values from -6 to 6
- key_lengths: int32 [16], P('dp'), may hold values from 128 to 256, as said below
- masked: int32 [16, 256], P('dp'), may hold values from 0 to 1, as said below
- attn_gain: bfloat16 [2, 640], P(None, 'dp'), may hold values from 0.099609375 to 1.8984375
- attn_shift: bfloat16 [2, 640], P(None, 'dp'), may hold values from -3 to 3
- qkv_weight: bfloat16 [2, 640, 1920], P(None, 'dp'), may hold values from -0.25 to 0.25
- query_bias: bfloat16 [2, 640], P(None, 'dp'), may hold values from -3 to 3
- value_bias: bfloat16 [2, 640], P(None, 'dp'), may hold values from -0.29882812 to 0.29882812
- out_weight: bfloat16 [2, 640, 640], P(None, 'dp'), may hold values from -2.5 to 2.5
- out_bias: bfloat16 [2, 640], P(None, 'dp'), may hold values from -3 to 3
- ffn_gain: bfloat16 [2, 640], P(None, 'dp'), may hold values from 0.099609375 to 1.8984375
- ffn_shift: bfloat16 [2, 640], P(None, 'dp'), may hold values from -3 to 3
- up_weight: bfloat16 [2, 640, 5120], P(None, 'dp'), may hold values from -0.25 to 0.25
- up_bias: bfloat16 [2, 5120], P(None, 'dp'), may hold values from -3 to 3
- down_weight: bfloat16 [2, 5120, 640], P(None, 'dp'), may hold values from -0.078125 to 0.078125
- down_bias: bfloat16 [2, 640], P(None, 'dp'), may hold values from -3 to 3
Outputs:
- final_stream: bfloat16 [16, 256, 640], P('dp')
- residues_grad: float32 [16, 256, 640], P('dp')
- attn_gain_grad: float32 [2, 640], P(None, 'dp')
- attn_shift_grad: float32 [2, 640], P(None, 'dp')
- qkv_weight_grad: float32 [2, 640, 1920], P(None, 'dp')
- query_bias_grad: float32 [2, 640], P(None, 'dp')
- value_bias_grad: float32 [2, 640], P(None, 'dp')
- out_weight_grad: float32 [2, 640, 640], P(None, 'dp')
- out_bias_grad: float32 [2, 640], P(None, 'dp')
- ffn_gain_grad: float32 [2, 640], P(None, 'dp')
- ffn_shift_grad: float32 [2, 640], P(None, 'dp')
- up_weight_grad: float32 [2, 640, 5120], P(None, 'dp')
- up_bias_grad: float32 [2, 5120], P(None, 'dp')
- down_weight_grad: float32 [2, 5120, 640], P(None, 'dp')
- down_bias_grad: float32 [2, 640], P(None, 'dp')
Inputs may be any that keep to these rules, and one draw needn't show every extreme that they name: `key_lengths`: keys at positions at or beyond a crop's length are padding; some crop is 256 long. `masked`: marks only positions below the crop's length; each crop has its own marking rate.
All inputs are finite; a program needn't handle non-finite values.
Results may differ from a plain program's by a relative error of at most 0.018.
Values may be sent and summed in bfloat16 or wider, within the bound.
No kernel may reach another device: no remote copies, remote signals or barrier semaphores. Data moves between devices by JAX's collectives and lax.ppermute only.
A program may use at most 640 MiB of HBM per device.

v0:
```python
import jax
import jax.numpy as jnp
from jax import lax
from jax.sharding import PartitionSpec as P

HEADS = 20
HEAD_BLOCK = 4
MICRO_BATCHES = 2
SEQS_MICRO = 1


EPSILON = 1e-05
ROOT_HALF = 0.7071067811865476
INV_ROOT_TAU = 0.3989422804014327
NEGATIVE = -1e30


def shortened(x):

    def short(part):
        return part.astype(jnp.bfloat16) if part.dtype == jnp.float32 else part

    return jax.tree.map(short, x)


def from_behind(x, axis, by):
    length = lax.axis_size(axis)
    pairs = [(i, i + by) for i in range(length) if 0 <= i + by < length]
    return lax.ppermute(x, axis, pairs)


def norm_rows(stream, norm_gain, norm_shift):
    average = jnp.mean(stream, axis=-1, keepdims=True)
    centered = stream - average
    reciprocal = lax.rsqrt(jnp.mean(centered * centered, axis=-1, keepdims=True) + EPSILON)
    scaled = centered * reciprocal
    return (scaled * norm_gain + norm_shift, scaled, reciprocal)


def norm_rows_back(grad_normed, scaled, reciprocal, norm_gain):
    gain_grad = jnp.sum(grad_normed * scaled, axis=0)
    shift_grad = jnp.sum(grad_normed, axis=0)
    inner_term = grad_normed * norm_gain
    grad_stream = reciprocal * (
        inner_term
        - jnp.mean(inner_term, axis=-1, keepdims=True)
        - scaled * jnp.mean(inner_term * scaled, axis=-1, keepdims=True)
    )
    return (grad_stream, gain_grad, shift_grad)


def gelu_exact(values):
    return 0.5 * values * (1.0 + lax.erf(values * ROOT_HALF))


def gelu_slope(values):
    return 0.5 * (1.0 + lax.erf(values * ROOT_HALF)) + values * INV_ROOT_TAU * jnp.exp(
        -0.5 * values * values
    )


def split_heads(projected, sequences, head_count, head_block):
    row_count, triple_width = projected.shape
    length = row_count // sequences
    head_size = triple_width // (3 * head_count)
    shaped = projected.reshape(
        sequences, length, 3, head_count // head_block, head_block, head_size
    )
    return jnp.transpose(shaped, (3, 2, 0, 1, 4, 5))


def key_mask(lengths, length):
    places = jnp.arange(length, dtype=jnp.int32)[None, :]
    return (places < lengths[:, None])[:, None, None, :]


def attend_forward(projected, lengths, head_count, head_block):
    sequences = lengths.shape[0]
    split = split_heads(projected, sequences, head_count, head_block)
    length = split.shape[3]
    head_size = split.shape[5]
    key_valid = key_mask(lengths, length)
    score_scale = head_size ** (-0.5)

    def one_block(operands):
        raw_scores = (
            jnp.einsum(
                "sqhc,skhc->shqk", operands[0], operands[1], preferred_element_type=jnp.float32
            )
            * score_scale
        )
        scores = jnp.where(key_valid, raw_scores, NEGATIVE)
        largest = jnp.max(scores, axis=-1, keepdims=True)
        exponent = jnp.exp(scores - largest)
        denominator = jnp.sum(exponent, axis=-1, keepdims=True)
        probabilities = (exponent / denominator).astype(jnp.bfloat16)
        context = jnp.einsum(
            "shqk,skhc->sqhc", probabilities, operands[2], preferred_element_type=jnp.float32
        )
        return (context.astype(jnp.bfloat16), (largest + jnp.log(denominator))[..., 0])

    contexts, log_total = lax.map(one_block, split)
    context = jnp.transpose(contexts, (1, 2, 0, 3, 4)).reshape(
        sequences * length, head_count * head_size
    )
    return (context, log_total)


def attend_backward(projected, grad_context, log_total, lengths, head_count, head_block):
    sequences = lengths.shape[0]
    split = split_heads(projected, sequences, head_count, head_block)
    blocks = split.shape[0]
    length = split.shape[3]
    head_size = split.shape[5]
    key_valid = key_mask(lengths, length)
    score_scale = head_size ** (-0.5)
    grad_split = jnp.transpose(
        grad_context.reshape(sequences, length, blocks, head_block, head_size), (2, 0, 1, 3, 4)
    )

    def one_block(operands):
        triple, grad_block, block_total = operands
        queries = triple[0]
        key_rows = triple[1]
        value_rows = triple[2]
        raw_scores = (
            jnp.einsum("sqhc,skhc->shqk", queries, key_rows, preferred_element_type=jnp.float32)
            * score_scale
        )
        scores = jnp.where(key_valid, raw_scores, NEGATIVE)
        probabilities = jnp.exp(scores - block_total[..., None])
        grad_probs = jnp.einsum(
            "sqhc,skhc->shqk", grad_block, value_rows, preferred_element_type=jnp.float32
        )
        row_inner = jnp.sum(probabilities * grad_probs, axis=-1, keepdims=True)
        grad_scores = (probabilities * (grad_probs - row_inner)).astype(jnp.bfloat16)
        grad_queries = (
            jnp.einsum("shqk,skhc->sqhc", grad_scores, key_rows, preferred_element_type=jnp.float32)
            * score_scale
        )
        grad_keys = (
            jnp.einsum("shqk,sqhc->skhc", grad_scores, queries, preferred_element_type=jnp.float32)
            * score_scale
        )
        grad_values = jnp.einsum(
            "shqk,sqhc->skhc",
            probabilities.astype(jnp.bfloat16),
            grad_block,
            preferred_element_type=jnp.float32,
        )
        return jnp.stack([grad_queries, grad_keys, grad_values]).astype(jnp.bfloat16)

    grads_all = lax.map(one_block, (split, grad_split, log_total))
    return jnp.transpose(grads_all, (2, 3, 1, 0, 4, 5)).reshape(
        sequences * length, 3 * head_count * head_size
    )


def attention_forward(stream_in, lengths, layer_weights, head_count, head_block):
    norm_gain, norm_shift, qkv_matrix, query_add, value_add, out_matrix, out_add = layer_weights
    stream = stream_in.astype(jnp.float32)
    normed, scaled, reciprocal = norm_rows(
        stream, norm_gain.astype(jnp.float32), norm_shift.astype(jnp.float32)
    )
    projected = jnp.dot(normed.astype(jnp.bfloat16), qkv_matrix, preferred_element_type=jnp.float32)
    bias_row = jnp.concatenate([query_add, jnp.zeros_like(query_add), value_add]).astype(
        jnp.float32
    )
    projected = (projected + bias_row).astype(jnp.bfloat16)
    context, log_total = attend_forward(projected, lengths, head_count, head_block)
    branch = jnp.dot(context, out_matrix, preferred_element_type=jnp.float32) + out_add.astype(
        jnp.float32
    )
    return ((stream + branch).astype(jnp.bfloat16), projected, context, log_total)


def attention_backward(
    stream_in,
    grad_in,
    lengths,
    layer_weights,
    projected,
    context,
    log_total,
    head_count,
    head_block,
):
    norm_gain, norm_shift, qkv_matrix, query_add, value_add, out_matrix, out_add = layer_weights
    model_width = stream_in.shape[1]
    stream = stream_in.astype(jnp.float32)
    normed, scaled, reciprocal = norm_rows(
        stream, norm_gain.astype(jnp.float32), norm_shift.astype(jnp.float32)
    )
    grad_rows = grad_in.astype(jnp.float32)
    out_matrix_grad = jnp.dot(context.T, grad_in, preferred_element_type=jnp.float32)
    out_add_grad = jnp.sum(grad_rows, axis=0)
    grad_context = jnp.dot(grad_in, out_matrix.T, preferred_element_type=jnp.float32).astype(
        jnp.bfloat16
    )
    grad_proj = attend_backward(projected, grad_context, log_total, lengths, head_count, head_block)
    query_add_grad = jnp.sum(grad_proj[:, :model_width], axis=0, dtype=jnp.float32)
    value_add_grad = jnp.sum(grad_proj[:, 2 * model_width :], axis=0, dtype=jnp.float32)
    qkv_matrix_grad = jnp.dot(
        normed.astype(jnp.bfloat16).T, grad_proj, preferred_element_type=jnp.float32
    )
    grad_normed = jnp.dot(grad_proj, qkv_matrix.T, preferred_element_type=jnp.float32)
    grad_stream, gain_grad, shift_grad = norm_rows_back(
        grad_normed, scaled, reciprocal, norm_gain.astype(jnp.float32)
    )
    return (
        grad_rows + grad_stream,
        (
            gain_grad,
            shift_grad,
            qkv_matrix_grad,
            query_add_grad,
            value_add_grad,
            out_matrix_grad,
            out_add_grad,
        ),
    )


def ffn_forward(stream_in, layer_weights):
    norm_gain, norm_shift, up_matrix, up_add, down_matrix, down_add = layer_weights
    stream = stream_in.astype(jnp.float32)
    normed, scaled, reciprocal = norm_rows(
        stream, norm_gain.astype(jnp.float32), norm_shift.astype(jnp.float32)
    )
    up_value = jnp.dot(
        normed.astype(jnp.bfloat16), up_matrix, preferred_element_type=jnp.float32
    ) + up_add.astype(jnp.float32)
    hidden = gelu_exact(up_value).astype(jnp.bfloat16)
    branch = jnp.dot(hidden, down_matrix, preferred_element_type=jnp.float32) + down_add.astype(
        jnp.float32
    )
    return ((stream + branch).astype(jnp.bfloat16), up_value)


def ffn_backward(stream_in, grad_in, layer_weights, up_value):
    norm_gain, norm_shift, up_matrix, up_add, down_matrix, down_add = layer_weights
    stream = stream_in.astype(jnp.float32)
    normed, scaled, reciprocal = norm_rows(
        stream, norm_gain.astype(jnp.float32), norm_shift.astype(jnp.float32)
    )
    grad_rows = grad_in.astype(jnp.float32)
    hidden = gelu_exact(up_value).astype(jnp.bfloat16)
    down_matrix_grad = jnp.dot(hidden.T, grad_in, preferred_element_type=jnp.float32)
    down_add_grad = jnp.sum(grad_rows, axis=0)
    grad_hidden = jnp.dot(grad_in, down_matrix.T, preferred_element_type=jnp.float32)
    grad_up = (grad_hidden * gelu_slope(up_value)).astype(jnp.bfloat16)
    up_matrix_grad = jnp.dot(
        normed.astype(jnp.bfloat16).T, grad_up, preferred_element_type=jnp.float32
    )
    up_add_grad = jnp.sum(grad_up, axis=0, dtype=jnp.float32)
    grad_normed = jnp.dot(grad_up, up_matrix.T, preferred_element_type=jnp.float32)
    grad_stream, gain_grad, shift_grad = norm_rows_back(
        grad_normed, scaled, reciprocal, norm_gain.astype(jnp.float32)
    )
    return (
        grad_rows + grad_stream,
        (gain_grad, shift_grad, up_matrix_grad, up_add_grad, down_matrix_grad, down_add_grad),
    )


def pick_layer(part_list, layer_index):
    return tuple(
        (lax.dynamic_index_in_dim(tensor, layer_index, 0, keepdims=False) for tensor in part_list)
    )


def place_layer(part_list, share_list, layer_index):
    return tuple(
        (
            lax.dynamic_update_index_in_dim(
                jnp.zeros(tensor.shape, jnp.float32), share, layer_index, 0
            )
            for tensor, share in zip(part_list, share_list)
        )
    )


def take_slot(buffer, slot_index):
    return lax.dynamic_index_in_dim(buffer, slot_index, 0, keepdims=False)


def put_slot(buffer, values, slot_index):
    return lax.dynamic_update_index_in_dim(buffer, values, slot_index, 0)


def pack_flat(tensors, total_width):
    flat = jnp.concatenate([tensor.reshape(-1) for tensor in tensors])
    return jnp.pad(flat, (0, total_width - flat.shape[0]))


def unpack_gathered(flat_all, templates, count):
    rows = flat_all.reshape(count, -1)
    offset = 0
    pieces = []
    for template in templates:
        size = template.size
        piece = rows[:, offset : offset + size]
        pieces.append(piece.reshape((count * template.shape[0],) + template.shape[1:]))
        offset = offset + size
    return tuple(pieces)


def pack_grads(full_tensors, count, total_width):
    blocks = jnp.concatenate([tensor.reshape(count, -1) for tensor in full_tensors], axis=1)
    return jnp.pad(blocks, ((0, 0), (0, total_width - blocks.shape[1])))


def unpack_share(flat_row, templates, keep_flag):
    row = flat_row.reshape(-1)
    offset = 0
    pieces = []
    for template in templates:
        size = template.size
        piece = row[offset : offset + size].reshape(template.shape)
        pieces.append(jnp.where(keep_flag, piece, jnp.zeros_like(piece)))
        offset = offset + size
    return tuple(pieces)


def shards(
    residues,
    out_grad,
    key_lengths,
    masked,
    attn_gain,
    attn_shift,
    qkv_weight,
    query_bias,
    value_bias,
    out_weight,
    out_bias,
    ffn_gain,
    ffn_shift,
    up_weight,
    up_bias,
    down_weight,
    down_bias,
):
    section_count = lax.axis_size("section")
    data_count = lax.axis_size("dp")
    section_index = lax.axis_index("section")
    layer_index = section_index // 2
    sub_kind = section_index % 2
    seqs_here, length, model_width = residues.shape
    micro_count = MICRO_BATCHES
    seqs_micro = SEQS_MICRO
    row_count = seqs_micro * length
    hidden_width = up_weight.shape[2]
    head_count = HEADS
    head_block = HEAD_BLOCK
    weighted = out_grad.astype(jnp.float32) * masked.astype(jnp.float32)[:, :, None]
    grad_blocks = weighted.astype(jnp.bfloat16)
    length_blocks = key_lengths.reshape(micro_count, seqs_micro)
    attn_parts = (attn_gain, attn_shift, qkv_weight, query_bias, value_bias, out_weight, out_bias)
    ffn_parts = (ffn_gain, ffn_shift, up_weight, up_bias, down_weight, down_bias)
    attn_local = pick_layer(attn_parts, layer_index)
    ffn_local = pick_layer(ffn_parts, layer_index)
    pack_width = max(
        sum((tensor.size for tensor in attn_local)), sum((tensor.size for tensor in ffn_local))
    )
    own_flat = jnp.where(
        sub_kind == 0, pack_flat(attn_local, pack_width), pack_flat(ffn_local, pack_width)
    )
    gathered_flat = lax.all_gather(own_flat, "dp", axis=0, tiled=True)
    attn_full = unpack_gathered(gathered_flat, attn_local, data_count)
    ffn_full = unpack_gathered(gathered_flat, ffn_local, data_count)
    block_count = head_count // head_block
    kept_state = (
        jnp.zeros((micro_count, row_count, model_width), jnp.bfloat16),
        jnp.zeros((micro_count, row_count, 3 * model_width), jnp.bfloat16),
        jnp.zeros((micro_count, row_count, model_width), jnp.bfloat16),
        jnp.zeros((micro_count, block_count, seqs_micro, head_block, length), jnp.float32),
        jnp.zeros((micro_count, row_count, hidden_width), jnp.float32),
    )

    def forward_attention(incoming, slot_index, kept):
        input_store, proj_store, context_store, total_store, up_store = kept
        lengths = take_slot(length_blocks, slot_index)
        leaving, projected, context, log_total = attention_forward(
            incoming, lengths, attn_full, head_count, head_block
        )
        return (
            leaving,
            (
                put_slot(input_store, incoming, slot_index),
                put_slot(proj_store, projected, slot_index),
                put_slot(context_store, context, slot_index),
                put_slot(total_store, log_total, slot_index),
                up_store,
            ),
        )

    def forward_ffn(incoming, slot_index, kept):
        input_store, proj_store, context_store, total_store, up_store = kept
        leaving, up_value = ffn_forward(incoming, ffn_full)
        return (
            leaving,
            (
                put_slot(input_store, incoming, slot_index),
                proj_store,
                context_store,
                total_store,
                put_slot(up_store, up_value, slot_index),
            ),
        )

    def forward_spare(incoming, slot_index, kept):
        return (incoming, kept)

    final_rows = jnp.zeros((micro_count, row_count, model_width), jnp.bfloat16)
    outgoing = jnp.zeros((row_count, model_width), jnp.bfloat16)
    for moment in range(micro_count + section_count - 1):
        if moment > 0:
            incoming = jax.tree.map(
                lambda part, own: part.astype(own.dtype),
                from_behind(shortened(outgoing), "section", 1),
                outgoing,
            )
        else:
            incoming = outgoing
        micro_index = moment - section_index
        is_live = (micro_index >= 0) & (micro_index < micro_count)
        slot_index = jnp.clip(micro_index, 0, micro_count - 1)
        incoming = jnp.where(section_index == 0, take_slot(residues, slot_index), incoming)
        branch_index = jnp.where(is_live, sub_kind, 2)
        outgoing, kept_state = lax.switch(
            branch_index,
            (forward_attention, forward_ffn, forward_spare),
            incoming,
            slot_index,
            kept_state,
        )
        final_rows = jnp.where(
            is_live & (section_index == section_count - 1),
            put_slot(final_rows, outgoing, slot_index),
            final_rows,
        )
    accumulated = jnp.zeros((data_count, pack_width), jnp.float32)

    def backward_attention(incoming, slot_index, kept):
        input_store, proj_store, context_store, total_store, up_store = kept
        lengths = take_slot(length_blocks, slot_index)
        grad_out, grad_terms = attention_backward(
            take_slot(input_store, slot_index),
            incoming,
            lengths,
            attn_full,
            take_slot(proj_store, slot_index),
            take_slot(context_store, slot_index),
            take_slot(total_store, slot_index),
            head_count,
            head_block,
        )
        return (grad_out, pack_grads(grad_terms, data_count, pack_width))

    def backward_ffn(incoming, slot_index, kept):
        input_store, proj_store, context_store, total_store, up_store = kept
        grad_out, grad_terms = ffn_backward(
            take_slot(input_store, slot_index), incoming, ffn_full, take_slot(up_store, slot_index)
        )
        return (grad_out, pack_grads(grad_terms, data_count, pack_width))

    def backward_spare(incoming, slot_index, kept):
        return (
            jnp.zeros((row_count, model_width), jnp.float32),
            jnp.zeros((data_count, pack_width), jnp.float32),
        )

    input_grad = jnp.zeros((micro_count, row_count, model_width), jnp.float32)
    outgoing = jnp.zeros((row_count, model_width), jnp.bfloat16)
    for moment in range(micro_count + section_count - 1):
        if moment > 0:
            incoming = from_behind(outgoing, "section", -1)
        else:
            incoming = outgoing
        micro_index = moment - (section_count - 1 - section_index)
        is_live = (micro_index >= 0) & (micro_index < micro_count)
        slot_index = jnp.clip(micro_index, 0, micro_count - 1)
        incoming = jnp.where(
            section_index == section_count - 1, take_slot(grad_blocks, slot_index), incoming
        )
        branch_index = jnp.where(is_live, sub_kind, 2)
        grad_out, packed_terms = lax.switch(
            branch_index,
            (backward_attention, backward_ffn, backward_spare),
            incoming,
            slot_index,
            kept_state,
        )
        accumulated = accumulated + packed_terms
        input_grad = jnp.where(
            is_live & (section_index == 0), put_slot(input_grad, grad_out, slot_index), input_grad
        )
        outgoing = grad_out.astype(jnp.bfloat16)
    share_row = lax.psum_scatter(accumulated, "dp", scatter_dimension=0, tiled=True)
    attn_shares = unpack_share(share_row, attn_local, sub_kind == 0)
    ffn_shares = unpack_share(share_row, ffn_local, sub_kind == 1)
    attn_sums = place_layer(attn_parts, attn_shares, layer_index)
    ffn_sums = place_layer(ffn_parts, ffn_shares, layer_index)
    totals = (
        lax.psum(attn_sums[0].astype(jnp.bfloat16), "section").astype(jnp.float32),
        lax.psum(attn_sums[1].astype(jnp.bfloat16), "section").astype(jnp.float32),
        lax.psum(attn_sums[2].astype(jnp.bfloat16), "section").astype(jnp.float32),
        lax.psum(attn_sums[3].astype(jnp.bfloat16), "section").astype(jnp.float32),
        lax.psum(attn_sums[4].astype(jnp.bfloat16), "section").astype(jnp.float32),
        lax.psum(attn_sums[5].astype(jnp.bfloat16), "section").astype(jnp.float32),
        lax.psum(attn_sums[6].astype(jnp.bfloat16), "section").astype(jnp.float32),
        lax.psum(ffn_sums[0].astype(jnp.bfloat16), "section").astype(jnp.float32),
        lax.psum(ffn_sums[1].astype(jnp.bfloat16), "section").astype(jnp.float32),
        lax.psum(ffn_sums[2].astype(jnp.bfloat16), "section").astype(jnp.float32),
        lax.psum(ffn_sums[3].astype(jnp.bfloat16), "section").astype(jnp.float32),
        lax.psum(ffn_sums[4].astype(jnp.bfloat16), "section").astype(jnp.float32),
        lax.psum(ffn_sums[5].astype(jnp.bfloat16), "section").astype(jnp.float32),
        lax.psum(final_rows.astype(jnp.float32).astype(jnp.bfloat16), "section").astype(
            jnp.float32
        ),
        lax.psum(input_grad.astype(jnp.bfloat16), "section").astype(jnp.float32),
    )
    final_stream = totals[13].astype(jnp.bfloat16)
    residues_grad = totals[14]
    grad_outs = tuple(totals[:13])
    return (final_stream, residues_grad) + tuple(grad_outs)


def solution(mesh):
    placed = (
        P("dp", None, None),
        P("dp", None, None),
        P("dp"),
        P("dp", None),
        P(None, "dp"),
        P(None, "dp"),
        P(None, "dp", None),
        P(None, "dp"),
        P(None, "dp"),
        P(None, "dp", None),
        P(None, "dp"),
        P(None, "dp"),
        P(None, "dp"),
        P(None, "dp", None),
        P(None, "dp"),
        P(None, "dp", None),
        P(None, "dp"),
    )
    return jax.shard_map(
        shards,
        mesh=mesh,
        in_specs=placed,
        out_specs=(
            P("dp", None, None),
            P("dp", None, None),
            P(None, "dp"),
            P(None, "dp"),
            P(None, "dp", None),
            P(None, "dp"),
            P(None, "dp"),
            P(None, "dp", None),
            P(None, "dp"),
            P(None, "dp"),
            P(None, "dp"),
            P(None, "dp", None),
            P(None, "dp"),
            P(None, "dp", None),
            P(None, "dp"),
        ),
        check_vma=False,
    )
```

profile of v0, /device:TPU:0, one launch (start us, length us, event | category | flops | bytes accessed | tf_op | source)
XLA Modules:
  0.0 1763.7 jit_solution(15308307766540828648)
XLA Ops:
  14.4 12.5 concatenate.132
  39.3 25.6 %dynamic-update-slice.10 = bf16[6560640]{0:T(1024)(128)(2,1)} dynamic-update-slice(bf16[6560640]{0:T(1024)(128)(2,1)} %broadcast.1368, bf16[820080]{0:T(1024)(128)(2,1)S(1)} %copy-done.19, u32[]{:T(128)} %bitcast.158) | dynamic-update-slice | bytes 3280324
  66.0 180.9 %all-reduce.14.cloned.1.call-done = bf16[6560640]{0:T(1024)(128)(2,1)} async-done(((bf16[6560640]{0:T(1024)(128)(2,1)}), bf16[6560640]{0:T(1024)(128)(2,1)}) %all-reduce.14.cloned.1.call-update) | async-done | bytes 13121296
  246.9 27.8 %reshape.2138 = bf16[8,820080]{1,0:T(8,128)(2,1)} reshape(bf16[6560640]{0:T(1024)(128)(2,1)} %all-reduce.14.cloned.1.call-done) | data formatting | bytes 26242560 | tf_op jit(solution)/shard_map/reshape | solution.py:297
  280.2 10.9 fusion.631
  314.1 30.4 %conditional.10 = (bf16[256,640]{1,0:T(8,128)(2,1)}, bf16[2,256,640]{2,1,0:T(8,128)(2,1)}, bf16[2,256,1920]{2,1,0:T(8,128)(2,1)}, bf16[2,256,640]{2,1,0:T(8,128)...) conditional(s32[]{:T(128)} %clamp.30, ...), branch_computations={%region_0.7_spmd, %region_7.10_spmd, %region_10.11_spmd} | conditional | flops 3365936128 | bytes 91543464 | solution.py:431
  321.6 12.3 while.110
  353.6 32.1 %conditional.11 = (bf16[256,640]{1,0:T(8,128)(2,1)}, bf16[2,256,640]{2,1,0:T(8,128)(2,1)}, bf16[2,256,1920]{2,1,0:T(8,128)(2,1)}, bf16[2,256,640]{1,2,0:T(8,128)...) conditional(s32[]{:T(128)} %clamp.31, ...), branch_computations={%region_11.18_spmd, %region_18.21_spmd, %region_21.22_spmd} | conditional | flops 3365936128 | bytes 52836240 | solution.py:431
  360.9 12.3 while.111
  396.0 16.8 collective-permute-start.2
  437.5 18.9 %conditional.15 = (bf16[256,640]{1,0:T(8,128)(2,1)}, f32[8,820080]{1,0:T(8,128)}) conditional(s32[]{:T(128)} %clamp.35, (bf16[256,640]{1,0:T(8,128)(2,1)}, s32[]{:T(128)}, bf16[2,256,640]{2,1,0:T(8,128)(2,1)}, bf16[2,256,1920]{2,1,0:T(8,128)(2,1)}, bf16[640,640]{1,0:T(8,128)(2,1)S(1)}, ...), branch_computations={%region_56.69_spmd, %region_69.78_spmd, %region_78.79_spmd} | conditional | flops 6738897408 | bytes 198754496 | solution.py:488
  447.4 8.8 broadcast.1294
  457.7 32.8 %collective-permute-done.4 = bf16[256,640]{1,0:T(8,128)(2,1)S(1)} collective-permute-done((bf16[256,640]{1,0:T(8,128)(2,1)}, bf16[256,640]{1,0:T(8,128)(2,1)S(1)}, u32[]{:S(2)}, u32[]{:S(2)}) %collective-permute-start.4) | collective-permute-done | bytes 327712 | tf_op jit(solution)/shard_map/ppermute | solution.py:29
  491.6 11.3 conditional.16
  493.6 8.8 broadcast.1310
  513.4 11.1 conditional.17
  515.4 8.9 broadcast.1326
  525.8 366.9 %collective-permute-done.6 = bf16[256,640]{1,0:T(8,128)(2,1)S(1)} collective-permute-done((bf16[256,640]{1,0:T(8,128)(2,1)}, bf16[256,640]{1,0:T(8,128)(2,1)S(1)}, u32[]{:S(2)}, u32[]{:S(2)}) %collective-permute-start.6) | collective-permute-done | bytes 327712 | tf_op jit(solution)/shard_map/ppermute | solution.py:29
  893.8 104.5 %conditional.18 = (bf16[256,640]{1,0:T(8,128)(2,1)}, f32[8,820080]{1,0:T(8,128)}) conditional(s32[]{:T(128)} %clamp.38, (bf16[256,640]{1,0:T(8,128)(2,1)S(1)}, s32[]{:T(128)}, bf16[2,256,640]{2,1,0:T(8,128)(2,1)}, bf16[2,256,1920]{2,1,0:T(8,128)(2,1)}, bf16[640,640]{1,0:T(8,128)(2,1)S(1)}, ...), branch_computations={%region_125.138_spmd, %region_138.147_spmd, %region_147.148_spmd} | conditional | flops 6738897408 | bytes 197443744 | solution.py:488
  904.3 28.4 %while.118 = (s32[]{:T(128)}, bf16[5,3,1,256,4,32]{3,5,4,0,1,2:T(8,128)(2,1)}, bf16[5,3,1,256,4,32]{3,5,4,0,1,2:T(8,128)(2,1)}, f32[5,1,4,256]{3,2,1,0:T(4,128)S...) while((s32[]{:T(128)}, bf16[5,3,1,256,4,32]{3,5,4,0,1,2:T(8,128)(2,1)}, ...), condition=%wide.region_130.130_spmd.clone, body=%wide.region_128.129_spmd.clone.sunk | while | flops 86998272 | bytes 9327469 | solution.py:153
  950.5 14.2 dynamic-update-slice.64
  978.6 12.9 pad.17
  999.6 43.2 %collective-permute-done.7 = bf16[256,640]{1,0:T(8,128)(2,1)S(1)} collective-permute-done((bf16[256,640]{1,0:T(8,128)(2,1)}, bf16[256,640]{1,0:T(8,128)(2,1)S(1)}, u32[]{:S(2)}, u32[]{:S(2)}) %collective-permute-start.7) | collective-permute-done | bytes 327712 | tf_op jit(solution)/shard_map/ppermute | solution.py:29
  1043.7 99.2 %conditional.19 = (f32[8,820080]{1,0:T(8,128)}, bf16[1,256,640]{2,1,0:T(8,128)(2,1)S(1)}) conditional(s32[]{:T(128)} %clamp.39, (s32[]{:T(128)}, bf16[2,256,1920]{2,1,0:T(8,128)(2,1)}, bf16[256,640]{1,0:T(8,128)(2,1)S(1)}, bf16[640,640]{1,0:T(8,128)(2,1)S(1)}, f32[2,5,1,4,256]{4,3,1,2,0:T(4,128)S(1)}, ...), branch_computations={%region_148.161_spmd, %region_161.170_spmd, %region_170.171_spmd} | conditional | flops 6738896896 | bytes 197443744 | solution.py:488
  1053.5 20.3 %while.119 = (s32[]{:T(128)}, bf16[5,3,1,256,4,32]{3,5,4,0,1,2:T(8,128)(2,1)}, bf16[5,3,1,256,4,32]{3,5,4,0,1,2:T(8,128)(2,1)}, f32[5,1,4,256]{3,2,1,0:T(4,128)S...) while((s32[]{:T(128)}, ...), condition=%wide.region_151.151_spmd.clone, body=%wide.region_149.150_spmd.clone.sunk | while | flops 86998272 | bytes 9327469 | solution.py:153
  1090.4 14.2 dynamic-update-slice.71
  1118.5 13.0 pad.18
  1142.9 49.4 %add_add_fusion = f32[8,820080]{1,0:T(8,128)} fusion(f32[8,820080]{1,0:T(8,128)} %get-tuple-element.1180, f32[8,820080]{1,0:T(8,128)} %get-tuple-element.1179, f32[8,820080]{1,0:T(8,128)} %get-tuple-element.1178, f32[8,820080]{1,0:T(8,128)} %get-tuple-element.1176, f32[8,820080]{1,0:T(8,128)} %get-tuple-element.1177), kind=kLoop, calls=%fused_computation.939 | loop fusion | flops 26242560 | bytes 157455360 | tf_op jit(solution)/shard_map/add | solution.py:495
  1196.6 313.4 %all-reduce.16.cloned.1.call-done = f32[8,820080]{1,0:T(8,128)} async-done(((f32[8,820080]{1,0:T(8,128)}), f32[8,820080]{1,0:T(8,128)}) %all-reduce.16.cloned.1.call-update) | async-done | bytes 26242576
  1522.2 21.1 %fusion.610 = (bf16[409600]{0:T(1024)(128)(2,1)S(1)}, bf16[409600]{0:T(1024)(128)(2,1)S(1)}) fusion(pred[]{:T(512)S(6)} %eq.13, f32[8,820080]{1,0:T(8,128)} %all-reduce.16.cloned.1.call-done, u32[]{:T(128)} %bitcast.308, u32[]{:T(128)S(6)} %convert.113, u32[]{:T(128)S(6)} %convert.106), kind=kLoop, calls=%fused_computation.944 | loop fusion | flops 819200 | bytes 4915213 | tf_op jit(solution)/shard_map/jit(_where)/select_n | solution.py:320
  1552.5 12.4 all-reduce.8
  1570.0 175.5 %all-reduce.18.cloned.1.call-done = (bf16[2,256,640]{2,1,0:T(8,128)(2,1)}, bf16[2,256,640]{2,1,0:T(8,128)(2,1)}, bf16[2,80,1920]{2,1,0:T(8,128)(2,1)}, bf16[2,80...) async-done(((bf16[2,256,640]{2,1,0:T(8,128)(2,1)}, bf16[2,256,640]{2,1,0:T(8,128)(2,1)}, bf16[2,80,1920]{2,1,0:T(8,128)(2,1)}, ...) | async-done | bytes 5406736 | tf_op jit(solution)/shard_map/psum | solution.py:519
  (502 shorter events, 341.3 us)
Async XLA Ops:
  7.2 5.9 copy-start.48
  7.3 5.8 copy-start.54
  7.3 5.8 copy-start.55
  7.3 5.8 copy-start.56
  7.3 5.8 copy-start.57
  7.3 239.6 %all-reduce.14.cloned.1.call-start = ((), (), s32[]{:S(2)}) async-start(), calls=%async_computation | async-start | bytes 26243072
  64.9 1445.1 %all-reduce.16.cloned.1.call-start = ((), (), s32[]{:S(2)}) async-start(), calls=%async_computation.1 | async-start | bytes 52486144
  305.5 8.6 copy-start.58
  344.5 9.1 copy-start.3
  344.5 9.0 collective-permute-start
  353.6 7.3 copy-start.15
  385.7 9.6 copy-start.9
  385.7 8.5 collective-permute-start.1
  395.2 17.6 copy-start.49
  396.0 24.1 %copy-start.5 = (bf16[1,256,640]{2,1,0:T(8,128)(2,1)}, bf16[1,256,640]{2,1,0:T(8,128)(2,1)S(1)}, u32[]{:S(2)}) copy-start(bf16[1,256,640]{2,1,0:T(8,128)(2,1)S(1)} %get-tuple-element.1151) | copy-start | bytes 983044
  396.0 23.1 %collective-permute-start.2 = (bf16[256,640]{1,0:T(8,128)(2,1)}, bf16[256,640]{1,0:T(8,128)(2,1)S(1)}, u32[]{:S(2)}, u32[]{:S(2)}) collective-permute-start(bf16[256,640]{1,0:T(8,128)(2,1)} %get-tuple-element.1152), channel_id=1, source_target_pairs={{0,8},{8,16},{16,24},{1,9},{9,17},{17,25},{2,10},{10,18},{18,26},{... | collective-permute-start | bytes 983048 | tf_op jit(solution)/shard_map/ppermute | solution.py:29
  426.0 10.7 copy-start.7
  426.0 9.7 collective-permute-start.3
  456.4 34.2 %collective-permute-start.4 = (bf16[256,640]{1,0:T(8,128)(2,1)}, bf16[256,640]{1,0:T(8,128)(2,1)S(1)}, u32[]{:S(2)}, u32[]{:S(2)}) collective-permute-start(bf16[256,640]{1,0:T(8,128)(2,1)} %get-tuple-element.1171), channel_id=1, source_target_pairs={{8,0},{16,8},{24,16},{9,1},{17,9},{25,17},{10,2},{18,10},{26,18},{... | collective-permute-start | bytes 983048 | tf_op jit(solution)/shard_map/ppermute | solution.py:29
  502.9 9.5 collective-permute-start.5
  524.5 368.2 %collective-permute-start.6 = (bf16[256,640]{1,0:T(8,128)(2,1)}, bf16[256,640]{1,0:T(8,128)(2,1)S(1)}, u32[]{:S(2)}, u32[]{:S(2)}) collective-permute-start(bf16[256,640]{1,0:T(8,128)(2,1)} %get-tuple-element.1173), channel_id=1, source_target_pairs={{8,0},{16,8},{24,16},{9,1},{17,9},{25,17},{10,2},{18,10},{26,18},{... | collective-permute-start | bytes 983048 | tf_op jit(solution)/shard_map/ppermute | solution.py:29
  932.6 8.2 copy-start.27
  998.3 44.5 %collective-permute-start.7 = (bf16[256,640]{1,0:T(8,128)(2,1)}, bf16[256,640]{1,0:T(8,128)(2,1)S(1)}, u32[]{:S(2)}, u32[]{:S(2)}) collective-permute-start(bf16[256,640]{1,0:T(8,128)(2,1)} %get-tuple-element.1174), channel_id=1, source_target_pairs={{8,0},{16,8},{24,16},{9,1},{17,9},{25,17},{10,2},{18,10},{26,18},{... | collective-permute-start | bytes 983048 | tf_op jit(solution)/shard_map/ppermute | solution.py:29
  1073.8 6.9 copy-start.28
  1118.5 13.0 copy-start.43
  1142.9 49.4 %copy-start.40 = (bf16[1,256,640]{2,1,0:T(8,128)(2,1)}, bf16[1,256,640]{2,1,0:T(8,128)(2,1)S(1)}, u32[]{:S(2)}) copy-start(bf16[1,256,640]{2,1,0:T(8,128)(2,1)S(1)} %get-tuple-element.1175) | copy-start | bytes 983044
  1192.4 553.1 %all-reduce.18.cloned.1.call-start = ((), (), s32[]{:S(2)}) async-start(), calls=%async_computation.2 | async-start | bytes 10813440 | tf_op jit(solution)/shard_map/psum | solution.py:519
  1194.0 349.3 %copy-start.16 = (bf16[2,256,640]{2,1,0:T(8,128)(2,1)}, bf16[2,256,640]{2,1,0:T(8,128)(2,1)S(1)}, u32[]{:S(2)}) copy-start(bf16[2,256,640]{2,1,0:T(8,128)(2,1)S(1)} %select_dynamic-update-slice_fusion.1) | copy-start | bytes 1966084
  1196.6 348.6 %copy-start.17 = (bf16[2,256,640]{2,1,0:T(8,128)(2,1)}, bf16[2,256,640]{2,1,0:T(8,128)(2,1)S(1)}, u32[]{:S(2)}) copy-start(bf16[2,256,640]{2,1,0:T(8,128)(2,1)S(1)} %select_dynamic-update-slice_fusion) | copy-start | bytes 1966084
  1745.5 6.3 copy-start.36
  1745.5 8.4 copy-start.35
  1750.1 5.8 copy-start.42
  (27 other events, 73.5 us)
Sparse Core Ops, SparseCore 0:
  65.0 181.8 all-reduce.13
  1192.5 317.4 all-reduce.15
  1549.2 196.2 all-reduce.17
where the time goes:
time: 1780 us; the launch traced here: 1760 us
  waiting for transfers between devices  1150 us (65%)
  local copies, waits for them, and re-layouts  311 us (17%)
  other arithmetic  147 us (8%)
  matrix products  60.3 us (3%)
  loops' own time  43.1 us (2%)
  starting transfers between devices  29.4 us (2%)
    unnamed x5, waiting for transfers between devices  494 us
    ppermute x8, waiting for transfers between devices, from_behind(): return lax.ppermute(x, axis, pairs)  476 us
    psum x1, waiting for transfers between devices, shards(): lax.psum(final_rows.astype(jnp.float32).astype(jnp.bfloat16), 'section')  176 us
    cond x28, local copies, waits for them, and re-layouts  54.1 us
    add x1, other arithmetic, shards(): accumulated = accumulated + packed_terms  49.4 us
    another operation x22, local copies, waits for them, and re-layouts  39.7 us
    unnamed x90, local copies, waits for them, and re-layouts  37.9 us
  transfers between devices with their start and end apart: 11, of which 11 were waited for; matrix products, arithmetic and copies ran while one was open for 1% of the time, Pallas kernels for 0%

commit v1 on v0

v1 whole, which is shorter than its diff:
```python
import functools

import jax
import jax.numpy as jnp
from jax import lax
from jax.experimental import pallas as pl
from jax.experimental.pallas import tpu as pltpu
from jax.sharding import PartitionSpec as P

HEADS = 20
EPSILON = 1e-05
ROOT_HALF = 0.7071067811865476
INV_ROOT_TAU = 0.3989422804014327
NEGATIVE = -1e30
BF = jnp.bfloat16
F32 = jnp.float32
VMEM_LIMIT = 56 * 1024 * 1024


def dot_nn(a, b):
    return jnp.dot(a, b, preferred_element_type=F32)


def dot_nt(a, b):
    return lax.dot_general(a, b, (((1,), (1,)), ((), ())), preferred_element_type=F32)


def dot_tn(a, b):
    return lax.dot_general(a, b, (((0,), (0,)), ((), ())), preferred_element_type=F32)


def norm_parts(stream):
    average = jnp.mean(stream, axis=-1, keepdims=True)
    centered = stream - average
    reciprocal = lax.rsqrt(jnp.mean(centered * centered, axis=-1, keepdims=True) + EPSILON)
    return centered * reciprocal, reciprocal


def norm_back(grad_n, scaled, reciprocal, gain):
    inner = grad_n * gain
    return reciprocal * (
        inner
        - jnp.mean(inner, axis=-1, keepdims=True)
        - scaled * jnp.mean(inner * scaled, axis=-1, keepdims=True)
    )


def own_columns(ref, step, core, width):
    if step == 0:
        return ref[:, :width]
    return ref[:, pl.ds(pl.multiple_of(core * step, 128), step)][:, :width]


def column_sum(values):
    return jnp.sum(values, axis=0, keepdims=True)


def key_valid_column(ids_ref, half):
    length, core = ids_ref[0], ids_ref[1]
    place = lax.broadcasted_iota(jnp.int32, (2 * half, 1), 0)
    own = place + core * half
    sibling = place - half + (1 - core) * half
    return jnp.where(place < half, own, sibling) < length


def head_probs(queries, key_rows, valid):
    head_size = queries.shape[1]
    scores = dot_nt(key_rows, queries) * head_size ** (-0.5)
    scores = jnp.where(valid, scores, NEGATIVE)
    exponent = jnp.exp(scores - jnp.max(scores, axis=0, keepdims=True))
    return exponent * (1.0 / jnp.sum(exponent, axis=0, keepdims=True))


def key_valid_row(ids_ref, half):
    length, core = ids_ref[0], ids_ref[1]
    place = lax.broadcasted_iota(jnp.int32, (1, 2 * half), 1)
    own = place + core * half
    sibling = place - half + (1 - core) * half
    return jnp.where(place < half, own, sibling) < length


def attn_forward_kernel(
    heads, step, ids_ref, own_ref, sib_ref, gain_ref, shift_ref, w_ref, bias_ref, *refs
):
    proj_ref, ctx_ref = refs
    half = own_ref.shape[0]
    width = ctx_ref.shape[1]
    size = width // heads
    w = own_columns(w_ref, step, ids_ref[1], 3 * width)
    for row, ref in ((0, own_ref), (half, sib_ref)):
        scaled, _ = norm_parts(ref[...].astype(F32))
        normed = (scaled * gain_ref[...] + shift_ref[...]).astype(BF)
        proj_ref[row : row + half, :] = (dot_nn(normed, w) + bias_ref[...]).astype(BF)
    valid = key_valid_row(ids_ref, half)
    for h in range(heads):
        at = h * size
        queries = proj_ref[:, at : at + size]
        key_rows = proj_ref[:, width + at : width + at + size]
        scores = dot_nt(queries, key_rows) * size ** (-0.5)
        scores = jnp.where(valid, scores, NEGATIVE)
        exponent = jnp.exp(scores - jnp.max(scores, axis=-1, keepdims=True))
        probs = exponent * (1.0 / jnp.sum(exponent, axis=-1, keepdims=True))
        ctx_ref[:, at : at + size] = dot_nn(
            probs.astype(BF), proj_ref[:, 2 * width + at : 2 * width + at + size]
        ).astype(BF)


def out_kernel(
    out_at, ids_ref, ctx_ref, other_ref, own_ref, w_ref, bias_ref, gain_ref, shift_ref, *refs
):
    mid_ref, n2_ref = refs
    half = own_ref.shape[0]
    width = ctx_ref.shape[1]
    core = ids_ref[1]
    mine = pl.ds(pl.multiple_of(core * width, 64), width)
    theirs = pl.ds(pl.multiple_of((1 - core) * width, 64), width)
    columns = slice(out_at, out_at + own_ref.shape[1])
    total = dot_nn(ctx_ref[:half, :], w_ref[mine, columns])
    total = total + dot_nn(other_ref[half:, :], w_ref[theirs, columns])
    mid = (own_ref[...].astype(F32) + total + bias_ref[...]).astype(BF)
    mid_ref[...] = mid
    scaled, _ = norm_parts(mid.astype(F32))
    n2_ref[...] = (scaled * gain_ref[...] + shift_ref[...]).astype(BF)


def ff_tiles(width):
    tile = 256 if width % 256 == 0 else width
    return [(at, tile) for at in range(0, width, tile)]


def ffn_forward_kernel(count, *refs):
    x_refs = refs[:count]
    up_ref, upb_ref, down_ref = refs[count : count + 3]
    out_refs = refs[count + 3 : 2 * count + 3]
    acc_ref = refs[-1]
    rows = x_refs[0].shape[0]
    shift = up_ref.shape[1] - upb_ref.shape[1]
    x = jnp.concatenate([ref[...] for ref in x_refs], axis=0)
    for at, tile in ff_tiles(upb_ref.shape[1]):
        up = dot_nn(x, up_ref[:, shift + at : shift + at + tile]) + upb_ref[:, at : at + tile]
        hidden = (0.5 * up * (1.0 + lax.erf(up * ROOT_HALF))).astype(BF)
        part = dot_nn(hidden, down_ref[at : at + tile, :])
        if at == 0:
            acc_ref[...] = part
        else:
            acc_ref[...] += part
    for j, ref in enumerate(out_refs):
        ref[...] = acc_ref[j * rows : (j + 1) * rows, :].astype(BF)


def ffn_backward_kernel(count, *refs):
    x_refs, g_refs = refs[:count], refs[count : 2 * count]
    up_ref, upb_ref, down_ref = refs[2 * count : 2 * count + 3]
    q_refs = refs[2 * count + 3 : 3 * count + 3]
    hidden_ref, gup_ref, dupb_ref, qacc_ref = refs[3 * count + 3 :]
    rows = x_refs[0].shape[0]
    shift = up_ref.shape[1] - upb_ref.shape[1]
    x = jnp.concatenate([ref[...] for ref in x_refs], axis=0)
    g = jnp.concatenate([ref[...] for ref in g_refs], axis=0)
    for at, tile in ff_tiles(upb_ref.shape[1]):
        up_tile = up_ref[:, shift + at : shift + at + tile]
        up = dot_nn(x, up_tile) + upb_ref[:, at : at + tile]
        bell = 0.5 * (1.0 + lax.erf(up * ROOT_HALF))
        hidden_ref[:, at : at + tile] = (up * bell).astype(BF)
        slope = bell + up * INV_ROOT_TAU * jnp.exp(-0.5 * up * up)
        grad_up = (dot_nt(g, down_ref[at : at + tile, :]) * slope).astype(BF)
        gup_ref[:, at : at + tile] = grad_up
        dupb_ref[:, at : at + tile] = column_sum(grad_up.astype(F32))
        part = dot_nt(grad_up, up_tile)
        if at == 0:
            qacc_ref[...] = part
        else:
            qacc_ref[...] += part
    for j, ref in enumerate(q_refs):
        ref[...] = qacc_ref[j * rows : (j + 1) * rows, :].astype(BF)


def ffn_weights_kernel(count, *refs):
    ids_ref, refs = refs[0], refs[1:]
    x_refs, g_refs = refs[:count], refs[count : 2 * count]
    hidden_ref, gup_ref, down_ref = refs[2 * count : 2 * count + 3]
    rest = refs[2 * count + 3 :]
    own_ref, sib_ref, dup_ref = rest[:3]
    p_refs = rest[3:-1]
    ddown_ref = rest[-1]
    rows = x_refs[0].shape[0]
    width = gup_ref.shape[1]
    core, chip = ids_ref[1], ids_ref[2]
    x = jnp.concatenate([ref[...] for ref in x_refs], axis=0)
    g = jnp.concatenate([ref[...] for ref in g_refs], axis=0)
    turned = x.T
    for at, tile in ff_tiles(width):
        ddown_ref[at : at + tile, :] = dot_tn(hidden_ref[:, at : at + tile], g).astype(BF)
        dup_ref[:, at : at + tile] = dot_nn(turned, gup_ref[:, at : at + tile]).astype(BF)
    model = x.shape[1]
    part = width // 2
    piece = model // (2 * count)
    for side, ref in ((core, own_ref), (1 - core, sib_ref)):
        for j in range(count if piece % 16 == 0 else 0):
            at = pl.multiple_of((2 * (chip ^ j) + side) * piece, 16)
            ref[j * piece : (j + 1) * piece, :] = dup_ref[pl.ds(at, piece), :]
        base = side * part
        for b in range(width // model):
            at = pl.multiple_of(base + b * (model // 2), 16)
            ref[model // 2 :, b * model : (b + 1) * model] = ddown_ref[pl.ds(at, model // 2), :]
        for b in range(model // width):
            rows_at = slice(model // 2 + b * part, model // 2 + (b + 1) * part)
            columns = slice(b * width, (b + 1) * width)
            ref[rows_at, :] = ddown_ref[pl.ds(pl.multiple_of(base, 16), part), columns]
    for j, ref in enumerate(p_refs):
        hidden = hidden_ref[j * rows : (j + 1) * rows, :]
        ref[...] = dot_nn(hidden, down_ref[...]).astype(BF)


def ffn_norm_back_kernel(count, *refs):
    q_refs = refs[:count]
    mid_ref, g_ref, gain_ref, gm_ref, small_ref = refs[count:]
    grad_n = q_refs[0][...].astype(F32)
    for ref in q_refs[1:]:
        grad_n = grad_n + ref[...].astype(F32)
    scaled, reciprocal = norm_parts(mid_ref[...].astype(F32))
    g = g_ref[...].astype(F32)
    gm = (g + norm_back(grad_n, scaled, reciprocal, gain_ref[...])).astype(BF)
    gm_ref[...] = gm
    small_ref[0:1, :] = column_sum(gm.astype(F32))
    small_ref[1:2, :] = column_sum(grad_n * scaled)
    small_ref[2:3, :] = column_sum(grad_n)
    small_ref[3:4, :] = column_sum(g)


def attn_backward_kernel(
    heads,
    step,
    out_at,
    ids_ref,
    w_ref,
    proj_ref,
    gm_ref,
    gm_sib_ref,
    wout_ref,
    gproj_ref,
    gn_own_ref,
    gn_sib_ref,
    bias_ref,
    gctx_ref,
    turned_ref,
):
    half = gm_ref.shape[0]
    width = proj_ref.shape[1] // 3
    size = width // heads
    scale = size ** (-0.5)
    core = ids_ref[1]
    mine = pl.ds(pl.multiple_of(core * width, 64), width)
    w_out = wout_ref[mine, out_at : out_at + gm_ref.shape[1]]
    for row, ref in ((0, gm_ref), (half, gm_sib_ref)):
        gctx_ref[row : row + half, :] = dot_nt(ref[...], w_out).astype(BF)
    valid = key_valid_column(ids_ref, half)
    for h in range(heads):
        at = h * size
        q_at, k_at, v_at = (slice(s * width + at, s * width + at + size) for s in range(3))
        queries, key_rows, value_rows = proj_ref[:, q_at], proj_ref[:, k_at], proj_ref[:, v_at]
        probs = head_probs(queries, key_rows, valid)
        gctx = gctx_ref[:, at : at + size]
        grad_probs = dot_nt(value_rows, gctx)
        inner = jnp.sum(probs * grad_probs, axis=0, keepdims=True)
        grad_scores = (probs * (grad_probs - inner)).astype(BF)
        turned_ref[at : at + size, :] = dot_tn(key_rows, grad_scores) * scale
        gproj_ref[:, k_at] = (dot_nn(grad_scores, queries) * scale).astype(BF)
        gproj_ref[:, v_at] = dot_nn(probs.astype(BF), gctx).astype(BF)
    gproj_ref[:, :width] = turned_ref[...].T.astype(BF)
    bias_ref[...] = column_sum(gproj_ref[...].astype(F32))
    grad_n = dot_nt(gproj_ref[...], own_columns(w_ref, step, core, 3 * width))
    gn_own_ref[...] = grad_n[:half, :]
    gn_sib_ref[...] = grad_n[half:, :].astype(BF)


def attn_weights_kernel(
    count,
    ids_ref,
    own_ref,
    sib_ref,
    gain_ref,
    shift_ref,
    ctx_ref,
    other_ref,
    gm_ref,
    gm_sib_ref,
    gproj_ref,
    *refs,
):
    out_refs, full_ref = refs[:-1], refs[-1]
    half = own_ref.shape[0]
    width = ctx_ref.shape[1]
    core, chip = ids_ref[1], ids_ref[2]
    gm = jnp.concatenate([gm_ref[...], gm_sib_ref[...]], axis=0)
    middle = gm.shape[1] // 2
    gm_part = jnp.where(core == 0, gm[:, :middle].astype(F32), gm[:, middle:].astype(F32)).astype(BF)
    other = jnp.concatenate([other_ref[half:, :], other_ref[:half, :]], axis=0)
    mine = pl.ds(pl.multiple_of(core * width, 64), width)
    theirs = pl.ds(pl.multiple_of((1 - core) * width, 64), width)
    full_ref[mine, 3 * width :] = dot_tn(ctx_ref[...], gm_part).astype(BF)
    full_ref[theirs, 3 * width :] = dot_tn(other, gm_part).astype(BF)
    stream = jnp.concatenate([own_ref[...], sib_ref[...]], axis=0)
    scaled, _ = norm_parts(stream.astype(F32))
    normed = (scaled * gain_ref[...] + shift_ref[...]).astype(BF)
    full_ref[:, : 3 * width] = dot_tn(normed, gproj_ref[...]).astype(BF)
    if len(out_refs) == count:
        rows = out_refs[0].shape[0]
        for j, ref in enumerate(out_refs):
            ref[...] = full_ref[pl.ds(pl.multiple_of((chip ^ j) * rows, 16), rows), :]
    else:
        out_refs[0][...] = full_ref[...]


def attn_norm_back_kernel(gn_ref, recv_ref, own_ref, gm_ref, gain_ref, gs_ref, small_ref):
    grad_n = gn_ref[...] + recv_ref[...].astype(F32)
    scaled, reciprocal = norm_parts(own_ref[...].astype(F32))
    term = norm_back(grad_n, scaled, reciprocal, gain_ref[...])
    gs_ref[...] = (gm_ref[...].astype(F32) + term).astype(BF)
    small_ref[0:1, :] = column_sum(grad_n * scaled)
    small_ref[1:2, :] = column_sum(grad_n)


def pack_kernel(step, count, places_ref, qkv_ref, out_ref, up_ref, *refs):
    small_refs, (mine_ref, theirs_ref, rest_ref) = refs[:8], refs[8:11]
    chip, share = places_ref[1], up_ref.shape[2] // count
    for j, ref in enumerate(refs[11:]):
        ref[:, : out_ref.shape[2]] = out_ref[0]
        at = pl.multiple_of((chip ^ j) * share, 128)
        ref[:, out_ref.shape[2] :] = up_ref[0, :, pl.ds(at, share)]
    width = out_ref.shape[2]
    cols = width // 2
    core = places_ref[0]

    def columns(l, c):
        return jnp.concatenate(
            [qkv_ref[l, :, s * width + c * cols : s * width + (c + 1) * cols] for s in range(3)],
            axis=1,
        )

    first, second = columns(0, 0).astype(F32), columns(0, 1).astype(F32)
    smalls = jnp.concatenate([ref[...].astype(F32) for ref in small_refs], axis=0).T.astype(BF)
    for flag, ref in ((core == 0, mine_ref), (core != 0, theirs_ref)):
        ref[:, : 3 * cols] = jnp.where(flag, first, second).astype(BF)
        ref[:, 3 * cols :] = smalls
    rest_ref[...] = jnp.zeros_like(rest_ref)
    for c in range(2):
        rest_ref[:, c * step : c * step + 3 * cols] = columns(1, c)
    rest_ref[:, 2 * step :] = out_ref[1]


def run(micros, kernel, outs, operands, scratch=(), smem=0):
    vmem = pl.BlockSpec(memory_space=pltpu.VMEM)
    specs = [pl.BlockSpec(memory_space=pltpu.SMEM)] * smem + [vmem] * (len(operands) - smem)
    moved = sum(o.size * o.dtype.itemsize for o in list(operands) + list(outs))
    return pl.pallas_call(
        kernel,
        out_shape=[jax.ShapeDtypeStruct(o.shape, o.dtype) for o in outs],
        in_specs=specs,
        out_specs=[vmem] * len(outs),
        scratch_shapes=[pltpu.VMEM(shape, dtype) for shape, dtype in scratch],
        cost_estimate=pl.CostEstimate(
            flops=int(micros * 1.1e9), bytes_accessed=moved, transcendentals=0
        ),
        compiler_params=pltpu.CompilerParams(vmem_limit_bytes=VMEM_LIMIT),
    )(*operands)


def like(shape, dtype):
    return jax.ShapeDtypeStruct(shape, dtype)


def swap(x, axis, bit):
    size = lax.axis_size(axis)
    return lax.ppermute(x, axis, [(i, i ^ bit) for i in range(size)])


def to_sibling(x):
    return swap(x, "dp", 1)


def swap_chip(x, j):
    return swap(x, "dp", 2 * j)


def pick(x, index):
    return lax.dynamic_index_in_dim(x, index, 0, keepdims=False)


def in_order(parts, index):
    parts, bit = list(parts), 1
    while bit < len(parts):
        flag = (index & bit) != 0
        parts = [jnp.where(flag, parts[i ^ bit], parts[i]) for i in range(len(parts))]
        bit *= 2
    return parts


def spread(x, count):
    return [x] + [swap_chip(x, j) for j in range(1, count)]


def trade(blocks, chip, count):
    return [pick(blocks, chip)] + [swap_chip(pick(blocks, chip ^ j), j) for j in range(1, count)]


def total(parts):
    return functools.reduce(lambda a, b: a + b, [p.astype(F32) for p in parts])


def section_sum(x, z):
    low, high = z % 2, z // 2
    x = x.reshape((2, 2, x.shape[0] // 4) + x.shape[1:])
    half = total([pick(x, low), swap(pick(x, 1 - low), "section", 1)]).astype(BF)
    quarter = total([pick(half, high), swap(pick(half, 1 - high), "section", 2)]).astype(BF)
    half = jnp.stack(in_order([quarter, swap(quarter, "section", 2)], high))
    whole = jnp.stack(in_order([half, swap(half, "section", 1)], low))
    return whole.reshape((-1,) + x.shape[3:])


def section_streams(own, z, core):
    far = swap(own, "section", 2)
    near = swap(jnp.stack([own, far]), "section", 1)
    crops = in_order([own, near[0], far, near[1]], z)
    mine = jnp.where(core == 0, jnp.stack(crops[:2]), jnp.stack(crops[2:]))
    theirs = jnp.where(core == 0, jnp.stack(crops[2:]), jnp.stack(crops[:2]))
    recv = to_sibling(theirs)
    return jnp.concatenate(
        [jnp.where(core == 0, mine, recv), jnp.where(core == 0, recv, mine)], axis=1
    )


def after(x, *others):
    return lax.optimization_barrier((x, *others))[0]


def shards(
    residues,
    out_grad,
    key_lengths,
    masked,
    attn_gain,
    attn_shift,
    qkv_weight,
    query_bias,
    value_bias,
    out_weight,
    out_bias,
    ffn_gain,
    ffn_shift,
    up_weight,
    up_bias,
    down_weight,
    down_bias,
):
    data_count = lax.axis_size("dp")
    count = data_count // 2
    z = lax.axis_index("section")
    device = lax.axis_index("dp")
    core, chip = device % 2, device // 2
    layers, piece, triple = qkv_weight.shape
    width = triple // 3
    ff = up_weight.shape[2]
    ff_chip = ff // count
    heads = HEADS // 2
    cols = width // 2
    length = residues.shape[1]
    half = length // 2
    holder = core == z // 2
    vectors = 8
    step = -(-3 * cols // 128) * 128
    row = like((half, width), BF)

    smalls = [
        attn_gain,
        attn_shift,
        query_bias,
        value_bias,
        out_bias,
        ffn_gain,
        ffn_shift,
        down_bias,
    ]
    places = jnp.stack([core, chip]).astype(jnp.int32)
    packed = like((piece, 3 * cols + layers * vectors), BF)
    aligned = ff_chip % 128 == 0
    qkv_mine, qkv_theirs, rest1, *feed0 = run(
        2.2,
        functools.partial(pack_kernel, step, count),
        [packed, packed, like((piece, 2 * step + width), BF)]
        + [like((piece, width + ff_chip), BF)] * (count if aligned else 0),
        [places, qkv_weight, out_weight, up_weight, *smalls],
        smem=1,
    )
    if not aligned:
        feed0 = [
            jnp.concatenate(
                [out_weight[0], lax.dynamic_slice_in_dim(up_weight[0], (chip ^ j) * ff_chip, ff_chip, 1)],
                axis=1,
            )
            for j in range(count)
        ]
    pair = jnp.stack(in_order([qkv_mine, to_sibling(qkv_theirs)], core))

    residues, out_grad, key_lengths = lax.optimization_barrier(
        (residues, out_grad, key_lengths, qkv_theirs)
    )[:3]
    length_own = lax.dynamic_slice_in_dim(key_lengths, z % 2, 1, 0)
    length_here = jnp.where(holder, length_own, to_sibling(length_own))
    ids = jnp.concatenate([length_here, places])
    stream0 = pick(residues, z % 2)
    grad0 = pick(out_grad, z % 2) * pick(masked, z % 2).astype(BF)[:, None]
    stream_recv = to_sibling(stream0)
    grad_recv = to_sibling(lax.dynamic_slice_in_dim(grad0, (1 - core) * half, half, 0))
    stream0 = jnp.where(holder, stream0, stream_recv)
    g_top = jnp.where(holder, lax.dynamic_slice_in_dim(grad0, core * half, half, 0), grad_recv)
    own = lax.dynamic_slice_in_dim(stream0, core * half, half, 0)
    sib = lax.dynamic_slice_in_dim(stream0, (1 - core) * half, half, 0)

    qkv0 = jnp.stack(in_order(spread(pair, count), chip))
    qkv0 = qkv0.reshape(width, 3 * cols + layers * vectors)
    small_full = qkv0[:, 3 * cols :].T.astype(F32)
    small_full = jnp.swapaxes(small_full.reshape(vectors, layers, 1, width), 0, 1)

    def trade_up(l, dep):
        own_up = after(up_weight[l], dep)

        def block(i):
            return lax.dynamic_slice_in_dim(own_up, i * ff_chip, ff_chip, 1)

        return [block(chip)] + [swap_chip(block(chip ^ j), j) for j in range(1, count)]

    def join(parts):
        got = jnp.stack(in_order(parts, chip))
        both = jnp.stack(in_order([got, to_sibling(got)], core), axis=1)
        return both.reshape(width, -1)

    def chip_rows(own_down):
        return jnp.concatenate(in_order([own_down, to_sibling(own_down)], core), axis=0)

    feed0 = [feed0[0]] + [swap_chip(feed0[j], j) for j in range(1, count)]
    own, *feed0 = lax.optimization_barrier((own, *feed0))
    g_sent = spread(after(g_top, qkv0), count)
    upb = jnp.concatenate(in_order([up_bias, to_sibling(up_bias)], core), axis=1).astype(F32)
    zero_cols = jnp.zeros((1, cols), F32)

    def vec(l, i):
        return small_full[l, i]

    def core_bias(l):
        q = jnp.where(core == 0, vec(l, 2)[:, :cols], vec(l, 2)[:, cols:])
        v = jnp.where(core == 0, vec(l, 3)[:, :cols], vec(l, 3)[:, cols:])
        return jnp.concatenate([q, zero_cols, v], axis=1)

    qkv_full, qkv_step, out_at = [qkv0, None], [0, step], [0, 2 * step]
    up_full, down_full, out_full = [None, None], [None, None], [None, None]
    saved = []
    for l in range(layers):
        proj, ctx = run(
            6,
            functools.partial(attn_forward_kernel, heads, qkv_step[l]),
            [like((length, 3 * cols), BF), like((length, cols), BF)],
            [ids, own, sib, vec(l, 0), vec(l, 1), qkv_full[l], core_bias(l)],
            smem=1,
        )
        if l == 0:
            ctx, *g_parts = lax.optimization_barrier((ctx, *g_sent))
            out_full[0] = up_full[0] = join(feed0)
            down_full[0] = chip_rows(after(down_weight[0], own))
            rest1 = lax.all_gather(after(rest1, ctx), "dp", axis=0, tiled=True)
            qkv_full[1] = out_full[1] = rest1
        else:
            ctx, *up1 = lax.optimization_barrier((ctx, *up1))
            up_full[1] = join(up1)
            down_full[1] = chip_rows(after(down_weight[1], own))
        other = to_sibling(ctx)
        mid, normed2 = run(
            2.6,
            functools.partial(out_kernel, out_at[l]),
            [row, row],
            [ids, ctx, other, own, out_full[l], vec(l, 4), vec(l, 5), vec(l, 6)],
            smem=1,
        )
        parts = spread(normed2, count)
        saved.append((own, sib, proj, ctx, other, mid, parts))
        if l + 1 < layers:
            sums = run(
                6,
                functools.partial(ffn_forward_kernel, count),
                [row] * count,
                [*parts, up_full[l], upb[l][None], down_full[l]],
                scratch=[((count * half, width), F32)],
            )
            got = [sums[0]] + [swap_chip(sums[j], j) for j in range(1, count)]
            own = (total([mid, *got]) + vec(l, 7)).astype(BF)
            sib = to_sibling(own)
            up1 = trade_up(1, own)

    small_grads, upb_grads, ffn_grads, attn_grads = {}, {}, {}, {}
    for l in reversed(range(layers)):
        own, sib, proj, ctx, other, mid, parts = saved[l]
        top = l + 1 == layers
        wide = like((count * half, ff_chip), BF)
        results = run(
            8.3,
            functools.partial(ffn_backward_kernel, count),
            [row] * count + [wide, wide, like((1, ff_chip), F32)],
            [*parts, *g_parts, up_full[l], upb[l][None], down_full[l]],
            scratch=[((count * half, width), F32)],
        )
        sums, (hidden, grad_up, upb_grads[l]) = results[:count], results[count:]
        got = [sums[0]] + [swap_chip(sums[j], j) for j in range(1, count)]
        form = like((width, ff_chip), BF)
        fw_own, fw_sib, dup, *outs = run(
            5,
            functools.partial(ffn_weights_kernel, count),
            [form, form, form] + ([row] * count if top else []),
            [ids, *parts, *g_parts, hidden, grad_up, down_full[l]],
            scratch=[((ff_chip, width), BF)],
            smem=1,
        )
        if piece % 16 != 0:
            by_core = jnp.moveaxis(dup.reshape(count, 2, piece, ff_chip), 1, 0)
            order = jnp.arange(count) ^ chip
            blocks = [
                jnp.take(pick(by_core, c), order, axis=0).reshape(cols, ff_chip)
                for c in (core, 1 - core)
            ]
            fw_own = jnp.concatenate([blocks[0], fw_own[cols:]], axis=0)
            fw_sib = jnp.concatenate([blocks[1], fw_sib[cols:]], axis=0)
        got[1] = after(got[1], fw_own)
        if not top:
            final_got = lax.optimization_barrier((*final_got, sums[0]))[:-1]
            final = (total([final_mid, *final_got]) + vec(1, 7)).astype(BF)
            final_stream = section_streams(final, z, core)
        grad_mid, small_ffn = run(
            2.3,
            functools.partial(ffn_norm_back_kernel, count),
            [row, like((4, width), F32)],
            [*got, mid, g_parts[0], vec(l, 5)],
        )
        gm_sib = to_sibling(grad_mid)
        fw_recv = to_sibling(after(fw_sib, grad_mid))
        if top:
            outs = lax.optimization_barrier((*outs, gm_sib))[:-1]
            final_got = [outs[0]] + [swap_chip(outs[j], j) for j in range(1, count)]
            final_mid = mid

        gproj, gn_own, gn_sib, gproj_sum = run(
            8,
            functools.partial(attn_backward_kernel, heads, qkv_step[l], out_at[l]),
            [like((length, 3 * cols), BF), like((half, width), F32), row, like((1, 3 * cols), F32)],
            [ids, qkv_full[l], proj, grad_mid, gm_sib, out_full[l]],
            scratch=[((length, cols), BF), ((cols, length), F32)],
            smem=1,
        )
        gn_recv = to_sibling(gn_sib)
        fw_sum = total([fw_own, fw_recv]).astype(BF)
        gn_recv, fw_sum = lax.optimization_barrier((gn_recv, fw_sum))
        if top:
            ffn_grads[1] = lax.psum(fw_sum, "section")
        else:
            order = [list(reversed(range(lax.axis_size("section"))))]
            up_sum = lax.psum(fw_sum[:cols], "section", axis_index_groups=order)
        block_form = 2 * piece % 16 == 0
        packed = run(
            3.8,
            functools.partial(attn_weights_kernel, count),
            [like((2 * piece, 4 * cols), BF)] * count
            if block_form
            else [like((width, 4 * cols), BF)],
            [ids, own, sib, vec(l, 0), vec(l, 1), ctx, other, grad_mid, gm_sib, gproj],
            scratch=[((width, 4 * cols), BF)],
            smem=1,
        )
        if not block_form:
            packed = packed[0].reshape(count, 2 * piece, 4 * cols)
            packed = [pick(packed, chip ^ j) for j in range(count)]
        grad_stream, small_attn = run(
            2.2,
            attn_norm_back_kernel,
            [row, like((2, width), F32)],
            [gn_own, gn_recv, own, grad_mid, vec(l, 0)],
        )
        if top:
            g_parts = spread(grad_stream, count)
            packed = list(lax.optimization_barrier((*packed, *g_parts)))
            packed, g_parts = packed[:count], packed[count:]
        else:
            residues_grad = section_streams(grad_stream, z, core).astype(F32)
        sent = [packed[0]] + [swap_chip(packed[j], j) for j in range(1, count)]

        def chip_sum(sent):
            packed = total(sent).astype(BF).reshape(2, piece, 4 * cols)
            mine, theirs = pick(packed, core), pick(packed, 1 - core)
            both = jnp.stack(in_order([mine, to_sibling(theirs)], core))
            return both.reshape(2 * piece, 4 * cols)

        if top:
            sent_top, sum_top = sent, chip_sum
        else:
            down_sum = section_sum(fw_sum[cols:], z)
            sent_top = lax.optimization_barrier((*sent_top, grad_stream))[:-1]
            sent = list(lax.optimization_barrier((*sent, grad_stream))[:-1])
            attn_grads[1] = section_sum(sum_top(sent_top), z)
            both, up_sum, ffn_grads[1] = lax.optimization_barrier(
                (chip_sum(sent), up_sum, ffn_grads[1])
            )
            attn_grads[0] = lax.psum(both, "section")
            start = after(ffn_grads[1], grad_stream)
            ffn_blocks = {
                1: (start[:cols], start[cols:]),
                0: (up_sum, down_sum),
            }
        q_sum, v_sum = gproj_sum[:, :cols], gproj_sum[:, 2 * cols :]
        spread_out = [
            jnp.where(core == 0, jnp.concatenate([s, zero_cols], 1), jnp.concatenate([zero_cols, s], 1))
            for s in (q_sum, v_sum)
        ]
        small_grads[l] = jnp.concatenate([small_attn, *spread_out, small_ffn], axis=0)

    packed = jnp.stack([small_grads[l] for l in range(layers)])
    packed = jnp.transpose(
        packed.reshape(layers, vectors, count, 2, piece), (2, 3, 0, 1, 4)
    ).reshape(count, 2, layers * vectors * piece)
    packed = total(trade(packed, chip, count))
    biases = jnp.stack([upb_grads[l] for l in range(layers)]).reshape(layers, 2, ff_chip // 2)
    biases = jnp.transpose(biases, (1, 0, 2)).reshape(2, layers * (ff_chip // 2))
    packed = jnp.concatenate([packed, biases], axis=1)
    packed = pick(packed, core) + to_sibling(pick(packed, 1 - core))
    one = packed + swap(packed, "section", 1)
    packed = one + swap(one, "section", 2)
    split = layers * vectors * piece
    grads = packed[:split].reshape(layers, vectors, piece)
    up_bias_grad = packed[split:].reshape(layers, ff_chip // 2)

    def weights(l):
        both = attn_grads[l].reshape(2, piece, 4, cols)
        qkv = jnp.transpose(both[:, :, :3], (1, 2, 0, 3)).reshape(piece, triple)
        out = jnp.transpose(both[:, :, 3], (1, 0, 2)).reshape(piece, width)
        blocks, down = ffn_blocks[l]
        blocks = [blocks[j * piece : (j + 1) * piece] for j in range(count)]
        up = in_order([blocks[0]] + [swap_chip(blocks[j], j) for j in range(1, count)], chip)
        if ff_chip >= width:
            down = [down[:, b : b + width] for b in range(0, ff_chip, width)]
            down = jnp.concatenate(down, axis=0)
        else:
            rows = ff_chip // 2
            down = [down[b : b + rows] for b in range(0, cols, rows)]
            down = jnp.concatenate(down, axis=1)
        return qkv, out, jnp.concatenate(up, axis=1), down

    per_layer = [weights(l) for l in range(layers)]
    stacked = [jnp.stack([p[i] for p in per_layer]).astype(F32) for i in range(4)]
    return (
        final_stream,
        residues_grad,
        grads[:, 0],
        grads[:, 1],
        stacked[0],
        grads[:, 2],
        grads[:, 3],
        stacked[1],
        grads[:, 4],
        grads[:, 5],
        grads[:, 6],
        stacked[2],
        up_bias_grad,
        stacked[3],
        grads[:, 7],
    )


def solution(mesh):
    rows, vector, matrix = P("dp", None, None), P(None, "dp"), P(None, "dp", None)
    weights = (
        vector,
        vector,
        matrix,
        vector,
        vector,
        matrix,
        vector,
        vector,
        vector,
        matrix,
        vector,
        matrix,
        vector,
    )
    return jax.shard_map(
        shards,
        mesh=mesh,
        in_specs=(rows, rows, P("dp"), P("dp", None), *weights),
        out_specs=(rows, rows, *weights),
        check_vma=False,
    )
```

time: 1780 us -> 421 us (0.24)
  waiting for transfers between devices: 1150 us -> 169 us
  local copies, waits for them, and re-layouts: 311 us -> 33.8 us
  other arithmetic: 147 us -> 30.6 us
  Pallas kernels: 0 us -> 94.1 us
  matrix products: 60.3 us -> 0 us
  loops' own time: 43.1 us -> 0 us
  starting transfers between devices: 29.4 us -> 72.1 us
    unnamed x5 -> x4, waiting for transfers between devices: 494 us -> 0.07 us
    ppermute x8 -> x85, waiting for transfers between devices: 476 us -> 158 us  [swap(): return lax.ppermute(x, axis, [(i, i ^ bit) for i in range(size)])]
    psum x1 -> x3, waiting for transfers between devices: 176 us -> 10.6 us  [the longest x1 10.6 us: shards(): attn_grads[0] = lax.psum(both, 'section')]
    pallas_call x0 -> x18, Pallas kernels: none -> 94.1 us  [run(): pl.pallas_call(kernel, out_shape=[jax.ShapeDtypeStruct(o.shape, o.dtype)...]
    reshape x29 -> x2, local copies, waits for them, and re-layouts: 66.6 us -> 1.44 us  [the longest x1 1.33 us: weights(): both = attn_grads[l].reshape(2, piece, 4, cols)]
    dot_general x82 -> x0, matrix products: 60.3 us -> none  [the longest x2 8.52 us: attention_backward(): jnp.dot(normed.astype(jnp.bfloat16).T, grad_proj, preferred_element_type=...]
    cond x28 -> x0, local copies, waits for them, and re-layouts: 54.1 us -> none
    add x2 -> x4, other arithmetic: 51.4 us -> 0.02 us  [the longest x1 0.01 us: total(): return functools.reduce(lambda a, b: a + b, [p.astype(F32) for p in parts])]
  transfers between devices with their start and end apart: 11 -> 89, of which waited for: 11 -> 32; matrix products, arithmetic and copies ran while one was open for 1% -> 11% of each run, Pallas kernels for 0% -> 19%
where the time goes in v1:
time: 421 us; the launch traced here: 416 us
  waiting for transfers between devices  169 us (40%)
  Pallas kernels  94.1 us (22%)
  starting transfers between devices  72.1 us (17%)
  local copies, waits for them, and re-layouts  33.8 us (8%)
  other arithmetic  30.6 us (7%)
  between operations  16.6 us (4%)
    ppermute x85, waiting for transfers between devices, swap(): return lax.ppermute(x, axis, [(i, i ^ bit) for i in range(size)])  158 us
    pallas_call x18, Pallas kernels, run(): pl.pallas_call(kernel, out_shape=[jax.ShapeDtypeStruct(o.shape, o.dtype)...  94.1 us
    ppermute x85, starting transfers between devices, swap(): return lax.ppermute(x, axis, [(i, i ^ bit) for i in range(size)])  71.8 us
    unnamed x137, local copies, waits for them, and re-layouts  10.7 us
    psum x1, waiting for transfers between devices, shards(): attn_grads[0] = lax.psum(both, 'section')  10.6 us
  transfers between devices with their start and end apart: 89, of which 32 were waited for; matrix products, arithmetic and copies ran while one was open for 11% of the time, Pallas kernels for 19%

profile of v1, /device:TPU:0, one launch (start us, length us, event | category | flops | bytes accessed | tf_op | source)
XLA Modules:
  0.0 416.0 jit_solution(5367550908202992967)
XLA Ops:
  27.5 10.4 %collective-permute-done.3 = bf16[80,1920]{1,0:T(8,128)(2,1)S(1)} collective-permute-done((bf16[80,1920]{1,0:T(8,128)(2,1)}, bf16[80,1920]{1,0:T(8,128)(2,1)S(1)}, u32[]{:S(2)}, u32[]{:S(2)}) %collective-permute-start.3) | collective-permute-done | bytes 307232 | tf_op jit(solution)/shard_map/ppermute | solution.py:375
  38.2 6.4 %collective-permute-done.7 = bf16[2,80,976]{2,1,0:T(8,128)(2,1)S(1)} collective-permute-done((bf16[2,80,976]{2,1,0:T(8,128)(2,1)S(1)}, bf16[2,80,976]{2,1,0:T(8,128)(2,1)S(1)}, u32[]{:S(2)}, u32[]{:S(2)}) %collective-permute-start.7) | collective-permute-done | bytes 312352 | tf_op jit(solution)/shard_map/ppermute | solution.py:375
  50.3 5.9 %shard_map.281 = (bf16[256,960]{1,0:T(8,128)(2,1)}, bf16[256,320]{1,0:T(8,128)(2,1)}) custom-call(s32[3]{0:T(128)} %pad_add_fusion.1.ids_ref.refs_0_, bf16[128,640]{1,0:T(8,128)(2,1)} %get-tuple-element.146.own_ref, bf16[128,640]{1,0:T(8,128)(2,1)} %get-tuple-element.337.sib_ref, f32[1,640]{1,0:T(1,128)} %get-tuple-element.359.gain_ref, ...), custom_call_target="tpu_custom_call" | custom-call | flops 6600000000 | bytes 2241292 | tf_op jit(solution)/shard_map/pallas_call | solution.py:356
  75.3 4.2 %collective-permute-done.17.refs_3_.refs_4_ = bf16[128,640]{1,0:T(8,128)(2,1)S(1)} collective-permute-done((bf16[128,640]{1,0:T(8,128)(2,1)}, bf16[128,640]{1,0:T(8,128)(2,1)S(1)}, u32[]{:S(2)}, u32[]{:S(2)}) %collective-permute-start.17) | collective-permute-done | bytes 163872 | tf_op jit(solution)/shard_map/ppermute | solution.py:375
  80.1 6.0 %shard_map.283 = (bf16[128,640]{1,0:T(8,128)(2,1)}, bf16[128,640]{1,0:T(8,128)(2,1)}, bf16[128,640]{1,0:T(8,128)(2,1)}, bf16[128,640]{1,0:T(8,128)(2,1)}) custom-call(bf16[128,640]{1,0:T(8,128)(2,1)} %get-tuple-element.157.refs_0_.refs_1_, bf16[128,640]{1,0:T(8,128)(2,1)} %copy-done.40, bf16[128,640]{1,0:T(8,128)(2,1)} %copy-done.41, ...), custom_call_target="tpu_custom_call" | custom-call | flops 6600000000 | bytes 5411840 | tf_op jit(solution)/shard_map/pallas_call | solution.py:356
  89.7 3.7 collective-permute-done.20
  93.4 3.5 collective-permute-done.22
  101.9 6.5 %shard_map.284 = (bf16[256,960]{1,0:T(8,128)(2,1)}, bf16[256,320]{1,0:T(8,128)(2,1)}) custom-call(s32[3]{0:T(128)} %pad_add_fusion.1.ids_ref.refs_0_, bf16[128,640]{1,0:T(8,128)(2,1)} %copy-done.21, bf16[128,640]{1,0:T(8,128)(2,1)} %copy-done.46, f32[1,640]{1,0:T(1,128)} %get-tuple-element.350.gain_ref, f32[1,640]{1,0:T(1,128)} %get-tuple-element.349.shift_ref, ...), custom_call_target="tpu_custom_call" | custom-call | flops 6600000000 | bytes 4432652 | tf_op jit(solution)/shard_map/pallas_call | solution.py:356
  113.2 3.4 shard_map.285
  123.8 3.7 collective-permute-done.29.refs_2_.refs_3_
  128.3 8.6 %shard_map.286 = (bf16[128,640]{1,0:T(8,128)(2,1)}, bf16[128,640]{1,0:T(8,128)(2,1)}, bf16[128,640]{1,0:T(8,128)(2,1)}, bf16[128,640]{1,0:T(8,128)(2,1)}, bf16[5...) custom-call(bf16[128,640]{1,0:T(8,128)(2,1)} %get-tuple-element.169.refs_0_.refs_1_, ...), custom_call_target="tpu_custom_call" | custom-call | flops 9130000384 | bytes 7874560 | tf_op jit(solution)/shard_map/pallas_call | solution.py:356
  140.4 7.7 %shard_map.287 = (bf16[640,1280]{1,0:T(8,128)(2,1)}, bf16[640,1280]{1,0:T(8,128)(2,1)}, bf16[640,1280]{1,0:T(8,128)(2,1)}, bf16[128,640]{1,0:T(8,128)(2,1)}, bf1...) custom-call(s32[3]{0:T(128)} %pad_add_fusion.1.ids_ref.refs_0_, ...), custom_call_target="tpu_custom_call" | custom-call | flops 5500000256 | bytes 11141132 | tf_op jit(solution)/shard_map/pallas_call | solution.py:356
  151.8 3.4 collective-permute-done.36.gm_sib_ref
  155.9 9.0 %shard_map.289 = (bf16[256,960]{1,0:T(8,128)(2,1)}, f32[128,640]{1,0:T(8,128)}, bf16[128,640]{1,0:T(8,128)(2,1)}, f32[1,960]{1,0:T(1,128)}) custom-call(s32[3]{0:T(128)} %pad_add_fusion.1.ids_ref.refs_0_, bf16[640,2688]{1,0:T(8,128)(2,1)} %all-gather.2.cloned.1.call-done.w_ref.wout_ref, bf16[256,960]{1,0:T(8,128)(2,1)} %get-tuple-element.196.proj_ref, ...), custom_call_target="tpu_custom_call" | custom-call | flops 8800000000 | bytes 8687372 | tf_op jit(solution)/shard_map/pallas_call | solution.py:356
  166.7 3.8 shard_map.290
  178.7 3.7 collective-permute-done.42.refs_5_.refs_6_
  184.3 4.6 %collective-permute-done.43.refs_6_.refs_7_ = bf16[128,640]{1,0:T(8,128)(2,1)S(1)} collective-permute-done((bf16[128,640]{1,0:T(8,128)(2,1)}, bf16[128,640]{1,0:T(8,128)(2,1)S(1)}, u32[]{:S(2)}, u32[]{:S(2)}) %collective-permute-start.43) | collective-permute-done | bytes 163872 | tf_op jit(solution)/shard_map/ppermute | solution.py:375
  189.6 8.6 %shard_map.292 = (bf16[128,640]{1,0:T(8,128)(2,1)}, bf16[128,640]{1,0:T(8,128)(2,1)}, bf16[128,640]{1,0:T(8,128)(2,1)}, bf16[128,640]{1,0:T(8,128)(2,1)}, bf16[5...) custom-call(bf16[128,640]{1,0:T(8,128)(2,1)} %get-tuple-element.157.refs_0_.refs_1_, ...), custom_call_target="tpu_custom_call" | custom-call | flops 9130000384 | bytes 8693760 | tf_op jit(solution)/shard_map/pallas_call | solution.py:356
  204.0 7.3 %shard_map.293 = (bf16[640,1280]{1,0:T(8,128)(2,1)}, bf16[640,1280]{1,0:T(8,128)(2,1)}, bf16[640,1280]{1,0:T(8,128)(2,1)}) custom-call(s32[3]{0:T(128)} %pad_add_fusion.1.ids_ref.refs_0_, bf16[128,640]{1,0:T(8,128)(2,1)} %get-tuple-element.157.refs_0_.refs_1_, bf16[128,640]{1,0:T(8,128)(2,1)} %copy-done.40, bf16[128,640]{1,0:T(8,128)(2,1)} %copy-done.41, ...), custom_call_target="tpu_custom_call" | custom-call | flops 5500000256 | bytes 10485772 | tf_op jit(solution)/shard_map/pallas_call | solution.py:356
  221.6 8.1 %shard_map.295 = (bf16[256,960]{1,0:T(8,128)(2,1)}, f32[128,640]{1,0:T(8,128)}, bf16[128,640]{1,0:T(8,128)(2,1)}, f32[1,960]{1,0:T(1,128)}) custom-call(s32[3]{0:T(128)} %pad_add_fusion.1.ids_ref.refs_0_, bf16[640,976]{1,0:T(8,128)(2,1)} %bitcast.283, bf16[256,960]{1,0:T(8,128)(2,1)} %get-tuple-element.217.proj_ref, ...), custom_call_target="tpu_custom_call" | custom-call | flops 8800000000 | bytes 5512972 | tf_op jit(solution)/shard_map/pallas_call | solution.py:356
  231.5 9.4 %collective-permute-done.46 = bf16[2,128,640]{2,1,0:T(8,128)(2,1)S(1)} collective-permute-done((bf16[2,128,640]{2,1,0:T(8,128)(2,1)S(1)}, bf16[2,128,640]{2,1,0:T(8,128)(2,1)S(1)}, u32[]{:S(2)}, u32[]{:S(2)}) %collective-permute-start.46) | collective-permute-done | bytes 327712 | tf_op jit(solution)/shard_map/ppermute | solution.py:375
  241.3 3.7 shard_map.297
  253.5 4.1 collective-permute-done.63
  257.6 10.2 %collective-permute-done.64 = bf16[160,1280]{1,0:T(8,128)(2,1)S(1)} collective-permute-done((bf16[160,1280]{1,0:T(8,128)(2,1)S(1)}, bf16[160,1280]{1,0:T(8,128)(2,1)S(1)}, u32[]{:S(2)}, u32[]{:S(2)}) %collective-permute-start.64) | collective-permute-done | bytes 409632 | tf_op jit(solution)/shard_map/ppermute | solution.py:375
  276.3 7.8 %collective-permute-done.69 = bf16[160,1280]{1,0:T(8,128)(2,1)S(1)} collective-permute-done((bf16[160,1280]{1,0:T(8,128)(2,1)S(1)}, bf16[160,1280]{1,0:T(8,128)(2,1)S(1)}, u32[]{:S(2)}, u32[]{:S(2)}) %collective-permute-start.69) | collective-permute-done | bytes 409632 | tf_op jit(solution)/shard_map/ppermute | solution.py:375
  285.3 5.0 %collective-permute-done.61 = f32[2560]{0:T(1024)S(1)} collective-permute-done((f32[2560]{0:T(1024)S(1)}, f32[2560]{0:T(1024)S(1)}, u32[]{:S(2)}, u32[]{:S(2)}) %collective-permute-start.61) | collective-permute-done | bytes 10272 | tf_op jit(solution)/shard_map/ppermute | solution.py:375
  290.5 4.4 %collective-permute-done.62 = f32[2560]{0:T(1024)S(1)} collective-permute-done((f32[2560]{0:T(1024)S(1)}, f32[2560]{0:T(1024)S(1)}, u32[]{:S(2)}, u32[]{:S(2)}) %collective-permute-start.62) | collective-permute-done | bytes 10272 | tf_op jit(solution)/shard_map/ppermute | solution.py:375
  299.8 26.6 %collective-permute-done.71 = bf16[2,40,1280]{2,1,0:T(8,128)(2,1)S(1)} collective-permute-done((bf16[2,40,1280]{2,1,0:T(8,128)(2,1)S(1)}, bf16[2,40,1280]{2,1,0:T(8,128)(2,1)S(1)}, u32[]{:S(2)}, u32[]{:S(2)}) %collective-permute-start.71) | collective-permute-done | bytes 204832 | tf_op jit(solution)/shard_map/ppermute | solution.py:375
  326.9 6.4 %collective-permute-done.72 = bf16[40,1280]{1,0:T(8,128)(2,1)S(1)} collective-permute-done((bf16[40,1280]{1,0:T(8,128)(2,1)S(1)}, bf16[40,1280]{1,0:T(8,128)(2,1)S(1)}, u32[]{:S(2)}, u32[]{:S(2)}) %collective-permute-start.72) | collective-permute-done | bytes 102432 | tf_op jit(solution)/shard_map/ppermute | solution.py:375
  336.4 13.3 %collective-permute-done.73 = bf16[40,1280]{1,0:T(8,128)(2,1)S(1)} collective-permute-done((bf16[40,1280]{1,0:T(8,128)(2,1)S(1)}, bf16[40,1280]{1,0:T(8,128)(2,1)S(1)}, u32[]{:S(2)}, u32[]{:S(2)}) %collective-permute-start.73) | collective-permute-done | bytes 102432 | tf_op jit(solution)/shard_map/ppermute | solution.py:375
  350.4 9.2 %collective-permute-done.83 = bf16[80,1280]{1,0:T(8,128)(2,1)S(1)} collective-permute-done((bf16[80,1280]{1,0:T(8,128)(2,1)S(1)}, bf16[80,1280]{1,0:T(8,128)(2,1)S(1)}, u32[]{:S(2)}, u32[]{:S(2)}) %collective-permute-start.83) | collective-permute-done | bytes 204832 | tf_op jit(solution)/shard_map/ppermute | solution.py:375
  392.1 10.6 %all-reduce.14.cloned.1.call-done = bf16[2,80,4,320]{3,2,1,0:T(4,128)(2,1)} async-done(((bf16[2,80,4,320]{3,2,1,0:T(4,128)(2,1)}), bf16[2,80,4,320]{3,2,1,0:T(4,128)(2,1)}) %all-reduce.14.cloned.1.call-update) | async-done | bytes 409616 | tf_op jit(solution)/shard_map/psum | solution.py:709
  (442 shorter events, 170.2 us)
Async XLA Ops:
  7.2 94.1 %all-gather.2.cloned.1.call-start = ((), (), s32[]{:S(2)}) async-start(), calls=%async_computation | async-start | bytes 3870720 | tf_op jit(solution)/shard_map/all_gather | solution.py:570
  14.8 23.1 %collective-permute-start.3 = (bf16[80,1920]{1,0:T(8,128)(2,1)}, bf16[80,1920]{1,0:T(8,128)(2,1)S(1)}, u32[]{:S(2)}, u32[]{:S(2)}) collective-permute-start(bf16[80,1920]{1,0:T(8,128)(2,1)} %get-tuple-element.144), channel_id=1, source_target_pairs={{0,4},{1,5},{2,6},{3,7},{4,0},{5,1},{6,2},{7,3},{8,12},{9,13},{10,... | collective-permute-start | bytes 921608 | tf_op jit(solution)/shard_map/ppermute | solution.py:375
  18.3 19.6 %collective-permute-start.4 = (bf16[80,1920]{1,0:T(8,128)(2,1)}, bf16[80,1920]{1,0:T(8,128)(2,1)S(1)}, u32[]{:S(2)}, u32[]{:S(2)}) collective-permute-start(bf16[80,1920]{1,0:T(8,128)(2,1)} %get-tuple-element.145), channel_id=1, source_target_pairs={{0,6},{1,7},{2,4},{3,5},{4,2},{5,3},{6,0},{7,1},{8,14},{9,15},{10,... | collective-permute-start | bytes 921608 | tf_op jit(solution)/shard_map/ppermute | solution.py:375
  21.6 16.7 %collective-permute-start.6 = (bf16[2,80,976]{2,1,0:T(8,128)(2,1)S(1)}, bf16[2,80,976]{2,1,0:T(8,128)(2,1)S(1)}, u32[]{:S(2)}, u32[]{:S(2)}) collective-permute-start(bf16[2,80,976]{2,1,0:T(8,128)(2,1)S(1)} %pad_maximum_fusion.11), channel_id=1, source_target_pairs={{0,6},{1,7},{2,4},{3,5},{4,2},{5,3},{6,0},{7,1},{8,14},{9,15},{10,... | collective-permute-start | bytes 936968 | tf_op jit(solution)/shard_map/ppermute | solution.py:375
  24.5 20.1 %collective-permute-start.7 = (bf16[2,80,976]{2,1,0:T(8,128)(2,1)S(1)}, bf16[2,80,976]{2,1,0:T(8,128)(2,1)S(1)}, u32[]{:S(2)}, u32[]{:S(2)}) collective-permute-start(bf16[2,80,976]{2,1,0:T(8,128)(2,1)S(1)} %pad_maximum_fusion.11), channel_id=1, source_target_pairs={{0,4},{1,5},{2,6},{3,7},{4,0},{5,1},{6,2},{7,3},{8,12},{9,13},{10,... | collective-permute-start | bytes 936968 | tf_op jit(solution)/shard_map/ppermute | solution.py:375
  25.2 19.4 %collective-permute-start.8 = (bf16[2,80,976]{2,1,0:T(8,128)(2,1)S(1)}, bf16[2,80,976]{2,1,0:T(8,128)(2,1)S(1)}, u32[]{:S(2)}, u32[]{:S(2)}) collective-permute-start(bf16[2,80,976]{2,1,0:T(8,128)(2,1)S(1)} %pad_maximum_fusion.11), channel_id=1, source_target_pairs={{0,2},{1,3},{2,0},{3,1},{4,6},{5,7},{6,4},{7,5},{8,10},{9,11},{10,... | collective-permute-start | bytes 936968 | tf_op jit(solution)/shard_map/ppermute | solution.py:375
  56.3 304.2 %all-reduce.12.cloned.1.call-start = ((), (), s32[]{:S(2)}) async-start(), calls=%async_computation.2 | async-start | bytes 3276800 | tf_op jit(solution)/shard_map/psum | solution.py:661
  151.2 19.3 %collective-permute-start.41 = (bf16[640,1280]{1,0:T(8,128)(2,1)}, bf16[640,1280]{1,0:T(8,128)(2,1)S(1)}, u32[]{:S(2)}, u32[]{:S(2)}) collective-permute-start(bf16[640,1280]{1,0:T(8,128)(2,1)} %get-tuple-element.205), channel_id=1, source_target_pairs={{0,1},{1,0},{2,3},{3,2},{4,5},{5,4},{6,7},{7,6},{8,9},{9,8},{10,11... | collective-permute-start | bytes 4915208 | tf_op jit(solution)/shard_map/ppermute | solution.py:375
  165.0 35.5 %collective-permute-start.37 = (bf16[128,640]{1,0:T(8,128)(2,1)S(1)}, bf16[128,640]{1,0:T(8,128)(2,1)S(1)}, u32[]{:S(2)}, u32[]{:S(2)}) collective-permute-start(bf16[128,640]{1,0:T(8,128)(2,1)S(1)} %copy-done.49), channel_id=1, source_target_pairs={{0,2},{1,3},{2,0},{3,1},{4,6},{5,7},{6,4},{7,5},{8,10},{9,11},{10,... | collective-permute-start | bytes 491528 | tf_op jit(solution)/shard_map/ppermute | solution.py:375
  165.8 36.7 %collective-permute-start.38 = (bf16[128,640]{1,0:T(8,128)(2,1)S(1)}, bf16[128,640]{1,0:T(8,128)(2,1)S(1)}, u32[]{:S(2)}, u32[]{:S(2)}) collective-permute-start(bf16[128,640]{1,0:T(8,128)(2,1)S(1)} %copy-done.48), channel_id=1, source_target_pairs={{0,4},{1,5},{2,6},{3,7},{4,0},{5,1},{6,2},{7,3},{8,12},{9,13},{10,... | collective-permute-start | bytes 491528 | tf_op jit(solution)/shard_map/ppermute | solution.py:375
  178.7 181.8 %all-reduce.10.cloned.1.call-start = ((), (), s32[]{:S(2)}) async-start(), calls=%async_computation.1 | async-start | bytes 1638400 | tf_op jit(solution)/shard_map/psum | solution.py:664
  182.5 20.1 %collective-permute-start.39 = (bf16[128,640]{1,0:T(8,128)(2,1)S(1)}, bf16[128,640]{1,0:T(8,128)(2,1)S(1)}, u32[]{:S(2)}, u32[]{:S(2)}) collective-permute-start(bf16[128,640]{1,0:T(8,128)(2,1)S(1)} %copy-done.47), channel_id=1, source_target_pairs={{0,6},{1,7},{2,4},{3,5},{4,2},{5,3},{6,0},{7,1},{8,14},{9,15},{10,... | collective-permute-start | bytes 491528 | tf_op jit(solution)/shard_map/ppermute | solution.py:375
  202.5 73.1 %collective-permute-start.67 = (bf16[160,1280]{1,0:T(8,128)(2,1)}, bf16[160,1280]{1,0:T(8,128)(2,1)S(1)}, u32[]{:S(2)}, u32[]{:S(2)}) collective-permute-start(bf16[160,1280]{1,0:T(8,128)(2,1)} %get-tuple-element.253), channel_id=1, source_target_pairs={{0,2},{1,3},{2,0},{3,1},{4,6},{5,7},{6,4},{7,5},{8,10},{9,11},{10,... | collective-permute-start | bytes 1228808 | tf_op jit(solution)/shard_map/ppermute | solution.py:375
  202.6 73.1 %collective-permute-start.68 = (bf16[160,1280]{1,0:T(8,128)(2,1)}, bf16[160,1280]{1,0:T(8,128)(2,1)}, u32[]{:S(2)}, u32[]{:S(2)}) collective-permute-start(bf16[160,1280]{1,0:T(8,128)(2,1)} %get-tuple-element.254), channel_id=1, source_target_pairs={{0,4},{1,5},{2,6},{3,7},{4,0},{5,1},{6,2},{7,3},{8,12},{9,13},{10,... | collective-permute-start | bytes 1228808 | tf_op jit(solution)/shard_map/ppermute | solution.py:375
  217.6 29.7 %collective-permute-start.53 = (bf16[640,1280]{1,0:T(8,128)(2,1)}, bf16[640,1280]{1,0:T(8,128)(2,1)S(1)}, u32[]{:S(2)}, u32[]{:S(2)}) collective-permute-start(bf16[640,1280]{1,0:T(8,128)(2,1)} %get-tuple-element.229), channel_id=1, source_target_pairs={{0,1},{1,0},{2,3},{3,2},{4,5},{5,4},{6,7},{7,6},{8,9},{9,8},{10,11... | collective-permute-start | bytes 4915208 | tf_op jit(solution)/shard_map/ppermute | solution.py:375
  220.9 20.0 %collective-permute-start.46 = (bf16[2,128,640]{2,1,0:T(8,128)(2,1)S(1)}, bf16[2,128,640]{2,1,0:T(8,128)(2,1)S(1)}, u32[]{:S(2)}, u32[]{:S(2)}) collective-permute-start(bf16[2,128,640]{2,1,0:T(8,128)(2,1)S(1)} %pad_maximum_fusion.12), channel_id=1, source_target_pairs={{0,8},{8,0},{16,24},{24,16},{1,9},{9,1},{17,25},{25,17},{2,10},{10... | collective-permute-start | bytes 983048 | tf_op jit(solution)/shard_map/ppermute | solution.py:375
  229.8 19.9 %collective-permute-start.52 = (bf16[128,640]{1,0:T(8,128)(2,1)}, bf16[128,640]{1,0:T(8,128)(2,1)S(1)}, u32[]{:S(2)}, u32[]{:S(2)}) collective-permute-start(bf16[128,640]{1,0:T(8,128)(2,1)} %get-tuple-element.227), channel_id=1, source_target_pairs={{0,1},{1,0},{2,3},{3,2},{4,5},{5,4},{6,7},{7,6},{8,9},{9,8},{10,11... | collective-permute-start | bytes 491528 | tf_op jit(solution)/shard_map/ppermute | solution.py:375
  247.3 20.5 %collective-permute-start.64 = (bf16[160,1280]{1,0:T(8,128)(2,1)S(1)}, bf16[160,1280]{1,0:T(8,128)(2,1)S(1)}, u32[]{:S(2)}, u32[]{:S(2)}) collective-permute-start(bf16[160,1280]{1,0:T(8,128)(2,1)S(1)} %copy-done.35), channel_id=1, source_target_pairs={{0,4},{1,5},{2,6},{3,7},{4,0},{5,1},{6,2},{7,3},{8,12},{9,13},{10,... | collective-permute-start | bytes 1228808 | tf_op jit(solution)/shard_map/ppermute | solution.py:375
  249.6 18.2 %collective-permute-start.65 = (bf16[160,1280]{1,0:T(8,128)(2,1)S(1)}, bf16[160,1280]{1,0:T(8,128)(2,1)S(1)}, u32[]{:S(2)}, u32[]{:S(2)}) collective-permute-start(bf16[160,1280]{1,0:T(8,128)(2,1)S(1)} %copy-done.34), channel_id=1, source_target_pairs={{0,6},{1,7},{2,4},{3,5},{4,2},{5,3},{6,0},{7,1},{8,14},{9,15},{10,... | collective-permute-start | bytes 1228808 | tf_op jit(solution)/shard_map/ppermute | solution.py:375
  275.0 21.2 %collective-permute-start.54 = (bf16[128,640]{1,0:T(8,128)(2,1)S(1)}, bf16[128,640]{1,0:T(8,128)(2,1)S(1)}, u32[]{:S(2)}, u32[]{:S(2)}) collective-permute-start(bf16[128,640]{1,0:T(8,128)(2,1)S(1)} %copy-done.8), channel_id=1, source_target_pairs={{0,16},{8,24},{16,0},{24,8},{1,17},{9,25},{17,1},{25,9},{2,18},{10... | collective-permute-start | bytes 491528 | tf_op jit(solution)/shard_map/ppermute | solution.py:375
  275.6 23.9 %collective-permute-start.81 = (bf16[2,80,1280]{2,1,0:T(8,128)(2,1)S(1)}, bf16[2,80,1280]{2,1,0:T(8,128)(2,1)S(1)}, u32[]{:S(2)}, u32[]{:S(2)}) collective-permute-start(bf16[2,80,1280]{2,1,0:T(8,128)(2,1)S(1)} %dynamic-slice_bitcast_fusion), channel_id=1, source_target_pairs={{0,8},{8,0},{16,24},{24,16},{1,9},{9,1},{17,25},{25,17},{2,10},{10... | collective-permute-start | bytes 1228808 | tf_op jit(solution)/shard_map/ppermute | solution.py:375
  275.7 22.8 %collective-permute-start.66 = (bf16[80,1280]{1,0:T(8,128)(2,1)S(1)}, bf16[80,1280]{1,0:T(8,128)(2,1)}, u32[]{:S(2)}, u32[]{:S(2)}) collective-permute-start(bf16[80,1280]{1,0:T(8,128)(2,1)S(1)} %dynamic-slice_bitcast_fusion.4), channel_id=1, source_target_pairs={{0,1},{1,0},{2,3},{3,2},{4,5},{5,4},{6,7},{7,6},{8,9},{9,8},{10,11... | collective-permute-start | bytes 614408 | tf_op jit(solution)/shard_map/ppermute | solution.py:375
  290.5 112.2 %all-reduce.14.cloned.1.call-start = ((), (), s32[]{:S(2)}) async-start(), calls=%async_computation.3 | async-start | bytes 983040 | tf_op jit(solution)/shard_map/psum | solution.py:709
  296.2 30.4 %collective-permute-start.55 = (bf16[2,128,640]{2,1,0:T(8,128)(2,1)S(1)}, bf16[2,128,640]{2,1,0:T(8,128)(2,1)S(1)}, u32[]{:S(2)}, u32[]{:S(2)}) collective-permute-start(bf16[2,128,640]{2,1,0:T(8,128)(2,1)S(1)} %pad_maximum_fusion.15), channel_id=1, source_target_pairs={{0,8},{8,0},{16,24},{24,16},{1,9},{9,1},{17,25},{25,17},{2,10},{10... | collective-permute-start | bytes 983048 | tf_op jit(solution)/shard_map/ppermute | solution.py:375
  296.4 29.9 %collective-permute-start.71 = (bf16[2,40,1280]{2,1,0:T(8,128)(2,1)S(1)}, bf16[2,40,1280]{2,1,0:T(8,128)(2,1)S(1)}, u32[]{:S(2)}, u32[]{:S(2)}) collective-permute-start(bf16[2,40,1280]{2,1,0:T(8,128)(2,1)S(1)} %fusion.4), channel_id=1, source_target_pairs={{0,8},{8,0},{16,24},{24,16},{1,9},{9,1},{17,25},{25,17},{2,10},{10... | collective-permute-start | bytes 614408 | tf_op jit(solution)/shard_map/ppermute | solution.py:375
  299.7 33.7 %collective-permute-start.82 = (bf16[80,1280]{1,0:T(8,128)(2,1)S(1)}, bf16[80,1280]{1,0:T(8,128)(2,1)S(1)}, u32[]{:S(2)}, u32[]{:S(2)}) collective-permute-start(bf16[80,1280]{1,0:T(8,128)(2,1)S(1)} %dynamic-slice_bitcast_fusion.2), channel_id=1, source_target_pairs={{0,16},{8,24},{16,0},{24,8},{1,17},{9,25},{17,1},{25,9},{2,18},{10... | collective-permute-start | bytes 614408 | tf_op jit(solution)/shard_map/ppermute | solution.py:375
  326.8 40.5 %collective-permute-start.56 = (bf16[2,128,640]{2,1,0:T(8,128)(2,1)S(1)}, bf16[2,128,640]{2,1,0:T(8,128)(2,1)S(1)}, u32[]{:S(2)}, u32[]{:S(2)}) collective-permute-start(bf16[2,128,640]{2,1,0:T(8,128)(2,1)S(1)} %broadcast_select_fusion.11), channel_id=1, source_target_pairs={{0,1},{1,0},{2,3},{3,2},{4,5},{5,4},{6,7},{7,6},{8,9},{9,8},{10,11... | collective-permute-start | bytes 983048 | tf_op jit(solution)/shard_map/ppermute | solution.py:375
  333.4 26.2 %collective-permute-start.83 = (bf16[80,1280]{1,0:T(8,128)(2,1)S(1)}, bf16[80,1280]{1,0:T(8,128)(2,1)S(1)}, u32[]{:S(2)}, u32[]{:S(2)}) collective-permute-start(bf16[80,1280]{1,0:T(8,128)(2,1)S(1)} %fusion.1), channel_id=1, source_target_pairs={{0,16},{8,24},{16,0},{24,8},{1,17},{9,25},{17,1},{25,9},{2,18},{10... | collective-permute-start | bytes 614408 | tf_op jit(solution)/shard_map/ppermute | solution.py:375
  350.4 19.2 %collective-permute-start.74 = (bf16[2,40,1280]{2,1,0:T(8,128)(2,1)}, bf16[2,40,1280]{2,1,0:T(8,128)(2,1)}, u32[]{:S(2)}, u32[]{:S(2)}) collective-permute-start(bf16[2,40,1280]{2,1,0:T(8,128)(2,1)} %pad_maximum_fusion.18), channel_id=1, source_target_pairs={{0,8},{8,0},{16,24},{24,16},{1,9},{9,1},{17,25},{25,17},{2,10},{10... | collective-permute-start | bytes 614408 | tf_op jit(solution)/shard_map/ppermute | solution.py:375
  360.5 30.3 %collective-permute-start.84 = (bf16[2,80,1280]{2,1,0:T(8,128)(2,1)}, bf16[2,80,1280]{2,1,0:T(8,128)(2,1)}, u32[]{:S(2)}, u32[]{:S(2)}) collective-permute-start(bf16[2,80,1280]{2,1,0:T(8,128)(2,1)} %pad_maximum_fusion.10), channel_id=1, source_target_pairs={{0,8},{8,0},{16,24},{24,16},{1,9},{9,1},{17,25},{25,17},{2,10},{10... | collective-permute-start | bytes 1228808 | tf_op jit(solution)/shard_map/ppermute | solution.py:375
  362.6 17.0 %collective-permute-start.78 = (bf16[80,1280]{1,0:T(8,128)(2,1)}, bf16[80,1280]{1,0:T(8,128)(2,1)}, u32[]{:S(2)}, u32[]{:S(2)}) collective-permute-start(bf16[80,1280]{1,0:T(8,128)(2,1)} %get-tuple-element.279), channel_id=1, source_target_pairs={{0,6},{1,7},{2,4},{3,5},{4,2},{5,3},{6,0},{7,1},{8,14},{9,15},{10,... | collective-permute-start | bytes 614408 | tf_op jit(solution)/shard_map/ppermute | solution.py:375
  362.6 19.0 %collective-permute-start.79 = (bf16[80,1280]{1,0:T(8,128)(2,1)}, bf16[80,1280]{1,0:T(8,128)(2,1)}, u32[]{:S(2)}, u32[]{:S(2)}) collective-permute-start(bf16[80,1280]{1,0:T(8,128)(2,1)} %get-tuple-element.278), channel_id=1, source_target_pairs={{0,4},{1,5},{2,6},{3,7},{4,0},{5,1},{6,2},{7,3},{8,12},{9,13},{10,... | collective-permute-start | bytes 614408 | tf_op jit(solution)/shard_map/ppermute | solution.py:375
  (124 other events, 817.2 us)
Sparse Core Ops, SparseCore 0:
  56.4 34.2 all-gather.1
  178.8 77.6 all-reduce.11
  290.6 68.6 all-reduce.9
  366.5 36.0 all-reduce.13

commit v2 on v1

--- a/solution.py
+++ b/solution.py
@@ -288,7 +288,8 @@
     gproj_ref,
     *refs,
 ):
-    out_refs, full_ref = refs[:-1], refs[-1]
+    kept_refs = refs[: (len(refs) - 1) // 2] if len(refs) > count + 1 else ()
+    out_refs, full_ref = refs[len(kept_refs) : -1], refs[-1]
     half = own_ref.shape[0]
     width = ctx_ref.shape[1]
     core, chip = ids_ref[1], ids_ref[2]
@@ -305,9 +306,11 @@
     normed = (scaled * gain_ref[...] + shift_ref[...]).astype(BF)
     full_ref[:, : 3 * width] = dot_tn(normed, gproj_ref[...]).astype(BF)
     if len(out_refs) == count:
-        rows = out_refs[0].shape[0]
+        rows = full_ref.shape[0] // count
         for j, ref in enumerate(out_refs):
-            ref[...] = full_ref[pl.ds(pl.multiple_of((chip ^ j) * rows, 16), rows), :]
+            if kept_refs:
+                ref[rows:, :] = kept_refs[j][...]
+            ref[:rows, :] = full_ref[pl.ds(pl.multiple_of((chip ^ j) * rows, 16), rows), :]
     else:
         out_refs[0][...] = full_ref[...]
 
@@ -408,20 +411,25 @@
     return functools.reduce(lambda a, b: a + b, [p.astype(F32) for p in parts])
 
 
-def section_sum(x, z):
+def section_half(x, z):
+    x = x.reshape((2, 2, x.shape[0] // 4) + x.shape[1:])
+    return total([pick(x, z % 2), swap(pick(x, 1 - z % 2), "section", 1)]).astype(BF)
+
+
+def section_sum(half, z):
     low, high = z % 2, z // 2
-    x = x.reshape((2, 2, x.shape[0] // 4) + x.shape[1:])
-    half = total([pick(x, low), swap(pick(x, 1 - low), "section", 1)]).astype(BF)
     quarter = total([pick(half, high), swap(pick(half, 1 - high), "section", 2)]).astype(BF)
     half = jnp.stack(in_order([quarter, swap(quarter, "section", 2)], high))
     whole = jnp.stack(in_order([half, swap(half, "section", 1)], low))
-    return whole.reshape((-1,) + x.shape[3:])
-
-
-def section_streams(own, z, core):
-    far = swap(own, "section", 2)
-    near = swap(jnp.stack([own, far]), "section", 1)
-    crops = in_order([own, near[0], far, near[1]], z)
+    return whole.reshape((-1,) + whole.shape[3:])
+
+
+def far_and_own(own):
+    return jnp.stack([own, swap(own, "section", 2)])
+
+
+def section_streams(pair, near, z, core):
+    crops = in_order([pair[0], near[0], pair[1], near[1]], z)
     mine = jnp.where(core == 0, jnp.stack(crops[:2]), jnp.stack(crops[2:]))
     theirs = jnp.where(core == 0, jnp.stack(crops[2:]), jnp.stack(crops[:2]))
     recv = to_sibling(theirs)
@@ -596,7 +604,7 @@
             sib = to_sibling(own)
             up1 = trade_up(1, own)
 
-    small_grads, upb_grads, ffn_grads, attn_grads = {}, {}, {}, {}
+    small_grads, upb_grads, ffn_grads = {}, {}, {}
     for l in reversed(range(layers)):
         own, sib, proj, ctx, other, mid, parts = saved[l]
         top = l + 1 == layers
@@ -630,9 +638,8 @@
             fw_sib = jnp.concatenate([blocks[1], fw_sib[cols:]], axis=0)
         got[1] = after(got[1], fw_own)
         if not top:
-            final_got = lax.optimization_barrier((*final_got, sums[0]))[:-1]
-            final = (total([final_mid, *final_got]) + vec(1, 7)).astype(BF)
-            final_stream = section_streams(final, z, core)
+            final_pair, got[1] = lax.optimization_barrier((final_pair, got[1]))
+            final_near = swap(final_pair, "section", 1)
         grad_mid, small_ffn = run(
             2.3,
             functools.partial(ffn_norm_back_kernel, count),
@@ -641,10 +648,13 @@
         )
         gm_sib = to_sibling(grad_mid)
         fw_recv = to_sibling(after(fw_sib, grad_mid))
+        fw_sum = total([fw_own, fw_recv]).astype(BF)
+        if top:
+            gm_sib, fw_sum = lax.optimization_barrier((gm_sib, fw_sum))
+            ffn_grads[1] = lax.psum(fw_sum, "section")
         if top:
             outs = lax.optimization_barrier((*outs, gm_sib))[:-1]
             final_got = [outs[0]] + [swap_chip(outs[j], j) for j in range(1, count)]
-            final_mid = mid
 
         gproj, gn_own, gn_sib, gproj_sum = run(
             8,
@@ -655,27 +665,33 @@
             smem=1,
         )
         gn_recv = to_sibling(gn_sib)
-        fw_sum = total([fw_own, fw_recv]).astype(BF)
-        gn_recv, fw_sum = lax.optimization_barrier((gn_recv, fw_sum))
         if top:
-            ffn_grads[1] = lax.psum(fw_sum, "section")
+            gn_recv, *final_got = lax.optimization_barrier((gn_recv, *final_got))
+            final_pair = far_and_own((total([mid, *final_got]) + vec(1, 7)).astype(BF))
         else:
+            gn_recv, fw_sum, final_near = lax.optimization_barrier((gn_recv, fw_sum, final_near))
+            final_stream = section_streams(final_pair, final_near, z, core)
             order = [list(reversed(range(lax.axis_size("section"))))]
             up_sum = lax.psum(fw_sum[:cols], "section", axis_index_groups=order)
         block_form = 2 * piece % 16 == 0
+        kept = [] if top else list(packed)
+        out_rows = 2 * piece if top else 4 * piece
         packed = run(
             3.8,
             functools.partial(attn_weights_kernel, count),
-            [like((2 * piece, 4 * cols), BF)] * count
+            [like((out_rows, 4 * cols), BF)] * count
             if block_form
             else [like((width, 4 * cols), BF)],
-            [ids, own, sib, vec(l, 0), vec(l, 1), ctx, other, grad_mid, gm_sib, gproj],
+            [ids, own, sib, vec(l, 0), vec(l, 1), ctx, other, grad_mid, gm_sib, gproj]
+            + (kept if block_form else []),
             scratch=[((width, 4 * cols), BF)],
             smem=1,
         )
         if not block_form:
             packed = packed[0].reshape(count, 2 * piece, 4 * cols)
             packed = [pick(packed, chip ^ j) for j in range(count)]
+            if kept:
+                packed = [jnp.concatenate([a, b], axis=0) for a, b in zip(packed, kept)]
         grad_stream, small_attn = run(
             2.2,
             attn_norm_back_kernel,
@@ -684,29 +700,23 @@
         )
         if top:
             g_parts = spread(grad_stream, count)
-            packed = list(lax.optimization_barrier((*packed, *g_parts)))
-            packed, g_parts = packed[:count], packed[count:]
         else:
-            residues_grad = section_streams(grad_stream, z, core).astype(F32)
-        sent = [packed[0]] + [swap_chip(packed[j], j) for j in range(1, count)]
-
-        def chip_sum(sent):
-            packed = total(sent).astype(BF).reshape(2, piece, 4 * cols)
+            sent = [packed[0]] + [swap_chip(packed[j], j) for j in range(1, count)]
+            sent = list(lax.optimization_barrier((*sent, grad_stream))[:-1])
+            pair = far_and_own(grad_stream)
+            near = swap(pair, "section", 1)
+            residues_grad = section_streams(pair, near, z, core).astype(F32)
+            down = section_half(fw_sum[cols:], z)
+            down, up_sum = lax.optimization_barrier((down, up_sum))
+            down_sum = section_sum(down, z)
+            packed = total(sent).astype(BF).reshape(2, 2, piece, 4 * cols)
+            packed = jnp.swapaxes(packed, 0, 1)
             mine, theirs = pick(packed, core), pick(packed, 1 - core)
-            both = jnp.stack(in_order([mine, to_sibling(theirs)], core))
-            return both.reshape(2 * piece, 4 * cols)
-
-        if top:
-            sent_top, sum_top = sent, chip_sum
-        else:
-            down_sum = section_sum(fw_sum[cols:], z)
-            sent_top = lax.optimization_barrier((*sent_top, grad_stream))[:-1]
-            sent = list(lax.optimization_barrier((*sent, grad_stream))[:-1])
-            attn_grads[1] = section_sum(sum_top(sent_top), z)
-            both, up_sum, ffn_grads[1] = lax.optimization_barrier(
-                (chip_sum(sent), up_sum, ffn_grads[1])
-            )
-            attn_grads[0] = lax.psum(both, "section")
+            both = jnp.stack(in_order([mine, to_sibling(theirs)], core), axis=1)
+            both = both.reshape(4 * piece, 4 * cols)
+            both = lax.psum(both, "section", axis_index_groups=[[i ^ 1 for i in range(lax.axis_size("section"))]])
+            both, down_sum = lax.optimization_barrier((both, down_sum))
+            attn_grads = {0: both[: 2 * piece], 1: both[2 * piece :]}
             start = after(ffn_grads[1], grad_stream)
             ffn_blocks = {
                 1: (start[:cols], start[cols:]),

time: 421 us -> 394 us (0.936)
  waiting for transfers between devices: 169 us -> 140 us
    ppermute x85 -> x77, waiting for transfers between devices: 158 us -> 123 us  [swap(): return lax.ppermute(x, axis, [(i, i ^ bit) for i in range(size)])]
    psum x1, waiting for transfers between devices: 0.01 us -> 15.1 us  [shards(): ffn_grads[1] = lax.psum(fw_sum, 'section')]
    psum x1, waiting for transfers between devices: 10.6 us -> 1.63 us  [shards(): lax.psum(both, 'section', axis_index_groups=[[i ^ 1 for i in range(lax.ax...]
    ppermute x85 -> x77, starting transfers between devices: 71.8 us -> 73.7 us  [swap(): return lax.ppermute(x, axis, [(i, i ^ bit) for i in range(size)])]
    unnamed x137 -> x130, local copies, waits for them, and re-layouts: 10.7 us -> 9.97 us
  transfers between devices with their start and end apart: 89 -> 81, of which waited for: 32 -> 29; matrix products, arithmetic and copies ran while one was open for 11% -> 10% of each run, Pallas kernels for 19% -> 21%
where the time goes in v2:
time: 394 us; the launch traced here: 389 us
  waiting for transfers between devices  140 us (36%)
  Pallas kernels  95.4 us (24%)
  starting transfers between devices  74.7 us (19%)
  local copies, waits for them, and re-layouts  31.8 us (8%)
  other arithmetic  30.4 us (8%)
  between operations  16.5 us (4%)
    ppermute x77, waiting for transfers between devices, swap(): return lax.ppermute(x, axis, [(i, i ^ bit) for i in range(size)])  123 us
    pallas_call x18, Pallas kernels, run(): pl.pallas_call(kernel, out_shape=[jax.ShapeDtypeStruct(o.shape, o.dtype)...  95.4 us
    ppermute x77, starting transfers between devices, swap(): return lax.ppermute(x, axis, [(i, i ^ bit) for i in range(size)])  73.7 us
    psum x1, waiting for transfers between devices, shards(): ffn_grads[1] = lax.psum(fw_sum, 'section')  15.1 us
    unnamed x130, local copies, waits for them, and re-layouts  9.97 us
  transfers between devices with their start and end apart: 81, of which 29 were waited for; matrix products, arithmetic and copies ran while one was open for 10% of the time, Pallas kernels for 21%

profile of v2, /device:TPU:0, one launch (start us, length us, event | category | flops | bytes accessed | tf_op | source)
XLA Modules:
  0.0 388.8 jit_solution(10488353849787939871)
XLA Ops:
  7.8 3.3 shard_map.280
  11.8 2.9 collective-permute-start.6
  21.5 2.9 collective-permute-start.2
  27.5 10.4 %collective-permute-done.7 = bf16[80,1920]{1,0:T(8,128)(2,1)S(1)} collective-permute-done((bf16[80,1920]{1,0:T(8,128)(2,1)}, bf16[80,1920]{1,0:T(8,128)(2,1)S(1)}, u32[]{:S(2)}, u32[]{:S(2)}) %collective-permute-start.7) | collective-permute-done | bytes 307232 | tf_op jit(solution)/shard_map/ppermute | solution.py:378
  38.2 6.4 %collective-permute-done.3 = bf16[2,80,976]{2,1,0:T(8,128)(2,1)S(1)} collective-permute-done((bf16[2,80,976]{2,1,0:T(8,128)(2,1)S(1)}, bf16[2,80,976]{2,1,0:T(8,128)(2,1)S(1)}, u32[]{:S(2)}, u32[]{:S(2)}) %collective-permute-start.3) | collective-permute-done | bytes 312352 | tf_op jit(solution)/shard_map/ppermute | solution.py:378
  50.4 5.9 %shard_map.281 = (bf16[256,960]{1,0:T(8,128)(2,1)}, bf16[256,320]{1,0:T(8,128)(2,1)}) custom-call(s32[3]{0:T(128)} %pad_add_fusion.1.ids_ref.refs_0_, bf16[128,640]{1,0:T(8,128)(2,1)} %get-tuple-element.140.own_ref, bf16[128,640]{1,0:T(8,128)(2,1)} %get-tuple-element.319.sib_ref, f32[1,640]{1,0:T(1,128)} %get-tuple-element.341.gain_ref, ...), custom_call_target="tpu_custom_call" | custom-call | flops 6600000000 | bytes 2241292 | tf_op jit(solution)/shard_map/pallas_call | solution.py:359
  64.8 3.1 shard_map.282
  72.7 2.7 collective-permute-done.15.refs_1_.refs_2_
  75.6 3.9 %collective-permute-done.17.refs_3_.refs_4_ = bf16[128,640]{1,0:T(8,128)(2,1)S(1)} collective-permute-done((bf16[128,640]{1,0:T(8,128)(2,1)}, bf16[128,640]{1,0:T(8,128)(2,1)S(1)}, u32[]{:S(2)}, u32[]{:S(2)}) %collective-permute-start.17) | collective-permute-done | bytes 163872 | tf_op jit(solution)/shard_map/ppermute | solution.py:378
  80.2 6.0 %shard_map.283 = (bf16[128,640]{1,0:T(8,128)(2,1)}, bf16[128,640]{1,0:T(8,128)(2,1)}, bf16[128,640]{1,0:T(8,128)(2,1)}, bf16[128,640]{1,0:T(8,128)(2,1)}) custom-call(bf16[128,640]{1,0:T(8,128)(2,1)} %get-tuple-element.150.refs_0_.refs_1_, bf16[128,640]{1,0:T(8,128)(2,1)} %copy-done.42, bf16[128,640]{1,0:T(8,128)(2,1)} %copy-done.43, ...), custom_call_target="tpu_custom_call" | custom-call | flops 6600000000 | bytes 5411840 | tf_op jit(solution)/shard_map/pallas_call | solution.py:359
  89.8 3.7 collective-permute-done.20
  93.5 3.4 collective-permute-done.22
  101.9 6.5 %shard_map.284 = (bf16[256,960]{1,0:T(8,128)(2,1)}, bf16[256,320]{1,0:T(8,128)(2,1)}) custom-call(s32[3]{0:T(128)} %pad_add_fusion.1.ids_ref.refs_0_, bf16[128,640]{1,0:T(8,128)(2,1)} %copy-done.23, bf16[128,640]{1,0:T(8,128)(2,1)} %copy-done.48, f32[1,640]{1,0:T(1,128)} %get-tuple-element.332.gain_ref, f32[1,640]{1,0:T(1,128)} %get-tuple-element.331.shift_ref, ...), custom_call_target="tpu_custom_call" | custom-call | flops 6600000000 | bytes 4432652 | tf_op jit(solution)/shard_map/pallas_call | solution.py:359
  113.2 3.4 shard_map.285
  123.9 3.7 collective-permute-done.29.refs_2_.refs_3_
  128.3 8.4 %shard_map.286 = (bf16[128,640]{1,0:T(8,128)(2,1)}, bf16[128,640]{1,0:T(8,128)(2,1)}, bf16[128,640]{1,0:T(8,128)(2,1)}, bf16[128,640]{1,0:T(8,128)(2,1)}, bf16[5...) custom-call(bf16[128,640]{1,0:T(8,128)(2,1)} %get-tuple-element.163.refs_0_.refs_1_, ...), custom_call_target="tpu_custom_call" | custom-call | flops 9130000384 | bytes 7874560 | tf_op jit(solution)/shard_map/pallas_call | solution.py:359
  140.2 7.6 %shard_map.287 = (bf16[640,1280]{1,0:T(8,128)(2,1)}, bf16[640,1280]{1,0:T(8,128)(2,1)}, bf16[640,1280]{1,0:T(8,128)(2,1)}, bf16[128,640]{1,0:T(8,128)(2,1)}, bf1...) custom-call(s32[3]{0:T(128)} %pad_add_fusion.1.ids_ref.refs_0_, ...), custom_call_target="tpu_custom_call" | custom-call | flops 5500000256 | bytes 11141132 | tf_op jit(solution)/shard_map/pallas_call | solution.py:359
  151.7 3.3 collective-permute-done.37
  160.1 9.0 %shard_map.289 = (bf16[256,960]{1,0:T(8,128)(2,1)}, f32[128,640]{1,0:T(8,128)}, bf16[128,640]{1,0:T(8,128)(2,1)}, f32[1,960]{1,0:T(1,128)}) custom-call(s32[3]{0:T(128)} %pad_add_fusion.1.ids_ref.refs_0_, bf16[640,2688]{1,0:T(8,128)(2,1)} %all-gather.2.cloned.1.call-done.w_ref.wout_ref, bf16[256,960]{1,0:T(8,128)(2,1)} %get-tuple-element.159.proj_ref, ...), custom_call_target="tpu_custom_call" | custom-call | flops 8800000000 | bytes 8687372 | tf_op jit(solution)/shard_map/pallas_call | solution.py:359
  169.6 3.7 shard_map.296
  183.6 3.6 collective-permute-done.43.refs_6_.refs_7_
  188.4 8.5 %shard_map.291 = (bf16[128,640]{1,0:T(8,128)(2,1)}, bf16[128,640]{1,0:T(8,128)(2,1)}, bf16[128,640]{1,0:T(8,128)(2,1)}, bf16[128,640]{1,0:T(8,128)(2,1)}, bf16[5...) custom-call(bf16[128,640]{1,0:T(8,128)(2,1)} %get-tuple-element.150.refs_0_.refs_1_, ...), custom_call_target="tpu_custom_call" | custom-call | flops 9130000384 | bytes 8693760 | tf_op jit(solution)/shard_map/pallas_call | solution.py:359
  200.4 7.4 %shard_map.292 = (bf16[640,1280]{1,0:T(8,128)(2,1)}, bf16[640,1280]{1,0:T(8,128)(2,1)}, bf16[640,1280]{1,0:T(8,128)(2,1)}) custom-call(s32[3]{0:T(128)} %pad_add_fusion.1.ids_ref.refs_0_, bf16[128,640]{1,0:T(8,128)(2,1)} %get-tuple-element.150.refs_0_.refs_1_, bf16[128,640]{1,0:T(8,128)(2,1)} %copy-done.42, bf16[128,640]{1,0:T(8,128)(2,1)} %copy-done.43, ...), custom_call_target="tpu_custom_call" | custom-call | flops 5500000256 | bytes 10485772 | tf_op jit(solution)/shard_map/pallas_call | solution.py:359
  214.6 8.3 %shard_map.294 = (bf16[256,960]{1,0:T(8,128)(2,1)}, f32[128,640]{1,0:T(8,128)}, bf16[128,640]{1,0:T(8,128)(2,1)}, f32[1,960]{1,0:T(1,128)}) custom-call(s32[3]{0:T(128)} %pad_add_fusion.1.ids_ref.refs_0_, bf16[640,976]{1,0:T(8,128)(2,1)} %bitcast.224, bf16[256,960]{1,0:T(8,128)(2,1)} %get-tuple-element.141.proj_ref, ...), custom_call_target="tpu_custom_call" | custom-call | flops 8800000000 | bytes 5512972 | tf_op jit(solution)/shard_map/pallas_call | solution.py:359
  222.9 4.9 %shard_map.297 = (bf16[320,1280]{1,0:T(8,128)(2,1)}, bf16[320,1280]{1,0:T(8,128)(2,1)}, bf16[320,1280]{1,0:T(8,128)(2,1)}, bf16[320,1280]{1,0:T(8,128)(2,1)}) custom-call(s32[3]{0:T(128)} %pad_add_fusion.1.ids_ref.refs_0_, bf16[128,640]{1,0:T(8,128)(2,1)} %get-tuple-element.140.own_ref, bf16[128,640]{1,0:T(8,128)(2,1)} %get-tuple-element.319.sib_ref, ...), custom_call_target="tpu_custom_call" | custom-call | flops 4180000000 | bytes 6394892 | tf_op jit(solution)/shard_map/pallas_call | solution.py:359
  234.2 4.2 %collective-permute-start.54 = (bf16[128,640]{1,0:T(8,128)(2,1)}, bf16[128,640]{1,0:T(8,128)(2,1)S(1)}, u32[]{:S(2)}, u32[]{:S(2)}) collective-permute-start(bf16[128,640]{1,0:T(8,128)(2,1)} %get-tuple-element.219), channel_id=1, source_target_pairs={{0,16},{8,24},{16,0},{24,8},{1,17},{9,25},{17,1},{25,9},{2,18},{10... | collective-permute-start | bytes 491528 | tf_op jit(solution)/shard_map/ppermute | solution.py:378
  240.3 15.1 %all-reduce.14.cloned.1.call-done = bf16[640,1280]{1,0:T(8,128)(2,1)} async-done(((bf16[640,1280]{1,0:T(8,128)(2,1)}), bf16[640,1280]{1,0:T(8,128)(2,1)}) %all-reduce.14.cloned.1.call-update) | async-done | bytes 1638416 | tf_op jit(solution)/shard_map/psum | solution.py:654
  258.7 8.5 %collective-permute-done.64 = bf16[320,1280]{1,0:T(8,128)(2,1)} collective-permute-done((bf16[320,1280]{1,0:T(8,128)(2,1)}, bf16[320,1280]{1,0:T(8,128)(2,1)}, u32[]{:S(2)}, u32[]{:S(2)}) %collective-permute-start.64) | collective-permute-done | bytes 819232 | tf_op jit(solution)/shard_map/ppermute | solution.py:378
  296.4 12.8 %collective-permute-done.55 = bf16[2,128,640]{2,1,0:T(8,128)(2,1)} collective-permute-done((bf16[2,128,640]{2,1,0:T(8,128)(2,1)}, bf16[2,128,640]{2,1,0:T(8,128)(2,1)}, u32[]{:S(2)}, u32[]{:S(2)}) %collective-permute-start.55) | collective-permute-done | bytes 327712 | tf_op jit(solution)/shard_map/ppermute | solution.py:378
  317.7 10.3 %collective-permute-done.68 = bf16[80,1280]{1,0:T(8,128)(2,1)S(1)} collective-permute-done((bf16[80,1280]{1,0:T(8,128)(2,1)S(1)}, bf16[80,1280]{1,0:T(8,128)(2,1)S(1)}, u32[]{:S(2)}, u32[]{:S(2)}) %collective-permute-start.68) | collective-permute-done | bytes 204832 | tf_op jit(solution)/shard_map/ppermute | solution.py:378
  329.4 15.3 %collective-permute-done.69 = bf16[80,1280]{1,0:T(8,128)(2,1)S(1)} collective-permute-done((bf16[80,1280]{1,0:T(8,128)(2,1)S(1)}, bf16[80,1280]{1,0:T(8,128)(2,1)S(1)}, u32[]{:S(2)}, u32[]{:S(2)}) %collective-permute-start.69) | collective-permute-done | bytes 204832 | tf_op jit(solution)/shard_map/ppermute | solution.py:378
  346.8 21.3 %collective-permute-done.70 = bf16[2,80,1280]{2,1,0:T(8,128)(2,1)S(1)} collective-permute-done((bf16[2,80,1280]{2,1,0:T(8,128)(2,1)S(1)}, bf16[2,80,1280]{2,1,0:T(8,128)(2,1)S(1)}, u32[]{:S(2)}, u32[]{:S(2)}) %collective-permute-start.70) | collective-permute-done | bytes 409632 | tf_op jit(solution)/shard_map/ppermute | solution.py:378
  (408 shorter events, 151.8 us)
Async XLA Ops:
  7.2 94.1 %all-gather.2.cloned.1.call-start = ((), (), s32[]{:S(2)}) async-start(), calls=%async_computation | async-start | bytes 3870720 | tf_op jit(solution)/shard_map/all_gather | solution.py:578
  11.7 13.4 %collective-permute-start.5 = (bf16[256,640]{1,0:T(8,128)(2,1)S(1)}, bf16[256,640]{1,0:T(8,128)(2,1)S(1)}, u32[]{:S(2)}, u32[]{:S(2)}) collective-permute-start(bf16[256,640]{1,0:T(8,128)(2,1)S(1)} %dynamic-slice_bitcast_fusion.2), channel_id=1, source_target_pairs={{0,1},{1,0},{2,3},{3,2},{4,5},{5,4},{6,7},{7,6},{8,9},{9,8},{10,11... | collective-permute-start | bytes 983048 | tf_op jit(solution)/shard_map/ppermute | solution.py:378
  11.8 12.6 %collective-permute-start.6 = (bf16[80,1920]{1,0:T(8,128)(2,1)}, bf16[80,1920]{1,0:T(8,128)(2,1)S(1)}, u32[]{:S(2)}, u32[]{:S(2)}) collective-permute-start(bf16[80,1920]{1,0:T(8,128)(2,1)} %get-tuple-element.137), channel_id=1, source_target_pairs={{0,2},{1,3},{2,0},{3,1},{4,6},{5,7},{6,4},{7,5},{8,10},{9,11},{10,... | collective-permute-start | bytes 921608 | tf_op jit(solution)/shard_map/ppermute | solution.py:378
  14.8 23.1 %collective-permute-start.7 = (bf16[80,1920]{1,0:T(8,128)(2,1)}, bf16[80,1920]{1,0:T(8,128)(2,1)S(1)}, u32[]{:S(2)}, u32[]{:S(2)}) collective-permute-start(bf16[80,1920]{1,0:T(8,128)(2,1)} %get-tuple-element.138), channel_id=1, source_target_pairs={{0,4},{1,5},{2,6},{3,7},{4,0},{5,1},{6,2},{7,3},{8,12},{9,13},{10,... | collective-permute-start | bytes 921608 | tf_op jit(solution)/shard_map/ppermute | solution.py:378
  18.3 19.6 %collective-permute-start.8 = (bf16[80,1920]{1,0:T(8,128)(2,1)}, bf16[80,1920]{1,0:T(8,128)(2,1)S(1)}, u32[]{:S(2)}, u32[]{:S(2)}) collective-permute-start(bf16[80,1920]{1,0:T(8,128)(2,1)} %get-tuple-element.139), channel_id=1, source_target_pairs={{0,6},{1,7},{2,4},{3,5},{4,2},{5,3},{6,0},{7,1},{8,14},{9,15},{10,... | collective-permute-start | bytes 921608 | tf_op jit(solution)/shard_map/ppermute | solution.py:378
  21.5 16.8 %collective-permute-start.2 = (bf16[2,80,976]{2,1,0:T(8,128)(2,1)S(1)}, bf16[2,80,976]{2,1,0:T(8,128)(2,1)S(1)}, u32[]{:S(2)}, u32[]{:S(2)}) collective-permute-start(bf16[2,80,976]{2,1,0:T(8,128)(2,1)S(1)} %pad_maximum_fusion.11), channel_id=1, source_target_pairs={{0,6},{1,7},{2,4},{3,5},{4,2},{5,3},{6,0},{7,1},{8,14},{9,15},{10,... | collective-permute-start | bytes 936968 | tf_op jit(solution)/shard_map/ppermute | solution.py:378
  24.5 20.1 %collective-permute-start.3 = (bf16[2,80,976]{2,1,0:T(8,128)(2,1)S(1)}, bf16[2,80,976]{2,1,0:T(8,128)(2,1)S(1)}, u32[]{:S(2)}, u32[]{:S(2)}) collective-permute-start(bf16[2,80,976]{2,1,0:T(8,128)(2,1)S(1)} %pad_maximum_fusion.11), channel_id=1, source_target_pairs={{0,4},{1,5},{2,6},{3,7},{4,0},{5,1},{6,2},{7,3},{8,12},{9,13},{10,... | collective-permute-start | bytes 936968 | tf_op jit(solution)/shard_map/ppermute | solution.py:378
  25.2 19.4 %collective-permute-start.4 = (bf16[2,80,976]{2,1,0:T(8,128)(2,1)S(1)}, bf16[2,80,976]{2,1,0:T(8,128)(2,1)S(1)}, u32[]{:S(2)}, u32[]{:S(2)}) collective-permute-start(bf16[2,80,976]{2,1,0:T(8,128)(2,1)S(1)} %pad_maximum_fusion.11), channel_id=1, source_target_pairs={{0,2},{1,3},{2,0},{3,1},{4,6},{5,7},{6,4},{7,5},{8,10},{9,11},{10,... | collective-permute-start | bytes 936968 | tf_op jit(solution)/shard_map/ppermute | solution.py:378
  44.9 11.4 %collective-permute-start.10 = (bf16[128,640]{1,0:T(8,128)(2,1)S(1)}, bf16[128,640]{1,0:T(8,128)(2,1)S(1)}, u32[]{:S(2)}, u32[]{:S(2)}) collective-permute-start(bf16[128,640]{1,0:T(8,128)(2,1)S(1)} %dynamic-slice_select_fusion.refs_4_.refs_5_), channel_id=1, source_target_pairs={{0,2},{1,3},{2,0},{3,1},{4,6},{5,7},{6,4},{7,5},{8,10},{9,11},{10,... | collective-permute-start | bytes 491528 | tf_op jit(solution)/shard_map/ppermute | solution.py:378
  56.4 199.1 %all-reduce.14.cloned.1.call-start = ((), (), s32[]{:S(2)}) async-start(), calls=%async_computation.3 | async-start | bytes 3276800 | tf_op jit(solution)/shard_map/psum | solution.py:654
  97.1 12.8 %collective-permute-start.32 = (bf16[640,640]{1,0:T(8,128)(2,1)S(1)}, bf16[640,640]{1,0:T(8,128)(2,1)S(1)}, u32[]{:S(2)}, u32[]{:S(2)}) collective-permute-start(bf16[640,640]{1,0:T(8,128)(2,1)S(1)} %get-tuple-element.172), channel_id=1, source_target_pairs={{0,1},{1,0},{2,3},{3,2},{4,5},{5,4},{6,7},{7,6},{8,9},{9,8},{10,11... | collective-permute-start | bytes 2457608 | tf_op jit(solution)/shard_map/ppermute | solution.py:378
  156.6 16.7 %collective-permute-start.39 = (bf16[128,640]{1,0:T(8,128)(2,1)}, bf16[128,640]{1,0:T(8,128)(2,1)S(1)}, u32[]{:S(2)}, u32[]{:S(2)}) collective-permute-start(bf16[128,640]{1,0:T(8,128)(2,1)} %get-tuple-element.193), channel_id=1, source_target_pairs={{0,2},{1,3},{2,0},{3,1},{4,6},{5,7},{6,4},{7,5},{8,10},{9,11},{10,... | collective-permute-start | bytes 491528 | tf_op jit(solution)/shard_map/ppermute | solution.py:378
  157.4 16.0 %collective-permute-start.40 = (bf16[128,640]{1,0:T(8,128)(2,1)}, bf16[128,640]{1,0:T(8,128)(2,1)S(1)}, u32[]{:S(2)}, u32[]{:S(2)}) collective-permute-start(bf16[128,640]{1,0:T(8,128)(2,1)} %get-tuple-element.194), channel_id=1, source_target_pairs={{0,4},{1,5},{2,6},{3,7},{4,0},{5,1},{6,2},{7,3},{8,12},{9,13},{10,... | collective-permute-start | bytes 491528 | tf_op jit(solution)/shard_map/ppermute | solution.py:378
  158.3 15.1 %collective-permute-start.41 = (bf16[128,640]{1,0:T(8,128)(2,1)}, bf16[128,640]{1,0:T(8,128)(2,1)S(1)}, u32[]{:S(2)}, u32[]{:S(2)}) collective-permute-start(bf16[128,640]{1,0:T(8,128)(2,1)} %get-tuple-element.195), channel_id=1, source_target_pairs={{0,6},{1,7},{2,4},{3,5},{4,2},{5,3},{6,0},{7,1},{8,14},{9,15},{10,... | collective-permute-start | bytes 491528 | tf_op jit(solution)/shard_map/ppermute | solution.py:378
  169.2 141.2 %all-reduce.12.cloned.1.call-start = ((), (), s32[]{:S(2)}) async-start(), calls=%async_computation.2 | async-start | bytes 1638400 | tf_op jit(solution)/shard_map/psum | solution.py:675
  180.0 27.8 %collective-permute-start.45 = (bf16[128,640]{1,0:T(8,128)(2,1)S(1)}, bf16[128,640]{1,0:T(8,128)(2,1)S(1)}, u32[]{:S(2)}, u32[]{:S(2)}) collective-permute-start(bf16[128,640]{1,0:T(8,128)(2,1)S(1)} %add_convert_fusion.3), channel_id=1, source_target_pairs={{0,16},{8,24},{16,0},{24,8},{1,17},{9,25},{17,1},{25,9},{2,18},{10... | collective-permute-start | bytes 491528 | tf_op jit(solution)/shard_map/ppermute | solution.py:378
  196.9 11.6 %collective-permute-start.46 = (bf16[128,640]{1,0:T(8,128)(2,1)}, bf16[128,640]{1,0:T(8,128)(2,1)S(1)}, u32[]{:S(2)}, u32[]{:S(2)}) collective-permute-start(bf16[128,640]{1,0:T(8,128)(2,1)} %get-tuple-element.203), channel_id=1, source_target_pairs={{0,2},{1,3},{2,0},{3,1},{4,6},{5,7},{6,4},{7,5},{8,10},{9,11},{10,... | collective-permute-start | bytes 491528 | tf_op jit(solution)/shard_map/ppermute | solution.py:378
  211.9 17.6 %collective-permute-start.51 = (bf16[640,1280]{1,0:T(8,128)(2,1)}, bf16[640,1280]{1,0:T(8,128)(2,1)S(1)}, u32[]{:S(2)}, u32[]{:S(2)}) collective-permute-start(bf16[640,1280]{1,0:T(8,128)(2,1)} %get-tuple-element.214), channel_id=1, source_target_pairs={{0,1},{1,0},{2,3},{3,2},{4,5},{5,4},{6,7},{7,6},{8,9},{9,8},{10,11... | collective-permute-start | bytes 4915208 | tf_op jit(solution)/shard_map/ppermute | solution.py:378
  212.4 19.6 %collective-permute-start.52 = (bf16[2,128,640]{2,1,0:T(8,128)(2,1)}, bf16[2,128,640]{2,1,0:T(8,128)(2,1)}, u32[]{:S(2)}, u32[]{:S(2)}) collective-permute-start(bf16[2,128,640]{2,1,0:T(8,128)(2,1)} %pad_maximum_fusion.12), channel_id=1, source_target_pairs={{0,8},{8,0},{16,24},{24,16},{1,9},{9,1},{17,25},{25,17},{2,10},{10... | collective-permute-start | bytes 983048 | tf_op jit(solution)/shard_map/ppermute | solution.py:378
  227.7 31.0 %collective-permute-start.63 = (bf16[320,1280]{1,0:T(8,128)(2,1)}, bf16[320,1280]{1,0:T(8,128)(2,1)}, u32[]{:S(2)}, u32[]{:S(2)}) collective-permute-start(bf16[320,1280]{1,0:T(8,128)(2,1)} %get-tuple-element.235), channel_id=1, source_target_pairs={{0,2},{1,3},{2,0},{3,1},{4,6},{5,7},{6,4},{7,5},{8,10},{9,11},{10,... | collective-permute-start | bytes 2457608 | tf_op jit(solution)/shard_map/ppermute | solution.py:378
  229.1 38.2 %collective-permute-start.64 = (bf16[320,1280]{1,0:T(8,128)(2,1)}, bf16[320,1280]{1,0:T(8,128)(2,1)}, u32[]{:S(2)}, u32[]{:S(2)}) collective-permute-start(bf16[320,1280]{1,0:T(8,128)(2,1)} %get-tuple-element.236), channel_id=1, source_target_pairs={{0,4},{1,5},{2,6},{3,7},{4,0},{5,1},{6,2},{7,3},{8,12},{9,13},{10,... | collective-permute-start | bytes 2457608 | tf_op jit(solution)/shard_map/ppermute | solution.py:378
  229.4 37.9 %collective-permute-start.65 = (bf16[320,1280]{1,0:T(8,128)(2,1)}, bf16[320,1280]{1,0:T(8,128)(2,1)}, u32[]{:S(2)}, u32[]{:S(2)}) collective-permute-start(bf16[320,1280]{1,0:T(8,128)(2,1)} %get-tuple-element.237), channel_id=1, source_target_pairs={{0,6},{1,7},{2,4},{3,5},{4,2},{5,3},{6,0},{7,1},{8,14},{9,15},{10,... | collective-permute-start | bytes 2457608 | tf_op jit(solution)/shard_map/ppermute | solution.py:378
  234.2 52.4 %collective-permute-start.54 = (bf16[128,640]{1,0:T(8,128)(2,1)}, bf16[128,640]{1,0:T(8,128)(2,1)S(1)}, u32[]{:S(2)}, u32[]{:S(2)}) collective-permute-start(bf16[128,640]{1,0:T(8,128)(2,1)} %get-tuple-element.219), channel_id=1, source_target_pairs={{0,16},{8,24},{16,0},{24,8},{1,17},{9,25},{17,1},{25,9},{2,18},{10... | collective-permute-start | bytes 491528 | tf_op jit(solution)/shard_map/ppermute | solution.py:378
  255.4 39.8 %collective-permute-start.67 = (bf16[2,80,1280]{2,1,0:T(8,128)(2,1)}, bf16[2,80,1280]{2,1,0:T(8,128)(2,1)}, u32[]{:S(2)}, u32[]{:S(2)}) collective-permute-start(bf16[2,80,1280]{2,1,0:T(8,128)(2,1)} %dynamic-slice_bitcast_fusion), channel_id=1, source_target_pairs={{0,8},{8,0},{16,24},{24,16},{1,9},{9,1},{17,25},{25,17},{2,10},{10... | collective-permute-start | bytes 1228808 | tf_op jit(solution)/shard_map/ppermute | solution.py:378
  255.5 114.4 %all-reduce.10.cloned.1.call-start = ((), (), s32[]{:S(2)}) async-start(), calls=%async_computation.1 | async-start | bytes 1638400 | tf_op jit(solution)/shard_map/psum | solution.py:717
  290.0 19.1 %collective-permute-start.55 = (bf16[2,128,640]{2,1,0:T(8,128)(2,1)}, bf16[2,128,640]{2,1,0:T(8,128)(2,1)}, u32[]{:S(2)}, u32[]{:S(2)}) collective-permute-start(bf16[2,128,640]{2,1,0:T(8,128)(2,1)} %pad_maximum_fusion.15), channel_id=1, source_target_pairs={{0,8},{8,0},{16,24},{24,16},{1,9},{9,1},{17,25},{25,17},{2,10},{10... | collective-permute-start | bytes 983048 | tf_op jit(solution)/shard_map/ppermute | solution.py:378
  310.5 17.5 %collective-permute-start.68 = (bf16[80,1280]{1,0:T(8,128)(2,1)S(1)}, bf16[80,1280]{1,0:T(8,128)(2,1)S(1)}, u32[]{:S(2)}, u32[]{:S(2)}) collective-permute-start(bf16[80,1280]{1,0:T(8,128)(2,1)S(1)} %dynamic-slice_bitcast_fusion.3), channel_id=1, source_target_pairs={{0,16},{8,24},{16,0},{24,8},{1,17},{9,25},{17,1},{25,9},{2,18},{10... | collective-permute-start | bytes 614408 | tf_op jit(solution)/shard_map/ppermute | solution.py:378
  312.8 15.3 %collective-permute-start.71 = (bf16[80,1280]{1,0:T(8,128)(2,1)S(1)}, bf16[80,1280]{1,0:T(8,128)(2,1)S(1)}, u32[]{:S(2)}, u32[]{:S(2)}) collective-permute-start(bf16[80,1280]{1,0:T(8,128)(2,1)S(1)} %get-tuple-element.296), channel_id=1, source_target_pairs={{0,6},{1,7},{2,4},{3,5},{4,2},{5,3},{6,0},{7,1},{8,14},{9,15},{10,... | collective-permute-start | bytes 614408 | tf_op jit(solution)/shard_map/ppermute | solution.py:378
  315.3 12.9 %collective-permute-start.72 = (bf16[80,1280]{1,0:T(8,128)(2,1)S(1)}, bf16[80,1280]{1,0:T(8,128)(2,1)S(1)}, u32[]{:S(2)}, u32[]{:S(2)}) collective-permute-start(bf16[80,1280]{1,0:T(8,128)(2,1)S(1)} %get-tuple-element.295), channel_id=1, source_target_pairs={{0,4},{1,5},{2,6},{3,7},{4,0},{5,1},{6,2},{7,3},{8,12},{9,13},{10,... | collective-permute-start | bytes 614408 | tf_op jit(solution)/shard_map/ppermute | solution.py:378
  315.8 12.3 %collective-permute-start.73 = (bf16[80,1280]{1,0:T(8,128)(2,1)S(1)}, bf16[80,1280]{1,0:T(8,128)(2,1)S(1)}, u32[]{:S(2)}, u32[]{:S(2)}) collective-permute-start(bf16[80,1280]{1,0:T(8,128)(2,1)S(1)} %get-tuple-element.294), channel_id=1, source_target_pairs={{0,2},{1,3},{2,0},{3,1},{4,6},{5,7},{6,4},{7,5},{8,10},{9,11},{10,... | collective-permute-start | bytes 614408 | tf_op jit(solution)/shard_map/ppermute | solution.py:378
  328.1 16.6 %collective-permute-start.69 = (bf16[80,1280]{1,0:T(8,128)(2,1)S(1)}, bf16[80,1280]{1,0:T(8,128)(2,1)S(1)}, u32[]{:S(2)}, u32[]{:S(2)}) collective-permute-start(bf16[80,1280]{1,0:T(8,128)(2,1)S(1)} %fusion.1), channel_id=1, source_target_pairs={{0,16},{8,24},{16,0},{24,8},{1,17},{9,25},{17,1},{25,9},{2,18},{10... | collective-permute-start | bytes 614408 | tf_op jit(solution)/shard_map/ppermute | solution.py:378
  344.8 23.3 %collective-permute-start.70 = (bf16[2,80,1280]{2,1,0:T(8,128)(2,1)S(1)}, bf16[2,80,1280]{2,1,0:T(8,128)(2,1)S(1)}, u32[]{:S(2)}, u32[]{:S(2)}) collective-permute-start(bf16[2,80,1280]{2,1,0:T(8,128)(2,1)S(1)} %pad_maximum_fusion.10), channel_id=1, source_target_pairs={{0,8},{8,0},{16,24},{24,16},{1,9},{9,1},{17,25},{25,17},{2,10},{10... | collective-permute-start | bytes 1228808 | tf_op jit(solution)/shard_map/ppermute | solution.py:378
  (113 other events, 678.0 us)
Sparse Core Ops, SparseCore 0:
  56.5 34.1 all-gather.1
  169.3 86.1 all-reduce.13
  257.9 49.1 all-reduce.11
  310.1 59.7 all-reduce.9

commit v3 on v2

--- a/solution.py
+++ b/solution.py
@@ -14,7 +14,8 @@
 NEGATIVE = -1e30
 BF = jnp.bfloat16
 F32 = jnp.float32
-VMEM_LIMIT = 56 * 1024 * 1024
+VMEM_LIMIT = 24 * 1024 * 1024
+VMEM_MOST = 56 * 1024 * 1024
 
 
 def dot_nn(a, b):
@@ -352,7 +353,21 @@
     rest_ref[:, 2 * step :] = out_ref[1]
 
 
-def run(micros, kernel, outs, operands, scratch=(), smem=0):
+def place_kernel(both_ref, qkv_ref, out_ref):
+    layers, piece, triple = qkv_ref.shape
+    width = triple // 3
+    cols = width // 2
+    for l in range(layers):
+        for c in range(2):
+            at = (2 * l + c) * piece
+            part = both_ref[at : at + piece, :].astype(F32)
+            for s in range(3):
+                to = s * width + c * cols
+                qkv_ref[l, :, to : to + cols] = part[:, s * cols : (s + 1) * cols]
+            out_ref[l, :, c * cols : (c + 1) * cols] = part[:, 3 * cols :]
+
+
+def run(micros, kernel, outs, operands, scratch=(), smem=0, limit=VMEM_LIMIT):
     vmem = pl.BlockSpec(memory_space=pltpu.VMEM)
     specs = [pl.BlockSpec(memory_space=pltpu.SMEM)] * smem + [vmem] * (len(operands) - smem)
     moved = sum(o.size * o.dtype.itemsize for o in list(operands) + list(outs))
@@ -365,7 +380,7 @@
         cost_estimate=pl.CostEstimate(
             flops=int(micros * 1.1e9), bytes_accessed=moved, transcendentals=0
         ),
-        compiler_params=pltpu.CompilerParams(vmem_limit_bytes=VMEM_LIMIT),
+        compiler_params=pltpu.CompilerParams(vmem_limit_bytes=limit),
     )(*operands)
 
 
@@ -499,6 +514,7 @@
         + [like((piece, width + ff_chip), BF)] * (count if aligned else 0),
         [places, qkv_weight, out_weight, up_weight, *smalls],
         smem=1,
+        limit=VMEM_MOST,
     )
     if not aligned:
         feed0 = [
@@ -575,7 +591,7 @@
             ctx, *g_parts = lax.optimization_barrier((ctx, *g_sent))
             out_full[0] = up_full[0] = join(feed0)
             down_full[0] = chip_rows(after(down_weight[0], own))
-            rest1 = lax.all_gather(after(rest1, ctx), "dp", axis=0, tiled=True)
+            rest1 = lax.all_gather(after(rest1, own), "dp", axis=0, tiled=True)
             qkv_full[1] = out_full[1] = rest1
         else:
             ctx, *up1 = lax.optimization_barrier((ctx, *up1))
@@ -669,7 +685,9 @@
             gn_recv, *final_got = lax.optimization_barrier((gn_recv, *final_got))
             final_pair = far_and_own((total([mid, *final_got]) + vec(1, 7)).astype(BF))
         else:
-            gn_recv, fw_sum, final_near = lax.optimization_barrier((gn_recv, fw_sum, final_near))
+            gn_recv, fw_sum, final_near, ffn_grads[1] = lax.optimization_barrier(
+                (gn_recv, fw_sum, final_near, ffn_grads[1])
+            )
             final_stream = section_streams(final_pair, final_near, z, core)
             order = [list(reversed(range(lax.axis_size("section"))))]
             up_sum = lax.psum(fw_sum[:cols], "section", axis_index_groups=order)
@@ -716,7 +734,7 @@
             both = both.reshape(4 * piece, 4 * cols)
             both = lax.psum(both, "section", axis_index_groups=[[i ^ 1 for i in range(lax.axis_size("section"))]])
             both, down_sum = lax.optimization_barrier((both, down_sum))
-            attn_grads = {0: both[: 2 * piece], 1: both[2 * piece :]}
+            attn_both = both
             start = after(ffn_grads[1], grad_stream)
             ffn_blocks = {
                 1: (start[:cols], start[cols:]),
@@ -745,9 +763,6 @@
     up_bias_grad = packed[split:].reshape(layers, ff_chip // 2)
 
     def weights(l):
-        both = attn_grads[l].reshape(2, piece, 4, cols)
-        qkv = jnp.transpose(both[:, :, :3], (1, 2, 0, 3)).reshape(piece, triple)
-        out = jnp.transpose(both[:, :, 3], (1, 0, 2)).reshape(piece, width)
         blocks, down = ffn_blocks[l]
         blocks = [blocks[j * piece : (j + 1) * piece] for j in range(count)]
         up = in_order([blocks[0]] + [swap_chip(blocks[j], j) for j in range(1, count)], chip)
@@ -758,25 +773,36 @@
             rows = ff_chip // 2
             down = [down[b : b + rows] for b in range(0, cols, rows)]
             down = jnp.concatenate(down, axis=1)
-        return qkv, out, jnp.concatenate(up, axis=1), down
-
+        return jnp.concatenate(up, axis=1), down
+
+    if piece % 16 == 0:
+        qkv_grad, out_grad = run(
+            1.5,
+            place_kernel,
+            [like((layers, piece, triple), F32), like((layers, piece, width), F32)],
+            [attn_both],
+        )
+    else:
+        rows = attn_both.reshape(layers, 2, piece, 4, cols).astype(F32)
+        qkv_grad = jnp.transpose(rows[:, :, :, :3], (0, 2, 3, 1, 4)).reshape(layers, piece, triple)
+        out_grad = jnp.transpose(rows[:, :, :, 3], (0, 2, 1, 3)).reshape(layers, piece, width)
     per_layer = [weights(l) for l in range(layers)]
-    stacked = [jnp.stack([p[i] for p in per_layer]).astype(F32) for i in range(4)]
+    stacked = [jnp.stack([p[i] for p in per_layer]).astype(F32) for i in range(2)]
     return (
         final_stream,
         residues_grad,
         grads[:, 0],
         grads[:, 1],
-        stacked[0],
+        qkv_grad,
         grads[:, 2],
         grads[:, 3],
-        stacked[1],
+        out_grad,
         grads[:, 4],
         grads[:, 5],
         grads[:, 6],
-        stacked[2],
+        stacked[0],
         up_bias_grad,
-        stacked[3],
+        stacked[1],
         grads[:, 7],
     )
 

time: 394 us -> 384 us (0.975)
  Pallas kernels: 95.4 us -> 57 us
  waiting for transfers between devices: 140 us -> 153 us
  other arithmetic: 30.4 us -> 41.2 us
  local copies, waits for them, and re-layouts: 31.8 us -> 40 us
    pallas_call x18 -> x19, Pallas kernels: 95.4 us -> 57 us  [run(): pl.pallas_call(kernel, out_shape=[jax.ShapeDtypeStruct(o.shape, o.dtype)...]
    unnamed x130 -> x178, local copies, waits for them, and re-layouts: 9.97 us -> 22.9 us
    psum x1, waiting for transfers between devices: 1.63 us -> 10.5 us  [shards(): lax.psum(both, 'section', axis_index_groups=[[i ^ 1 for i in range(lax.ax...]
    convert_element_type x2, other arithmetic: 1.95 us -> 6.54 us  [shards(): fw_sum = total([fw_own, fw_recv]).astype(BF)]
  transfers between devices with their start and end apart: 81 -> 81, of which waited for: 29 -> 31; matrix products, arithmetic and copies ran while one was open for 10% -> 15% of each run, Pallas kernels for 21% -> 13%
where the time goes in v3:
time: 384 us; the launch traced here: 380 us
  waiting for transfers between devices  153 us (40%)
  starting transfers between devices  72 us (19%)
  Pallas kernels  57 us (15%)
  other arithmetic  41.2 us (11%)
  local copies, waits for them, and re-layouts  40 us (10%)
  between operations  16.5 us (4%)
    ppermute x77, waiting for transfers between devices, swap(): return lax.ppermute(x, axis, [(i, i ^ bit) for i in range(size)])  124 us
    ppermute x77, starting transfers between devices, swap(): return lax.ppermute(x, axis, [(i, i ^ bit) for i in range(size)])  71.6 us
    pallas_call x19, Pallas kernels, run(): pl.pallas_call(kernel, out_shape=[jax.ShapeDtypeStruct(o.shape, o.dtype)...  57 us
    unnamed x178, local copies, waits for them, and re-layouts  22.9 us
    psum x1, waiting for transfers between devices, shards(): ffn_grads[1] = lax.psum(fw_sum, 'section')  17.6 us
    psum x1, waiting for transfers between devices, shards(): lax.psum(both, 'section', axis_index_groups=[[i ^ 1 for i in range(lax.ax...  10.5 us
  transfers between devices with their start and end apart: 81, of which 31 were waited for; matrix products, arithmetic and copies ran while one was open for 15% of the time, Pallas kernels for 13%

profile of v3, /device:TPU:0, one launch (start us, length us, event | category | flops | bytes accessed | tf_op | source)
XLA Modules:
  0.0 379.9 jit_solution(10975143335881469668)
XLA Ops:
  7.8 3.4 shard_map.280
  12.5 2.9 collective-permute-start.6
  26.8 11.2 %collective-permute-done.7 = bf16[80,1920]{1,0:T(8,128)(2,1)} collective-permute-done((bf16[80,1920]{1,0:T(8,128)(2,1)}, bf16[80,1920]{1,0:T(8,128)(2,1)}, u32[]{:S(2)}, u32[]{:S(2)}) %collective-permute-start.7) | collective-permute-done | bytes 307232 | tf_op jit(solution)/shard_map/ppermute | solution.py:393
  41.4 4.1 %collective-permute-done.3 = bf16[2,80,976]{2,1,0:T(8,128)(2,1)} collective-permute-done((bf16[2,80,976]{2,1,0:T(8,128)(2,1)}, bf16[2,80,976]{2,1,0:T(8,128)(2,1)}, u32[]{:S(2)}, u32[]{:S(2)}) %collective-permute-start.3) | collective-permute-done | bytes 312352 | tf_op jit(solution)/shard_map/ppermute | solution.py:393
  51.1 4.0 %shard_map.281 = (bf16[256,960]{1,0:T(8,128)(2,1)S(1)}, bf16[256,320]{1,0:T(8,128)(2,1)S(1)}) custom-call(s32[3]{0:T(128)S(1)} %pad_add_fusion.1.ids_ref.refs_0_, bf16[128,640]{1,0:T(8,128)(2,1)S(1)} %get-tuple-element.143.own_ref, bf16[128,640]{1,0:T(8,128)(2,1)S(1)} %get-tuple-element.323.sib_ref, f32[1,640]{1,0:T(1,128)S(1)} %get-tuple-element.345.gain_ref, ...), custom_call_target="tpu_custom_call" | custom-call | flops 6600000000 | bytes 2241292 | tf_op jit(solution)/shard_map/pallas_call | solution.py:374
  55.1 4.4 %collective-permute-done.11.refs_6_.refs_7_ = bf16[128,640]{1,0:T(8,128)(2,1)S(1)} collective-permute-done((bf16[128,640]{1,0:T(8,128)(2,1)S(1)}, bf16[128,640]{1,0:T(8,128)(2,1)S(1)}, u32[]{:S(2)}, u32[]{:S(2)}) %collective-permute-start.11) | collective-permute-done | bytes 163872 | tf_op jit(solution)/shard_map/ppermute | solution.py:393
  69.9 6.6 %collective-permute-done.15.refs_1_.refs_2_ = bf16[128,640]{1,0:T(8,128)(2,1)S(1)} collective-permute-done((bf16[128,640]{1,0:T(8,128)(2,1)S(1)}, bf16[128,640]{1,0:T(8,128)(2,1)S(1)}, u32[]{:S(2)}, u32[]{:S(2)}) %collective-permute-start.15) | collective-permute-done | bytes 163872 | tf_op jit(solution)/shard_map/ppermute | solution.py:393
  78.3 5.9 %collective-permute-done.17.refs_3_.refs_4_ = bf16[128,640]{1,0:T(8,128)(2,1)S(1)} collective-permute-done((bf16[128,640]{1,0:T(8,128)(2,1)S(1)}, bf16[128,640]{1,0:T(8,128)(2,1)S(1)}, u32[]{:S(2)}, u32[]{:S(2)}) %collective-permute-start.17) | collective-permute-done | bytes 163872 | tf_op jit(solution)/shard_map/ppermute | solution.py:393
  84.2 3.3 shard_map.283
  94.1 4.2 %collective-permute-done.21 = bf16[128,640]{1,0:T(8,128)(2,1)} collective-permute-done((bf16[128,640]{1,0:T(8,128)(2,1)}, bf16[128,640]{1,0:T(8,128)(2,1)}, u32[]{:S(2)}, u32[]{:S(2)}) %collective-permute-start.21) | collective-permute-done | bytes 163872 | tf_op jit(solution)/shard_map/ppermute | solution.py:393
  107.8 3.9 %shard_map.284 = (bf16[256,960]{1,0:T(8,128)(2,1)S(1)}, bf16[256,320]{1,0:T(8,128)(2,1)S(1)}) custom-call(s32[3]{0:T(128)S(1)} %pad_add_fusion.1.ids_ref.refs_0_, bf16[128,640]{1,0:T(8,128)(2,1)S(1)} %add_convert_fusion.4.own_ref, bf16[128,640]{1,0:T(8,128)(2,1)S(1)} %collective-permute-done.23.sib_ref, f32[1,640]{1,0:T(1,128)S(1)} %get-tuple-element.336.gain_ref, ...), custom_call_target="tpu_custom_call" | custom-call | flops 6600000000 | bytes 4432652 | tf_op jit(solution)/shard_map/pallas_call | solution.py:374
  124.1 3.1 collective-permute-done.28.refs_1_.refs_2_
  127.2 4.3 %collective-permute-done.29.refs_2_.refs_3_ = bf16[128,640]{1,0:T(8,128)(2,1)S(1)} collective-permute-done((bf16[128,640]{1,0:T(8,128)(2,1)S(1)}, bf16[128,640]{1,0:T(8,128)(2,1)S(1)}, u32[]{:S(2)}, u32[]{:S(2)}) %collective-permute-start.29) | collective-permute-done | bytes 163872 | tf_op jit(solution)/shard_map/ppermute | solution.py:393
  131.6 4.3 %shard_map.286 = (bf16[128,640]{1,0:T(8,128)(2,1)S(1)}, bf16[128,640]{1,0:T(8,128)(2,1)S(1)}, bf16[128,640]{1,0:T(8,128)(2,1)S(1)}, bf16[128,640]{1,0:T(8,128)(2...) custom-call(bf16[128,640]{1,0:T(8,128)(2,1)S(1)} %get-tuple-element.166.refs_0_.refs_1_, ...), custom_call_target="tpu_custom_call" | custom-call | flops 9130000384 | bytes 7874560 | tf_op jit(solution)/shard_map/pallas_call | solution.py:374
  139.4 5.4 %shard_map.287 = (bf16[640,1280]{1,0:T(8,128)(2,1)S(1)}, bf16[640,1280]{1,0:T(8,128)(2,1)}, bf16[640,1280]{1,0:T(8,128)(2,1)}, bf16[128,640]{1,0:T(8,128)(2,1)S(...) custom-call(s32[3]{0:T(128)S(1)} %pad_add_fusion.1.ids_ref.refs_0_, ...), custom_call_target="tpu_custom_call" | custom-call | flops 5500000256 | bytes 11141132 | tf_op jit(solution)/shard_map/pallas_call | solution.py:374
  147.3 3.2 collective-permute-done.37
  150.5 3.5 add_convert_fusion.1
  160.6 6.7 %shard_map.289 = (bf16[256,960]{1,0:T(8,128)(2,1)S(1)}, f32[128,640]{1,0:T(8,128)S(1)}, bf16[128,640]{1,0:T(8,128)(2,1)}, f32[1,960]{1,0:T(1,128)S(1)}) custom-call(s32[3]{0:T(128)S(1)} %pad_add_fusion.1.ids_ref.refs_0_, bf16[640,2688]{1,0:T(8,128)(2,1)S(1)} %copy-done.10, bf16[256,960]{1,0:T(8,128)(2,1)S(1)} %copy-done.59, bf16[128,640]{1,0:T(8,128)(2,1)S(1)} %copy-done.39, ...), custom_call_target="tpu_custom_call" | custom-call | flops 8800000000 | bytes 8687372 | tf_op jit(solution)/shard_map/pallas_call | solution.py:374
  190.4 4.3 %shard_map.291 = (bf16[128,640]{1,0:T(8,128)(2,1)S(1)}, bf16[128,640]{1,0:T(8,128)(2,1)S(1)}, bf16[128,640]{1,0:T(8,128)(2,1)S(1)}, bf16[128,640]{1,0:T(8,128)(2...) custom-call(bf16[128,640]{1,0:T(8,128)(2,1)S(1)} %copy-done.23, ...), custom_call_target="tpu_custom_call" | custom-call | flops 9130000384 | bytes 8693760 | tf_op jit(solution)/shard_map/pallas_call | solution.py:374
  198.3 4.0 %shard_map.292 = (bf16[640,1280]{1,0:T(8,128)(2,1)S(1)}, bf16[640,1280]{1,0:T(8,128)(2,1)S(1)}, bf16[640,1280]{1,0:T(8,128)(2,1)}) custom-call(s32[3]{0:T(128)S(1)} %pad_add_fusion.1.ids_ref.refs_0_, bf16[128,640]{1,0:T(8,128)(2,1)S(1)} %copy-done.23, bf16[128,640]{1,0:T(8,128)(2,1)S(1)} %copy-done.25, bf16[128,640]{1,0:T(8,128)(2,1)S(1)} %copy-done.27, ...), custom_call_target="tpu_custom_call" | custom-call | flops 5500000256 | bytes 10485772 | tf_op jit(solution)/shard_map/pallas_call | solution.py:374
  211.3 6.4 %shard_map.294 = (bf16[256,960]{1,0:T(8,128)(2,1)S(1)}, f32[128,640]{1,0:T(8,128)S(1)}, bf16[128,640]{1,0:T(8,128)(2,1)}, f32[1,960]{1,0:T(1,128)S(1)}) custom-call(s32[3]{0:T(128)S(1)} %pad_add_fusion.1.ids_ref.refs_0_, bf16[640,976]{1,0:T(8,128)(2,1)S(1)} %bitcast.204, bf16[256,960]{1,0:T(8,128)(2,1)S(1)} %copy-done.61, ...), custom_call_target="tpu_custom_call" | custom-call | flops 8800000000 | bytes 5512972 | tf_op jit(solution)/shard_map/pallas_call | solution.py:374
  227.2 3.0 add_convert_fusion
  230.2 17.6 %all-reduce.10.cloned.1.call-done = bf16[640,1280]{1,0:T(8,128)(2,1)} async-done(((bf16[640,1280]{1,0:T(8,128)(2,1)}), bf16[640,1280]{1,0:T(8,128)(2,1)}) %all-reduce.10.cloned.1.call-update) | async-done | bytes 1638416 | tf_op jit(solution)/shard_map/psum | solution.py:670
  257.5 5.0 %collective-permute-done.64 = bf16[320,1280]{1,0:T(8,128)(2,1)} collective-permute-done((bf16[320,1280]{1,0:T(8,128)(2,1)}, bf16[320,1280]{1,0:T(8,128)(2,1)}, u32[]{:S(2)}, u32[]{:S(2)}) %collective-permute-start.64) | collective-permute-done | bytes 819232 | tf_op jit(solution)/shard_map/ppermute | solution.py:393
  275.3 5.0 %collective-permute-done.61 = f32[2560]{0:T(1024)S(1)} collective-permute-done((f32[2560]{0:T(1024)S(1)}, f32[2560]{0:T(1024)S(1)}, u32[]{:S(2)}, u32[]{:S(2)}) %collective-permute-start.61) | collective-permute-done | bytes 10272 | tf_op jit(solution)/shard_map/ppermute | solution.py:393
  280.4 4.5 %collective-permute-done.62 = f32[2560]{0:T(1024)S(1)} collective-permute-done((f32[2560]{0:T(1024)S(1)}, f32[2560]{0:T(1024)S(1)}, u32[]{:S(2)}, u32[]{:S(2)}) %collective-permute-start.62) | collective-permute-done | bytes 10272 | tf_op jit(solution)/shard_map/ppermute | solution.py:393
  296.4 11.7 %collective-permute-done.55 = bf16[2,128,640]{2,1,0:T(8,128)(2,1)} collective-permute-done((bf16[2,128,640]{2,1,0:T(8,128)(2,1)}, bf16[2,128,640]{2,1,0:T(8,128)(2,1)}, u32[]{:S(2)}, u32[]{:S(2)}) %collective-permute-start.55) | collective-permute-done | bytes 327712 | tf_op jit(solution)/shard_map/ppermute | solution.py:393
  317.9 10.0 %collective-permute-done.68 = bf16[80,1280]{1,0:T(8,128)(2,1)S(1)} collective-permute-done((bf16[80,1280]{1,0:T(8,128)(2,1)S(1)}, bf16[80,1280]{1,0:T(8,128)(2,1)S(1)}, u32[]{:S(2)}, u32[]{:S(2)}) %collective-permute-start.68) | collective-permute-done | bytes 204832 | tf_op jit(solution)/shard_map/ppermute | solution.py:393
  329.2 12.8 %collective-permute-done.69 = bf16[80,1280]{1,0:T(8,128)(2,1)S(1)} collective-permute-done((bf16[80,1280]{1,0:T(8,128)(2,1)S(1)}, bf16[80,1280]{1,0:T(8,128)(2,1)S(1)}, u32[]{:S(2)}, u32[]{:S(2)}) %collective-permute-start.69) | collective-permute-done | bytes 204832 | tf_op jit(solution)/shard_map/ppermute | solution.py:393
  342.2 3.6 collective-permute-start.70
  347.6 10.3 %collective-permute-done.70 = bf16[2,80,1280]{2,1,0:T(8,128)(2,1)S(1)} collective-permute-done((bf16[2,80,1280]{2,1,0:T(8,128)(2,1)S(1)}, bf16[2,80,1280]{2,1,0:T(8,128)(2,1)S(1)}, u32[]{:S(2)}, u32[]{:S(2)}) %collective-permute-start.70) | collective-permute-done | bytes 409632 | tf_op jit(solution)/shard_map/ppermute | solution.py:393
  358.1 10.5 %all-reduce.12.cloned.1.call-done.both_ref = bf16[320,1280]{1,0:T(8,128)(2,1)} async-done(((bf16[320,1280]{1,0:T(8,128)(2,1)}), bf16[320,1280]{1,0:T(8,128)(2,1)}) %all-reduce.12.cloned.1.call-update) | async-done | bytes 819216 | tf_op jit(solution)/shard_map/psum | solution.py:735
  (440 shorter events, 170.1 us)
Async XLA Ops:
  7.2 98.6 %all-gather.2.cloned.1.call-start = ((), (), s32[]{:S(2)}) async-start(), calls=%async_computation | async-start | bytes 3870720 | tf_op jit(solution)/shard_map/all_gather | solution.py:594
  12.5 14.1 %collective-permute-start.6 = (bf16[80,1920]{1,0:T(8,128)(2,1)}, bf16[80,1920]{1,0:T(8,128)(2,1)}, u32[]{:S(2)}, u32[]{:S(2)}) collective-permute-start(bf16[80,1920]{1,0:T(8,128)(2,1)} %get-tuple-element.140), channel_id=1, source_target_pairs={{0,2},{1,3},{2,0},{3,1},{4,6},{5,7},{6,4},{7,5},{8,10},{9,11},{10,... | collective-permute-start | bytes 921608 | tf_op jit(solution)/shard_map/ppermute | solution.py:393
  15.4 22.5 %collective-permute-start.7 = (bf16[80,1920]{1,0:T(8,128)(2,1)}, bf16[80,1920]{1,0:T(8,128)(2,1)}, u32[]{:S(2)}, u32[]{:S(2)}) collective-permute-start(bf16[80,1920]{1,0:T(8,128)(2,1)} %get-tuple-element.141), channel_id=1, source_target_pairs={{0,4},{1,5},{2,6},{3,7},{4,0},{5,1},{6,2},{7,3},{8,12},{9,13},{10,... | collective-permute-start | bytes 921608 | tf_op jit(solution)/shard_map/ppermute | solution.py:393
  21.0 17.0 %collective-permute-start.8 = (bf16[80,1920]{1,0:T(8,128)(2,1)}, bf16[80,1920]{1,0:T(8,128)(2,1)S(1)}, u32[]{:S(2)}, u32[]{:S(2)}) collective-permute-start(bf16[80,1920]{1,0:T(8,128)(2,1)} %get-tuple-element.142), channel_id=1, source_target_pairs={{0,6},{1,7},{2,4},{3,5},{4,2},{5,3},{6,0},{7,1},{8,14},{9,15},{10,... | collective-permute-start | bytes 921608 | tf_op jit(solution)/shard_map/ppermute | solution.py:393
  23.0 18.4 %collective-permute-start.2 = (bf16[2,80,976]{2,1,0:T(8,128)(2,1)}, bf16[2,80,976]{2,1,0:T(8,128)(2,1)S(1)}, u32[]{:S(2)}, u32[]{:S(2)}) collective-permute-start(bf16[2,80,976]{2,1,0:T(8,128)(2,1)} %pad_maximum_fusion.11), channel_id=1, source_target_pairs={{0,6},{1,7},{2,4},{3,5},{4,2},{5,3},{6,0},{7,1},{8,14},{9,15},{10,... | collective-permute-start | bytes 936968 | tf_op jit(solution)/shard_map/ppermute | solution.py:393
  25.9 19.5 %collective-permute-start.3 = (bf16[2,80,976]{2,1,0:T(8,128)(2,1)}, bf16[2,80,976]{2,1,0:T(8,128)(2,1)}, u32[]{:S(2)}, u32[]{:S(2)}) collective-permute-start(bf16[2,80,976]{2,1,0:T(8,128)(2,1)} %pad_maximum_fusion.11), channel_id=1, source_target_pairs={{0,4},{1,5},{2,6},{3,7},{4,0},{5,1},{6,2},{7,3},{8,12},{9,13},{10,... | collective-permute-start | bytes 936968 | tf_op jit(solution)/shard_map/ppermute | solution.py:393
  26.6 18.8 %collective-permute-start.4 = (bf16[2,80,976]{2,1,0:T(8,128)(2,1)}, bf16[2,80,976]{2,1,0:T(8,128)(2,1)}, u32[]{:S(2)}, u32[]{:S(2)}) collective-permute-start(bf16[2,80,976]{2,1,0:T(8,128)(2,1)} %pad_maximum_fusion.11), channel_id=1, source_target_pairs={{0,2},{1,3},{2,0},{3,1},{4,6},{5,7},{6,4},{7,5},{8,10},{9,11},{10,... | collective-permute-start | bytes 936968 | tf_op jit(solution)/shard_map/ppermute | solution.py:393
  37.9 23.2 %collective-permute-start.19 = (bf16[640,640]{1,0:T(8,128)(2,1)}, bf16[640,640]{1,0:T(8,128)(2,1)}, u32[]{:S(2)}, u32[]{:S(2)}) collective-permute-start(bf16[640,640]{1,0:T(8,128)(2,1)} %get-tuple-element.157), channel_id=1, source_target_pairs={{0,1},{1,0},{2,3},{3,2},{4,5},{5,4},{6,7},{7,6},{8,9},{9,8},{10,11... | collective-permute-start | bytes 2457608 | tf_op jit(solution)/shard_map/ppermute | solution.py:393
  40.6 22.3 %collective-permute-start.14 = (bf16[4,80,1920]{2,1,0:T(8,128)(2,1)}, bf16[4,80,1920]{2,1,0:T(8,128)(2,1)}, u32[]{:S(2)}, u32[]{:S(2)}) collective-permute-start(bf16[4,80,1920]{2,1,0:T(8,128)(2,1)} %pad_maximum_fusion.5), channel_id=1, source_target_pairs={{0,1},{1,0},{2,3},{3,2},{4,5},{5,4},{6,7},{7,6},{8,9},{9,8},{10,11... | collective-permute-start | bytes 3686408 | tf_op jit(solution)/shard_map/ppermute | solution.py:393
  41.1 206.7 %all-reduce.10.cloned.1.call-start = ((), (), s32[]{:S(2)}) async-start(), calls=%async_computation.1 | async-start | bytes 3276800 | tf_op jit(solution)/shard_map/psum | solution.py:670
  69.0 15.2 %collective-permute-start.17 = (bf16[128,640]{1,0:T(8,128)(2,1)S(1)}, bf16[128,640]{1,0:T(8,128)(2,1)S(1)}, u32[]{:S(2)}, u32[]{:S(2)}) collective-permute-start(bf16[128,640]{1,0:T(8,128)(2,1)S(1)} %get-tuple-element.153.refs_0_.refs_1_), channel_id=1, source_target_pairs={{0,6},{1,7},{2,4},{3,5},{4,2},{5,3},{6,0},{7,1},{8,14},{9,15},{10,... | collective-permute-start | bytes 491528 | tf_op jit(solution)/shard_map/ppermute | solution.py:393
  99.6 16.4 %collective-permute-start.32 = (bf16[640,640]{1,0:T(8,128)(2,1)}, bf16[640,640]{1,0:T(8,128)(2,1)}, u32[]{:S(2)}, u32[]{:S(2)}) collective-permute-start(bf16[640,640]{1,0:T(8,128)(2,1)} %get-tuple-element.175), channel_id=1, source_target_pairs={{0,1},{1,0},{2,3},{3,2},{4,5},{5,4},{6,7},{7,6},{8,9},{9,8},{10,11... | collective-permute-start | bytes 2457608 | tf_op jit(solution)/shard_map/ppermute | solution.py:393
  154.1 24.6 %collective-permute-start.39 = (bf16[128,640]{1,0:T(8,128)(2,1)}, bf16[128,640]{1,0:T(8,128)(2,1)}, u32[]{:S(2)}, u32[]{:S(2)}) collective-permute-start(bf16[128,640]{1,0:T(8,128)(2,1)} %get-tuple-element.196), channel_id=1, source_target_pairs={{0,2},{1,3},{2,0},{3,1},{4,6},{5,7},{6,4},{7,5},{8,10},{9,11},{10,... | collective-permute-start | bytes 491528 | tf_op jit(solution)/shard_map/ppermute | solution.py:393
  155.2 23.6 %collective-permute-start.40 = (bf16[128,640]{1,0:T(8,128)(2,1)}, bf16[128,640]{1,0:T(8,128)(2,1)}, u32[]{:S(2)}, u32[]{:S(2)}) collective-permute-start(bf16[128,640]{1,0:T(8,128)(2,1)} %get-tuple-element.197), channel_id=1, source_target_pairs={{0,4},{1,5},{2,6},{3,7},{4,0},{5,1},{6,2},{7,3},{8,12},{9,13},{10,... | collective-permute-start | bytes 491528 | tf_op jit(solution)/shard_map/ppermute | solution.py:393
  155.8 22.9 %collective-permute-start.41 = (bf16[128,640]{1,0:T(8,128)(2,1)}, bf16[128,640]{1,0:T(8,128)(2,1)}, u32[]{:S(2)}, u32[]{:S(2)}) collective-permute-start(bf16[128,640]{1,0:T(8,128)(2,1)} %get-tuple-element.198), channel_id=1, source_target_pairs={{0,6},{1,7},{2,4},{3,5},{4,2},{5,3},{6,0},{7,1},{8,14},{9,15},{10,... | collective-permute-start | bytes 491528 | tf_op jit(solution)/shard_map/ppermute | solution.py:393
  168.9 141.0 %all-reduce.14.cloned.1.call-start = ((), (), s32[]{:S(2)}) async-start(), calls=%async_computation.3 | async-start | bytes 1638400 | tf_op jit(solution)/shard_map/psum | solution.py:693
  185.0 21.1 %collective-permute-start.45 = (bf16[128,640]{1,0:T(8,128)(2,1)S(1)}, bf16[128,640]{1,0:T(8,128)(2,1)S(1)}, u32[]{:S(2)}, u32[]{:S(2)}) collective-permute-start(bf16[128,640]{1,0:T(8,128)(2,1)S(1)} %add_convert_fusion.3), channel_id=1, source_target_pairs={{0,16},{8,24},{16,0},{24,8},{1,17},{9,25},{17,1},{25,9},{2,18},{10... | collective-permute-start | bytes 491528 | tf_op jit(solution)/shard_map/ppermute | solution.py:393
  207.5 18.1 %collective-permute-start.51 = (bf16[640,1280]{1,0:T(8,128)(2,1)}, bf16[640,1280]{1,0:T(8,128)(2,1)}, u32[]{:S(2)}, u32[]{:S(2)}) collective-permute-start(bf16[640,1280]{1,0:T(8,128)(2,1)} %copy-done.11), channel_id=1, source_target_pairs={{0,1},{1,0},{2,3},{3,2},{4,5},{5,4},{6,7},{7,6},{8,9},{9,8},{10,11... | collective-permute-start | bytes 4915208 | tf_op jit(solution)/shard_map/ppermute | solution.py:393
  208.1 22.1 %collective-permute-start.52 = (bf16[2,128,640]{2,1,0:T(8,128)(2,1)}, bf16[2,128,640]{2,1,0:T(8,128)(2,1)}, u32[]{:S(2)}, u32[]{:S(2)}) collective-permute-start(bf16[2,128,640]{2,1,0:T(8,128)(2,1)} %pad_maximum_fusion.12), channel_id=1, source_target_pairs={{0,8},{8,0},{16,24},{24,16},{1,9},{9,1},{17,25},{25,17},{2,10},{10... | collective-permute-start | bytes 983048 | tf_op jit(solution)/shard_map/ppermute | solution.py:393
  223.3 34.2 %collective-permute-start.63 = (bf16[320,1280]{1,0:T(8,128)(2,1)}, bf16[320,1280]{1,0:T(8,128)(2,1)}, u32[]{:S(2)}, u32[]{:S(2)}) collective-permute-start(bf16[320,1280]{1,0:T(8,128)(2,1)} %get-tuple-element.239), channel_id=1, source_target_pairs={{0,2},{1,3},{2,0},{3,1},{4,6},{5,7},{6,4},{7,5},{8,10},{9,11},{10,... | collective-permute-start | bytes 2457608 | tf_op jit(solution)/shard_map/ppermute | solution.py:393
  224.4 38.1 %collective-permute-start.64 = (bf16[320,1280]{1,0:T(8,128)(2,1)}, bf16[320,1280]{1,0:T(8,128)(2,1)}, u32[]{:S(2)}, u32[]{:S(2)}) collective-permute-start(bf16[320,1280]{1,0:T(8,128)(2,1)} %get-tuple-element.240), channel_id=1, source_target_pairs={{0,4},{1,5},{2,6},{3,7},{4,0},{5,1},{6,2},{7,3},{8,12},{9,13},{10,... | collective-permute-start | bytes 2457608 | tf_op jit(solution)/shard_map/ppermute | solution.py:393
  225.6 36.8 %collective-permute-start.65 = (bf16[320,1280]{1,0:T(8,128)(2,1)}, bf16[320,1280]{1,0:T(8,128)(2,1)}, u32[]{:S(2)}, u32[]{:S(2)}) collective-permute-start(bf16[320,1280]{1,0:T(8,128)(2,1)} %copy-done.13), channel_id=1, source_target_pairs={{0,6},{1,7},{2,4},{3,5},{4,2},{5,3},{6,0},{7,1},{8,14},{9,15},{10,... | collective-permute-start | bytes 2457608 | tf_op jit(solution)/shard_map/ppermute | solution.py:393
  250.6 37.1 %collective-permute-start.54 = (bf16[128,640]{1,0:T(8,128)(2,1)S(1)}, bf16[128,640]{1,0:T(8,128)(2,1)S(1)}, u32[]{:S(2)}, u32[]{:S(2)}) collective-permute-start(bf16[128,640]{1,0:T(8,128)(2,1)S(1)} %get-tuple-element.223), channel_id=1, source_target_pairs={{0,16},{8,24},{16,0},{24,8},{1,17},{9,25},{17,1},{25,9},{2,18},{10... | collective-permute-start | bytes 491528 | tf_op jit(solution)/shard_map/ppermute | solution.py:393
  252.9 42.4 %collective-permute-start.67 = (bf16[2,80,1280]{2,1,0:T(8,128)(2,1)}, bf16[2,80,1280]{2,1,0:T(8,128)(2,1)}, u32[]{:S(2)}, u32[]{:S(2)}) collective-permute-start(bf16[2,80,1280]{2,1,0:T(8,128)(2,1)} %dynamic-slice_bitcast_fusion), channel_id=1, source_target_pairs={{0,8},{8,0},{16,24},{24,16},{1,9},{9,1},{17,25},{25,17},{2,10},{10... | collective-permute-start | bytes 1228808 | tf_op jit(solution)/shard_map/ppermute | solution.py:393
  253.5 115.1 %all-reduce.12.cloned.1.call-start = ((), (), s32[]{:S(2)}) async-start(), calls=%async_computation.2 | async-start | bytes 1638400 | tf_op jit(solution)/shard_map/psum | solution.py:735
  272.8 15.7 %collective-permute-start.74 = (bf16[80,1280]{1,0:T(8,128)(2,1)}, bf16[80,1280]{1,0:T(8,128)(2,1)}, u32[]{:S(2)}, u32[]{:S(2)}) collective-permute-start(bf16[80,1280]{1,0:T(8,128)(2,1)} %get-tuple-element.269), channel_id=1, source_target_pairs={{0,6},{1,7},{2,4},{3,5},{4,2},{5,3},{6,0},{7,1},{8,14},{9,15},{10,... | collective-permute-start | bytes 614408 | tf_op jit(solution)/shard_map/ppermute | solution.py:393
  274.3 14.6 %collective-permute-start.75 = (bf16[80,1280]{1,0:T(8,128)(2,1)}, bf16[80,1280]{1,0:T(8,128)(2,1)}, u32[]{:S(2)}, u32[]{:S(2)}) collective-permute-start(bf16[80,1280]{1,0:T(8,128)(2,1)} %get-tuple-element.268), channel_id=1, source_target_pairs={{0,4},{1,5},{2,6},{3,7},{4,0},{5,1},{6,2},{7,3},{8,12},{9,13},{10,... | collective-permute-start | bytes 614408 | tf_op jit(solution)/shard_map/ppermute | solution.py:393
  289.0 19.1 %collective-permute-start.55 = (bf16[2,128,640]{2,1,0:T(8,128)(2,1)}, bf16[2,128,640]{2,1,0:T(8,128)(2,1)}, u32[]{:S(2)}, u32[]{:S(2)}) collective-permute-start(bf16[2,128,640]{2,1,0:T(8,128)(2,1)} %pad_maximum_fusion.15), channel_id=1, source_target_pairs={{0,8},{8,0},{16,24},{24,16},{1,9},{9,1},{17,25},{25,17},{2,10},{10... | collective-permute-start | bytes 983048 | tf_op jit(solution)/shard_map/ppermute | solution.py:393
  309.9 17.9 %collective-permute-start.68 = (bf16[80,1280]{1,0:T(8,128)(2,1)S(1)}, bf16[80,1280]{1,0:T(8,128)(2,1)S(1)}, u32[]{:S(2)}, u32[]{:S(2)}) collective-permute-start(bf16[80,1280]{1,0:T(8,128)(2,1)S(1)} %dynamic-slice_bitcast_fusion.3), channel_id=1, source_target_pairs={{0,16},{8,24},{16,0},{24,8},{1,17},{9,25},{17,1},{25,9},{2,18},{10... | collective-permute-start | bytes 614408 | tf_op jit(solution)/shard_map/ppermute | solution.py:393
  313.0 14.9 %collective-permute-start.71 = (bf16[80,1280]{1,0:T(8,128)(2,1)S(1)}, bf16[80,1280]{1,0:T(8,128)(2,1)S(1)}, u32[]{:S(2)}, u32[]{:S(2)}) collective-permute-start(bf16[80,1280]{1,0:T(8,128)(2,1)S(1)} %get-tuple-element.302), channel_id=1, source_target_pairs={{0,6},{1,7},{2,4},{3,5},{4,2},{5,3},{6,0},{7,1},{8,14},{9,15},{10,... | collective-permute-start | bytes 614408 | tf_op jit(solution)/shard_map/ppermute | solution.py:393
  327.9 14.2 %collective-permute-start.69 = (bf16[80,1280]{1,0:T(8,128)(2,1)S(1)}, bf16[80,1280]{1,0:T(8,128)(2,1)S(1)}, u32[]{:S(2)}, u32[]{:S(2)}) collective-permute-start(bf16[80,1280]{1,0:T(8,128)(2,1)S(1)} %fusion.1), channel_id=1, source_target_pairs={{0,16},{8,24},{16,0},{24,8},{1,17},{9,25},{17,1},{25,9},{2,18},{10... | collective-permute-start | bytes 614408 | tf_op jit(solution)/shard_map/ppermute | solution.py:393
  342.2 15.8 %collective-permute-start.70 = (bf16[2,80,1280]{2,1,0:T(8,128)(2,1)S(1)}, bf16[2,80,1280]{2,1,0:T(8,128)(2,1)S(1)}, u32[]{:S(2)}, u32[]{:S(2)}) collective-permute-start(bf16[2,80,1280]{2,1,0:T(8,128)(2,1)S(1)} %pad_maximum_fusion.10), channel_id=1, source_target_pairs={{0,8},{8,0},{16,24},{24,16},{1,9},{9,1},{17,25},{25,17},{2,10},{10... | collective-permute-start | bytes 1228808 | tf_op jit(solution)/shard_map/ppermute | solution.py:393
  (138 other events, 879.4 us)
Sparse Core Ops, SparseCore 0:
  41.3 46.1 all-gather.1
  169.0 78.8 all-reduce.9
  253.6 56.2 all-reduce.13
  312.8 55.7 all-reduce.11

commit v4 on v3

--- a/solution.py
+++ b/solution.py
@@ -576,7 +576,7 @@
         v = jnp.where(core == 0, vec(l, 3)[:, :cols], vec(l, 3)[:, cols:])
         return jnp.concatenate([q, zero_cols, v], axis=1)
 
-    qkv_full, qkv_step, out_at = [qkv0, None], [0, step], [0, 2 * step]
+    qkv_full, qkv_step, out_at = [qkv0, None], [0, 0], [0, 0]
     up_full, down_full, out_full = [None, None], [None, None], [None, None]
     saved = []
     for l in range(layers):
@@ -586,13 +586,15 @@
             [like((length, 3 * cols), BF), like((length, cols), BF)],
             [ids, own, sib, vec(l, 0), vec(l, 1), qkv_full[l], core_bias(l)],
             smem=1,
+            limit=VMEM_MOST,
         )
         if l == 0:
             ctx, *g_parts = lax.optimization_barrier((ctx, *g_sent))
             out_full[0] = up_full[0] = join(feed0)
             down_full[0] = chip_rows(after(down_weight[0], own))
             rest1 = lax.all_gather(after(rest1, own), "dp", axis=0, tiled=True)
-            qkv_full[1] = out_full[1] = rest1
+            qkv_full[1] = lax.dynamic_slice_in_dim(rest1, core * step, step, 1)
+            out_full[1] = rest1[:, 2 * step :]
         else:
             ctx, *up1 = lax.optimization_barrier((ctx, *up1))
             up_full[1] = join(up1)
@@ -616,6 +618,9 @@
                 scratch=[((count * half, width), F32)],
             )
             got = [sums[0]] + [swap_chip(sums[j], j) for j in range(1, count)]
+            got[1], qkv_full[1], out_full[1] = lax.optimization_barrier(
+                (got[1], qkv_full[1], out_full[1])
+            )
             own = (total([mid, *got]) + vec(l, 7)).astype(BF)
             sib = to_sibling(own)
             up1 = trade_up(1, own)
@@ -679,6 +684,7 @@
             [ids, qkv_full[l], proj, grad_mid, gm_sib, out_full[l]],
             scratch=[((length, cols), BF), ((cols, length), F32)],
             smem=1,
+            limit=VMEM_MOST,
         )
         gn_recv = to_sibling(gn_sib)
         if top:

time: 384 us -> 369 us (0.961)
  waiting for transfers between devices: 153 us -> 133 us
  Pallas kernels: 57 us -> 64.4 us
    ppermute x77, waiting for transfers between devices: 124 us -> 107 us  [swap(): return lax.ppermute(x, axis, [(i, i ^ bit) for i in range(size)])]
    pallas_call x19, Pallas kernels: 57 us -> 64.4 us  [run(): pl.pallas_call(kernel, out_shape=[jax.ShapeDtypeStruct(o.shape, o.dtype)...]
    unnamed x178 -> x196, local copies, waits for them, and re-layouts: 22.9 us -> 18.8 us
  transfers between devices with their start and end apart: 81 -> 81, of which waited for: 31 -> 28; matrix products, arithmetic and copies ran while one was open for 15% -> 16% of each run, Pallas kernels for 13% -> 15%
where the time goes in v4:
time: 369 us; the launch traced here: 365 us
  waiting for transfers between devices  133 us (36%)
  starting transfers between devices  71.8 us (19%)
  Pallas kernels  64.4 us (17%)
  other arithmetic  40.6 us (11%)
  local copies, waits for them, and re-layouts  39 us (11%)
  between operations  16.6 us (4%)
    ppermute x77, waiting for transfers between devices, swap(): return lax.ppermute(x, axis, [(i, i ^ bit) for i in range(size)])  107 us
    ppermute x77, starting transfers between devices, swap(): return lax.ppermute(x, axis, [(i, i ^ bit) for i in range(size)])  71.5 us
    pallas_call x19, Pallas kernels, run(): pl.pallas_call(kernel, out_shape=[jax.ShapeDtypeStruct(o.shape, o.dtype)...  64.4 us
    unnamed x196, local copies, waits for them, and re-layouts  18.8 us
    psum x1, waiting for transfers between devices, shards(): ffn_grads[1] = lax.psum(fw_sum, 'section')  16.4 us
    psum x1, waiting for transfers between devices, shards(): lax.psum(both, 'section', axis_index_groups=[[i ^ 1 for i in range(lax.ax...  8.59 us
  transfers between devices with their start and end apart: 81, of which 28 were waited for; matrix products, arithmetic and copies ran while one was open for 16% of the time, Pallas kernels for 15%

profile of v4, /device:TPU:0, one launch (start us, length us, event | category | flops | bytes accessed | tf_op | source)
XLA Modules:
  0.0 365.1 jit_solution(4771352294827238731)
XLA Ops:
  7.8 3.4 shard_map.280
  12.5 2.9 collective-permute-start.6
  24.7 2.9 collective-permute-start.2
  29.2 4.4 %collective-permute-done.8 = bf16[80,1920]{1,0:T(8,128)(2,1)S(1)} collective-permute-done((bf16[80,1920]{1,0:T(8,128)(2,1)}, bf16[80,1920]{1,0:T(8,128)(2,1)S(1)}, u32[]{:S(2)}, u32[]{:S(2)}) %collective-permute-start.8) | collective-permute-done | bytes 307232 | tf_op jit(solution)/shard_map/ppermute | solution.py:393
  36.8 3.9 %collective-permute-done.2 = bf16[2,80,976]{2,1,0:T(8,128)(2,1)} collective-permute-done((bf16[2,80,976]{2,1,0:T(8,128)(2,1)}, bf16[2,80,976]{2,1,0:T(8,128)(2,1)}, u32[]{:S(2)}, u32[]{:S(2)}) %collective-permute-start.2) | collective-permute-done | bytes 312352 | tf_op jit(solution)/shard_map/ppermute | solution.py:393
  40.7 6.1 %collective-permute-done.3 = bf16[2,80,976]{2,1,0:T(8,128)(2,1)} collective-permute-done((bf16[2,80,976]{2,1,0:T(8,128)(2,1)}, bf16[2,80,976]{2,1,0:T(8,128)(2,1)}, u32[]{:S(2)}, u32[]{:S(2)}) %collective-permute-start.3) | collective-permute-done | bytes 312352 | tf_op jit(solution)/shard_map/ppermute | solution.py:393
  53.7 5.8 %shard_map.281 = (bf16[256,960]{1,0:T(8,128)(2,1)}, bf16[256,320]{1,0:T(8,128)(2,1)}) custom-call(s32[3]{0:T(128)} %pad_add_fusion.1.ids_ref.refs_0_, bf16[128,640]{1,0:T(8,128)(2,1)} %get-tuple-element.146.own_ref, bf16[128,640]{1,0:T(8,128)(2,1)} %get-tuple-element.329.sib_ref, f32[1,640]{1,0:T(1,128)} %get-tuple-element.351.gain_ref, ...), custom_call_target="tpu_custom_call" | custom-call | flops 6600000000 | bytes 2241292 | tf_op jit(solution)/shard_map/pallas_call | solution.py:374
  70.6 3.4 collective-permute-done.15.refs_1_.refs_2_
  74.1 3.2 collective-permute-done.17.refs_3_.refs_4_
  77.3 3.3 shard_map.283
  98.1 6.2 %shard_map.284 = (bf16[256,960]{1,0:T(8,128)(2,1)}, bf16[256,320]{1,0:T(8,128)(2,1)}) custom-call(s32[3]{0:T(128)} %pad_add_fusion.1.ids_ref.refs_0_, bf16[128,640]{1,0:T(8,128)(2,1)} %copy-done.12, bf16[128,640]{1,0:T(8,128)(2,1)} %copy-done.52, f32[1,640]{1,0:T(1,128)} %get-tuple-element.342.gain_ref, f32[1,640]{1,0:T(1,128)} %get-tuple-element.341.shift_ref, ...), custom_call_target="tpu_custom_call" | custom-call | flops 6600000000 | bytes 2302732 | tf_op jit(solution)/shard_map/pallas_call | solution.py:374
  115.9 3.7 %collective-permute-done.29.refs_2_.refs_3_ = bf16[128,640]{1,0:T(8,128)(2,1)S(1)} collective-permute-done((bf16[128,640]{1,0:T(8,128)(2,1)S(1)}, bf16[128,640]{1,0:T(8,128)(2,1)S(1)}, u32[]{:S(2)}, u32[]{:S(2)}) %collective-permute-start.29) | collective-permute-done | bytes 163872 | tf_op jit(solution)/shard_map/ppermute | solution.py:393
  119.6 4.3 %shard_map.286 = (bf16[128,640]{1,0:T(8,128)(2,1)S(1)}, bf16[128,640]{1,0:T(8,128)(2,1)S(1)}, bf16[128,640]{1,0:T(8,128)(2,1)S(1)}, bf16[128,640]{1,0:T(8,128)(2...) custom-call(bf16[128,640]{1,0:T(8,128)(2,1)S(1)} %get-tuple-element.172.refs_0_.refs_1_, ...), custom_call_target="tpu_custom_call" | custom-call | flops 9130000384 | bytes 7874560 | tf_op jit(solution)/shard_map/pallas_call | solution.py:374
  127.4 5.5 %shard_map.287 = (bf16[640,1280]{1,0:T(8,128)(2,1)S(1)}, bf16[640,1280]{1,0:T(8,128)(2,1)}, bf16[640,1280]{1,0:T(8,128)(2,1)}, bf16[128,640]{1,0:T(8,128)(2,1)S(...) custom-call(s32[3]{0:T(128)S(1)} %copy-done.24, ...), custom_call_target="tpu_custom_call" | custom-call | flops 5500000256 | bytes 11141132 | tf_op jit(solution)/shard_map/pallas_call | solution.py:374
  134.8 3.5 collective-permute-done.37
  138.3 3.6 add_convert_fusion.1
  145.4 7.6 %shard_map.289 = (bf16[256,960]{1,0:T(8,128)(2,1)}, f32[128,640]{1,0:T(8,128)}, bf16[128,640]{1,0:T(8,128)(2,1)}, f32[1,960]{1,0:T(1,128)}) custom-call(s32[3]{0:T(128)} %pad_add_fusion.1.ids_ref.refs_0_, bf16[640,1024]{1,0:T(8,128)(2,1)} %constant_dynamic-slice_fusion.4.w_ref, bf16[256,960]{1,0:T(8,128)(2,1)} %get-tuple-element.167.proj_ref, ...), custom_call_target="tpu_custom_call" | custom-call | flops 8800000000 | bytes 3936012 | tf_op jit(solution)/shard_map/pallas_call | solution.py:374
  174.0 4.3 %shard_map.291 = (bf16[128,640]{1,0:T(8,128)(2,1)S(1)}, bf16[128,640]{1,0:T(8,128)(2,1)S(1)}, bf16[128,640]{1,0:T(8,128)(2,1)S(1)}, bf16[128,640]{1,0:T(8,128)(2...) custom-call(bf16[128,640]{1,0:T(8,128)(2,1)S(1)} %copy-done.39, ...), custom_call_target="tpu_custom_call" | custom-call | flops 9130000384 | bytes 8693760 | tf_op jit(solution)/shard_map/pallas_call | solution.py:374
  181.9 4.0 %shard_map.292 = (bf16[640,1280]{1,0:T(8,128)(2,1)S(1)}, bf16[640,1280]{1,0:T(8,128)(2,1)S(1)}, bf16[640,1280]{1,0:T(8,128)(2,1)}) custom-call(s32[3]{0:T(128)S(1)} %copy-done.25, bf16[128,640]{1,0:T(8,128)(2,1)S(1)} %copy-done.39, bf16[128,640]{1,0:T(8,128)(2,1)S(1)} %copy-done.41, bf16[128,640]{1,0:T(8,128)(2,1)S(1)} %copy-done.43, ...), custom_call_target="tpu_custom_call" | custom-call | flops 5500000256 | bytes 10485772 | tf_op jit(solution)/shard_map/pallas_call | solution.py:374
  185.9 4.3 %collective-permute-done.45 = bf16[128,640]{1,0:T(8,128)(2,1)S(1)} collective-permute-done((bf16[128,640]{1,0:T(8,128)(2,1)S(1)}, bf16[128,640]{1,0:T(8,128)(2,1)S(1)}, u32[]{:S(2)}, u32[]{:S(2)}) %collective-permute-start.45) | collective-permute-done | bytes 163872 | tf_op jit(solution)/shard_map/ppermute | solution.py:393
  193.7 8.4 %shard_map.294 = (bf16[256,960]{1,0:T(8,128)(2,1)}, f32[128,640]{1,0:T(8,128)}, bf16[128,640]{1,0:T(8,128)(2,1)}, f32[1,960]{1,0:T(1,128)}) custom-call(s32[3]{0:T(128)} %pad_add_fusion.1.ids_ref.refs_0_, bf16[640,976]{1,0:T(8,128)(2,1)} %bitcast.212, bf16[256,960]{1,0:T(8,128)(2,1)} %get-tuple-element.147.proj_ref, bf16[128,640]{1,0:T(8,128)(2,1)} %copy-done.57, ...), custom_call_target="tpu_custom_call" | custom-call | flops 8800000000 | bytes 5512972 | tf_op jit(solution)/shard_map/pallas_call | solution.py:374
  212.9 3.0 add_convert_fusion
  215.9 16.4 %all-reduce.10.cloned.1.call-done = bf16[640,1280]{1,0:T(8,128)(2,1)} async-done(((bf16[640,1280]{1,0:T(8,128)(2,1)}), bf16[640,1280]{1,0:T(8,128)(2,1)}) %all-reduce.10.cloned.1.call-update) | async-done | bytes 1638416 | tf_op jit(solution)/shard_map/psum | solution.py:675
  242.7 4.6 %collective-permute-done.64 = bf16[320,1280]{1,0:T(8,128)(2,1)} collective-permute-done((bf16[320,1280]{1,0:T(8,128)(2,1)}, bf16[320,1280]{1,0:T(8,128)(2,1)}, u32[]{:S(2)}, u32[]{:S(2)}) %collective-permute-start.64) | collective-permute-done | bytes 819232 | tf_op jit(solution)/shard_map/ppermute | solution.py:393
  260.8 4.8 %collective-permute-done.61 = f32[2560]{0:T(1024)S(1)} collective-permute-done((f32[2560]{0:T(1024)S(1)}, f32[2560]{0:T(1024)S(1)}, u32[]{:S(2)}, u32[]{:S(2)}) %collective-permute-start.61) | collective-permute-done | bytes 10272 | tf_op jit(solution)/shard_map/ppermute | solution.py:393
  265.7 4.5 %collective-permute-done.62 = f32[2560]{0:T(1024)S(1)} collective-permute-done((f32[2560]{0:T(1024)S(1)}, f32[2560]{0:T(1024)S(1)}, u32[]{:S(2)}, u32[]{:S(2)}) %collective-permute-start.62) | collective-permute-done | bytes 10272 | tf_op jit(solution)/shard_map/ppermute | solution.py:393
  281.7 11.7 %collective-permute-done.55 = bf16[2,128,640]{2,1,0:T(8,128)(2,1)} collective-permute-done((bf16[2,128,640]{2,1,0:T(8,128)(2,1)}, bf16[2,128,640]{2,1,0:T(8,128)(2,1)}, u32[]{:S(2)}, u32[]{:S(2)}) %collective-permute-start.55) | collective-permute-done | bytes 327712 | tf_op jit(solution)/shard_map/ppermute | solution.py:393
  303.2 10.0 %collective-permute-done.68 = bf16[80,1280]{1,0:T(8,128)(2,1)S(1)} collective-permute-done((bf16[80,1280]{1,0:T(8,128)(2,1)S(1)}, bf16[80,1280]{1,0:T(8,128)(2,1)S(1)}, u32[]{:S(2)}, u32[]{:S(2)}) %collective-permute-start.68) | collective-permute-done | bytes 204832 | tf_op jit(solution)/shard_map/ppermute | solution.py:393
  314.6 12.7 %collective-permute-done.69 = bf16[80,1280]{1,0:T(8,128)(2,1)S(1)} collective-permute-done((bf16[80,1280]{1,0:T(8,128)(2,1)S(1)}, bf16[80,1280]{1,0:T(8,128)(2,1)S(1)}, u32[]{:S(2)}, u32[]{:S(2)}) %collective-permute-start.69) | collective-permute-done | bytes 204832 | tf_op jit(solution)/shard_map/ppermute | solution.py:393
  327.4 3.7 %collective-permute-start.70 = (bf16[2,80,1280]{2,1,0:T(8,128)(2,1)S(1)}, bf16[2,80,1280]{2,1,0:T(8,128)(2,1)S(1)}, u32[]{:S(2)}, u32[]{:S(2)}) collective-permute-start(bf16[2,80,1280]{2,1,0:T(8,128)(2,1)S(1)} %pad_maximum_fusion.10), channel_id=1, source_target_pairs={{0,8},{8,0},{16,24},{24,16},{1,9},{9,1},{17,25},{25,17},{2,10},{10... | collective-permute-start | bytes 1228808 | tf_op jit(solution)/shard_map/ppermute | solution.py:393
  333.0 12.0 %collective-permute-done.70 = bf16[2,80,1280]{2,1,0:T(8,128)(2,1)S(1)} collective-permute-done((bf16[2,80,1280]{2,1,0:T(8,128)(2,1)S(1)}, bf16[2,80,1280]{2,1,0:T(8,128)(2,1)S(1)}, u32[]{:S(2)}, u32[]{:S(2)}) %collective-permute-start.70) | collective-permute-done | bytes 409632 | tf_op jit(solution)/shard_map/ppermute | solution.py:393
  345.2 8.6 %all-reduce.12.cloned.1.call-done.both_ref = bf16[320,1280]{1,0:T(8,128)(2,1)} async-done(((bf16[320,1280]{1,0:T(8,128)(2,1)}), bf16[320,1280]{1,0:T(8,128)(2,1)}) %all-reduce.12.cloned.1.call-update) | async-done | bytes 819216 | tf_op jit(solution)/shard_map/psum | solution.py:741
  (460 shorter events, 161.7 us)
Async XLA Ops:
  7.2 78.6 %all-gather.2.cloned.1.call-start = ((), (), s32[]{:S(2)}) async-start(), calls=%async_computation | async-start | bytes 3870720 | tf_op jit(solution)/shard_map/all_gather | solution.py:595
  12.4 15.3 %collective-permute-start.5 = (bf16[256,640]{1,0:T(8,128)(2,1)}, bf16[256,640]{1,0:T(8,128)(2,1)S(1)}, u32[]{:S(2)}, u32[]{:S(2)}) collective-permute-start(bf16[256,640]{1,0:T(8,128)(2,1)} %dynamic-slice_bitcast_fusion.2), channel_id=1, source_target_pairs={{0,1},{1,0},{2,3},{3,2},{4,5},{5,4},{6,7},{7,6},{8,9},{9,8},{10,11... | collective-permute-start | bytes 983048 | tf_op jit(solution)/shard_map/ppermute | solution.py:393
  12.5 16.6 %collective-permute-start.6 = (bf16[80,1920]{1,0:T(8,128)(2,1)}, bf16[80,1920]{1,0:T(8,128)(2,1)}, u32[]{:S(2)}, u32[]{:S(2)}) collective-permute-start(bf16[80,1920]{1,0:T(8,128)(2,1)} %get-tuple-element.143), channel_id=1, source_target_pairs={{0,2},{1,3},{2,0},{3,1},{4,6},{5,7},{6,4},{7,5},{8,10},{9,11},{10,... | collective-permute-start | bytes 921608 | tf_op jit(solution)/shard_map/ppermute | solution.py:393
  15.4 13.8 %collective-permute-start.7 = (bf16[80,1920]{1,0:T(8,128)(2,1)}, bf16[80,1920]{1,0:T(8,128)(2,1)}, u32[]{:S(2)}, u32[]{:S(2)}) collective-permute-start(bf16[80,1920]{1,0:T(8,128)(2,1)} %get-tuple-element.144), channel_id=1, source_target_pairs={{0,4},{1,5},{2,6},{3,7},{4,0},{5,1},{6,2},{7,3},{8,12},{9,13},{10,... | collective-permute-start | bytes 921608 | tf_op jit(solution)/shard_map/ppermute | solution.py:393
  24.7 16.0 %collective-permute-start.2 = (bf16[2,80,976]{2,1,0:T(8,128)(2,1)}, bf16[2,80,976]{2,1,0:T(8,128)(2,1)}, u32[]{:S(2)}, u32[]{:S(2)}) collective-permute-start(bf16[2,80,976]{2,1,0:T(8,128)(2,1)} %pad_maximum_fusion.11), channel_id=1, source_target_pairs={{0,6},{1,7},{2,4},{3,5},{4,2},{5,3},{6,0},{7,1},{8,14},{9,15},{10,... | collective-permute-start | bytes 936968 | tf_op jit(solution)/shard_map/ppermute | solution.py:393
  27.7 19.0 %collective-permute-start.3 = (bf16[2,80,976]{2,1,0:T(8,128)(2,1)}, bf16[2,80,976]{2,1,0:T(8,128)(2,1)}, u32[]{:S(2)}, u32[]{:S(2)}) collective-permute-start(bf16[2,80,976]{2,1,0:T(8,128)(2,1)} %pad_maximum_fusion.11), channel_id=1, source_target_pairs={{0,4},{1,5},{2,6},{3,7},{4,0},{5,1},{6,2},{7,3},{8,12},{9,13},{10,... | collective-permute-start | bytes 936968 | tf_op jit(solution)/shard_map/ppermute | solution.py:393
  29.1 17.6 %collective-permute-start.4 = (bf16[2,80,976]{2,1,0:T(8,128)(2,1)}, bf16[2,80,976]{2,1,0:T(8,128)(2,1)}, u32[]{:S(2)}, u32[]{:S(2)}) collective-permute-start(bf16[2,80,976]{2,1,0:T(8,128)(2,1)} %pad_maximum_fusion.11), channel_id=1, source_target_pairs={{0,2},{1,3},{2,0},{3,1},{4,6},{5,7},{6,4},{7,5},{8,10},{9,11},{10,... | collective-permute-start | bytes 936968 | tf_op jit(solution)/shard_map/ppermute | solution.py:393
  33.6 27.3 %collective-permute-start.19 = (bf16[640,640]{1,0:T(8,128)(2,1)S(1)}, bf16[640,640]{1,0:T(8,128)(2,1)}, u32[]{:S(2)}, u32[]{:S(2)}) collective-permute-start(bf16[640,640]{1,0:T(8,128)(2,1)S(1)} %get-tuple-element.157), channel_id=1, source_target_pairs={{0,1},{1,0},{2,3},{3,2},{4,5},{5,4},{6,7},{7,6},{8,9},{9,8},{10,11... | collective-permute-start | bytes 2457608 | tf_op jit(solution)/shard_map/ppermute | solution.py:393
  36.1 26.2 %collective-permute-start.14 = (bf16[4,80,1920]{2,1,0:T(8,128)(2,1)}, bf16[4,80,1920]{2,1,0:T(8,128)(2,1)}, u32[]{:S(2)}, u32[]{:S(2)}) collective-permute-start(bf16[4,80,1920]{2,1,0:T(8,128)(2,1)} %pad_maximum_fusion.5), channel_id=1, source_target_pairs={{0,1},{1,0},{2,3},{3,2},{4,5},{5,4},{6,7},{7,6},{8,9},{9,8},{10,11... | collective-permute-start | bytes 3686408 | tf_op jit(solution)/shard_map/ppermute | solution.py:393
  36.6 195.7 %all-reduce.10.cloned.1.call-start = ((), (), s32[]{:S(2)}) async-start(), calls=%async_computation.1 | async-start | bytes 3276800 | tf_op jit(solution)/shard_map/psum | solution.py:675
  93.3 19.0 %collective-permute-start.32 = (bf16[640,640]{1,0:T(8,128)(2,1)S(1)}, bf16[640,640]{1,0:T(8,128)(2,1)S(1)}, u32[]{:S(2)}, u32[]{:S(2)}) collective-permute-start(bf16[640,640]{1,0:T(8,128)(2,1)S(1)} %copy-done.76), channel_id=1, source_target_pairs={{0,1},{1,0},{2,3},{3,2},{4,5},{5,4},{6,7},{7,6},{8,9},{9,8},{10,11... | collective-permute-start | bytes 2457608 | tf_op jit(solution)/shard_map/ppermute | solution.py:393
  141.9 20.8 %collective-permute-start.39 = (bf16[128,640]{1,0:T(8,128)(2,1)}, bf16[128,640]{1,0:T(8,128)(2,1)}, u32[]{:S(2)}, u32[]{:S(2)}) collective-permute-start(bf16[128,640]{1,0:T(8,128)(2,1)} %get-tuple-element.202), channel_id=1, source_target_pairs={{0,2},{1,3},{2,0},{3,1},{4,6},{5,7},{6,4},{7,5},{8,10},{9,11},{10,... | collective-permute-start | bytes 491528 | tf_op jit(solution)/shard_map/ppermute | solution.py:393
  142.7 20.1 %collective-permute-start.40 = (bf16[128,640]{1,0:T(8,128)(2,1)}, bf16[128,640]{1,0:T(8,128)(2,1)}, u32[]{:S(2)}, u32[]{:S(2)}) collective-permute-start(bf16[128,640]{1,0:T(8,128)(2,1)} %get-tuple-element.203), channel_id=1, source_target_pairs={{0,4},{1,5},{2,6},{3,7},{4,0},{5,1},{6,2},{7,3},{8,12},{9,13},{10,... | collective-permute-start | bytes 491528 | tf_op jit(solution)/shard_map/ppermute | solution.py:393
  143.9 18.8 %collective-permute-start.41 = (bf16[128,640]{1,0:T(8,128)(2,1)}, bf16[128,640]{1,0:T(8,128)(2,1)}, u32[]{:S(2)}, u32[]{:S(2)}) collective-permute-start(bf16[128,640]{1,0:T(8,128)(2,1)} %get-tuple-element.204), channel_id=1, source_target_pairs={{0,6},{1,7},{2,4},{3,5},{4,2},{5,3},{6,0},{7,1},{8,14},{9,15},{10,... | collective-permute-start | bytes 491528 | tf_op jit(solution)/shard_map/ppermute | solution.py:393
  153.2 142.0 %all-reduce.14.cloned.1.call-start = ((), (), s32[]{:S(2)}) async-start(), calls=%async_computation.3 | async-start | bytes 1638400 | tf_op jit(solution)/shard_map/psum | solution.py:699
  169.0 21.2 %collective-permute-start.45 = (bf16[128,640]{1,0:T(8,128)(2,1)S(1)}, bf16[128,640]{1,0:T(8,128)(2,1)S(1)}, u32[]{:S(2)}, u32[]{:S(2)}) collective-permute-start(bf16[128,640]{1,0:T(8,128)(2,1)S(1)} %add_convert_fusion.3), channel_id=1, source_target_pairs={{0,16},{8,24},{16,0},{24,8},{1,17},{9,25},{17,1},{25,9},{2,18},{10... | collective-permute-start | bytes 491528 | tf_op jit(solution)/shard_map/ppermute | solution.py:393
  191.7 19.0 %collective-permute-start.51 = (bf16[640,1280]{1,0:T(8,128)(2,1)}, bf16[640,1280]{1,0:T(8,128)(2,1)}, u32[]{:S(2)}, u32[]{:S(2)}) collective-permute-start(bf16[640,1280]{1,0:T(8,128)(2,1)} %copy-done.27), channel_id=1, source_target_pairs={{0,1},{1,0},{2,3},{3,2},{4,5},{5,4},{6,7},{7,6},{8,9},{9,8},{10,11... | collective-permute-start | bytes 4915208 | tf_op jit(solution)/shard_map/ppermute | solution.py:393
  192.2 23.7 %collective-permute-start.52 = (bf16[2,128,640]{2,1,0:T(8,128)(2,1)}, bf16[2,128,640]{2,1,0:T(8,128)(2,1)}, u32[]{:S(2)}, u32[]{:S(2)}) collective-permute-start(bf16[2,128,640]{2,1,0:T(8,128)(2,1)} %pad_maximum_fusion.12), channel_id=1, source_target_pairs={{0,8},{8,0},{16,24},{24,16},{1,9},{9,1},{17,25},{25,17},{2,10},{10... | collective-permute-start | bytes 983048 | tf_op jit(solution)/shard_map/ppermute | solution.py:393
  202.1 13.7 %collective-permute-start.50 = (bf16[128,640]{1,0:T(8,128)(2,1)}, bf16[128,640]{1,0:T(8,128)(2,1)}, u32[]{:S(2)}, u32[]{:S(2)}) collective-permute-start(bf16[128,640]{1,0:T(8,128)(2,1)} %get-tuple-element.221), channel_id=1, source_target_pairs={{0,1},{1,0},{2,3},{3,2},{4,5},{5,4},{6,7},{7,6},{8,9},{9,8},{10,11... | collective-permute-start | bytes 491528 | tf_op jit(solution)/shard_map/ppermute | solution.py:393
  209.0 33.8 %collective-permute-start.63 = (bf16[320,1280]{1,0:T(8,128)(2,1)}, bf16[320,1280]{1,0:T(8,128)(2,1)}, u32[]{:S(2)}, u32[]{:S(2)}) collective-permute-start(bf16[320,1280]{1,0:T(8,128)(2,1)} %get-tuple-element.245), channel_id=1, source_target_pairs={{0,2},{1,3},{2,0},{3,1},{4,6},{5,7},{6,4},{7,5},{8,10},{9,11},{10,... | collective-permute-start | bytes 2457608 | tf_op jit(solution)/shard_map/ppermute | solution.py:393
  209.3 38.1 %collective-permute-start.64 = (bf16[320,1280]{1,0:T(8,128)(2,1)}, bf16[320,1280]{1,0:T(8,128)(2,1)}, u32[]{:S(2)}, u32[]{:S(2)}) collective-permute-start(bf16[320,1280]{1,0:T(8,128)(2,1)} %get-tuple-element.246), channel_id=1, source_target_pairs={{0,4},{1,5},{2,6},{3,7},{4,0},{5,1},{6,2},{7,3},{8,12},{9,13},{10,... | collective-permute-start | bytes 2457608 | tf_op jit(solution)/shard_map/ppermute | solution.py:393
  210.8 36.6 %collective-permute-start.65 = (bf16[320,1280]{1,0:T(8,128)(2,1)}, bf16[320,1280]{1,0:T(8,128)(2,1)}, u32[]{:S(2)}, u32[]{:S(2)}) collective-permute-start(bf16[320,1280]{1,0:T(8,128)(2,1)} %copy-done.29), channel_id=1, source_target_pairs={{0,6},{1,7},{2,4},{3,5},{4,2},{5,3},{6,0},{7,1},{8,14},{9,15},{10,... | collective-permute-start | bytes 2457608 | tf_op jit(solution)/shard_map/ppermute | solution.py:393
  235.9 37.1 %collective-permute-start.54 = (bf16[128,640]{1,0:T(8,128)(2,1)S(1)}, bf16[128,640]{1,0:T(8,128)(2,1)S(1)}, u32[]{:S(2)}, u32[]{:S(2)}) collective-permute-start(bf16[128,640]{1,0:T(8,128)(2,1)S(1)} %get-tuple-element.229), channel_id=1, source_target_pairs={{0,16},{8,24},{16,0},{24,8},{1,17},{9,25},{17,1},{25,9},{2,18},{10... | collective-permute-start | bytes 491528 | tf_op jit(solution)/shard_map/ppermute | solution.py:393
  238.2 42.4 %collective-permute-start.67 = (bf16[2,80,1280]{2,1,0:T(8,128)(2,1)}, bf16[2,80,1280]{2,1,0:T(8,128)(2,1)}, u32[]{:S(2)}, u32[]{:S(2)}) collective-permute-start(bf16[2,80,1280]{2,1,0:T(8,128)(2,1)} %dynamic-slice_bitcast_fusion), channel_id=1, source_target_pairs={{0,8},{8,0},{16,24},{24,16},{1,9},{9,1},{17,25},{25,17},{2,10},{10... | collective-permute-start | bytes 1228808 | tf_op jit(solution)/shard_map/ppermute | solution.py:393
  238.8 115.0 %all-reduce.12.cloned.1.call-start = ((), (), s32[]{:S(2)}) async-start(), calls=%async_computation.2 | async-start | bytes 1638400 | tf_op jit(solution)/shard_map/psum | solution.py:741
  257.9 15.9 %collective-permute-start.74 = (bf16[80,1280]{1,0:T(8,128)(2,1)}, bf16[80,1280]{1,0:T(8,128)(2,1)}, u32[]{:S(2)}, u32[]{:S(2)}) collective-permute-start(bf16[80,1280]{1,0:T(8,128)(2,1)} %get-tuple-element.275), channel_id=1, source_target_pairs={{0,6},{1,7},{2,4},{3,5},{4,2},{5,3},{6,0},{7,1},{8,14},{9,15},{10,... | collective-permute-start | bytes 614408 | tf_op jit(solution)/shard_map/ppermute | solution.py:393
  259.4 14.9 %collective-permute-start.75 = (bf16[80,1280]{1,0:T(8,128)(2,1)}, bf16[80,1280]{1,0:T(8,128)(2,1)}, u32[]{:S(2)}, u32[]{:S(2)}) collective-permute-start(bf16[80,1280]{1,0:T(8,128)(2,1)} %get-tuple-element.274), channel_id=1, source_target_pairs={{0,4},{1,5},{2,6},{3,7},{4,0},{5,1},{6,2},{7,3},{8,12},{9,13},{10,... | collective-permute-start | bytes 614408 | tf_op jit(solution)/shard_map/ppermute | solution.py:393
  274.3 19.1 %collective-permute-start.55 = (bf16[2,128,640]{2,1,0:T(8,128)(2,1)}, bf16[2,128,640]{2,1,0:T(8,128)(2,1)}, u32[]{:S(2)}, u32[]{:S(2)}) collective-permute-start(bf16[2,128,640]{2,1,0:T(8,128)(2,1)} %pad_maximum_fusion.15), channel_id=1, source_target_pairs={{0,8},{8,0},{16,24},{24,16},{1,9},{9,1},{17,25},{25,17},{2,10},{10... | collective-permute-start | bytes 983048 | tf_op jit(solution)/shard_map/ppermute | solution.py:393
  295.3 18.0 %collective-permute-start.68 = (bf16[80,1280]{1,0:T(8,128)(2,1)S(1)}, bf16[80,1280]{1,0:T(8,128)(2,1)S(1)}, u32[]{:S(2)}, u32[]{:S(2)}) collective-permute-start(bf16[80,1280]{1,0:T(8,128)(2,1)S(1)} %dynamic-slice_bitcast_fusion.3), channel_id=1, source_target_pairs={{0,16},{8,24},{16,0},{24,8},{1,17},{9,25},{17,1},{25,9},{2,18},{10... | collective-permute-start | bytes 614408 | tf_op jit(solution)/shard_map/ppermute | solution.py:393
  298.4 15.0 %collective-permute-start.71 = (bf16[80,1280]{1,0:T(8,128)(2,1)S(1)}, bf16[80,1280]{1,0:T(8,128)(2,1)S(1)}, u32[]{:S(2)}, u32[]{:S(2)}) collective-permute-start(bf16[80,1280]{1,0:T(8,128)(2,1)S(1)} %get-tuple-element.308), channel_id=1, source_target_pairs={{0,6},{1,7},{2,4},{3,5},{4,2},{5,3},{6,0},{7,1},{8,14},{9,15},{10,... | collective-permute-start | bytes 614408 | tf_op jit(solution)/shard_map/ppermute | solution.py:393
  313.3 14.0 %collective-permute-start.69 = (bf16[80,1280]{1,0:T(8,128)(2,1)S(1)}, bf16[80,1280]{1,0:T(8,128)(2,1)S(1)}, u32[]{:S(2)}, u32[]{:S(2)}) collective-permute-start(bf16[80,1280]{1,0:T(8,128)(2,1)S(1)} %fusion.1), channel_id=1, source_target_pairs={{0,16},{8,24},{16,0},{24,8},{1,17},{9,25},{17,1},{25,9},{2,18},{10... | collective-permute-start | bytes 614408 | tf_op jit(solution)/shard_map/ppermute | solution.py:393
  327.4 17.6 %collective-permute-start.70 = (bf16[2,80,1280]{2,1,0:T(8,128)(2,1)S(1)}, bf16[2,80,1280]{2,1,0:T(8,128)(2,1)S(1)}, u32[]{:S(2)}, u32[]{:S(2)}) collective-permute-start(bf16[2,80,1280]{2,1,0:T(8,128)(2,1)S(1)} %pad_maximum_fusion.10), channel_id=1, source_target_pairs={{0,8},{8,0},{16,24},{24,16},{1,9},{9,1},{17,25},{25,17},{2,10},{10... | collective-permute-start | bytes 1228808 | tf_op jit(solution)/shard_map/ppermute | solution.py:393
  (147 other events, 1025.4 us)
Sparse Core Ops, SparseCore 0:
  36.7 33.2 all-gather.1
  153.3 78.8 all-reduce.9
  238.9 56.3 all-reduce.13
  298.2 55.5 all-reduce.11
